TPU v7x, 128 devices: a whole 4x4x4 slice. The times are simulated.
128 devices in a mesh: rows: 32 (over y, z, core), cols: 4 (over x).
Axes of the slice: x: 4, y: 4, z: 4, core: 2. Of those that a mesh axis runs over, the one named last changes fastest.
Arguments:
- pixels: bfloat16 [2048, 1024, 424], P('rows', 'cols'), as said below
- band_basis: bfloat16 [424, 48], replicated, may hold values from -0.3125 to 0.3125
- column_basis: bfloat16 [1024, 256], P('cols'), may hold values from -0.1875 to 0.1875
Outputs:
- gram: float32 [2048, 2048], P('rows', 'cols')
Inputs may be any that keep to these rules, and one draw needn't show every extreme that they name: `pixels`: pixel spectra of the frame.
All inputs are finite; a program needn't handle non-finite values.
Results may differ from a plain program's by a relative error of at most 0.0003.
Values may be sent and summed in bfloat16 or wider, within the bound.
No kernel may reach another device: no remote copies, remote signals or barrier semaphores. Data moves between devices by JAX's collectives and lax.ppermute only.
A program may use at most 128 MiB of HBM per device.

v0:
```python
import jax
import jax.numpy as jnp
from jax import lax
from jax.sharding import PartitionSpec as P

R3 = 48
R2 = 256


def local(pixels, band_basis, column_basis):
    scale = 1.0 / (R3 * R2)
    banded = jnp.einsum(
        "hcb,br->rhc", pixels, band_basis, preferred_element_type=jnp.float32
    ).astype(jnp.bfloat16)
    projected = lax.psum_scatter(
        jnp.einsum("rhc,cs->rhs", banded, column_basis, preferred_element_type=jnp.float32),
        "cols",
        scatter_dimension=0,
        tiled=True,
    ).astype(jnp.bfloat16)
    partial_rows = jnp.einsum(
        "rhs,rks->hk",
        projected,
        lax.all_gather(projected, "rows", axis=1, tiled=True),
        preferred_element_type=jnp.float32,
    )
    summed = lax.psum_scatter(partial_rows, "cols", scatter_dimension=1, tiled=True)
    return summed * scale


def solution(mesh):
    return jax.shard_map(
        local,
        mesh=mesh,
        in_specs=(P("rows", "cols", None), P(), P("cols", None)),
        out_specs=P("rows", "cols"),
        check_vma=False,
    )
```

profile of v0, /device:TPU:0, one launch (start us, length us, event | category | flops | bytes accessed | tf_op | source)
XLA Modules:
  0.0 161.0 jit_solution(11158547669331954946)
XLA Ops:
  6.5 0.0 copy-start
  6.5 0.0 reduce-scatter.3.cloned.1.call-start
  6.5 7.5 %fusion.2 = bf16[48,64,256]{2,0,1:T(8,128)(2,1)S(1)} fusion(bf16[64,256,424]{1,2,0:T(8,128)(2,1)} %param.3, bf16[424,48]{0,1:T(8,128)(2,1)} %param.4), kind=kOutput, calls=%fused_computation.5 | convolution fusion | flops 666894336 | bytes 15507200 | tf_op jit(solution)/shard_map/hcb,br->rhc/dot_general | solution.py:12
  14.1 0.0 copy-done
  14.1 2.3 %fusion = f32[48,64,256]{2,1,0:T(8,128)} fusion(bf16[48,64,256]{2,0,1:T(8,128)(2,1)S(1)} %fusion.2, bf16[256,256]{1,0:T(8,128)(2,1)S(1)} %copy-done), kind=kOutput, calls=%fused_computation.2 | convolution fusion | flops 402653184 | bytes 4849664 | tf_op jit(solution)/shard_map/rhc,cs->rhs/dot_general | solution.py:16
  16.5 0.0 reduce-scatter.3.cloned.1.call-update
  16.5 0.0 all-gather.2.cloned.1.call-start
  16.5 40.8 %reduce-scatter.3.cloned.1.call-done = f32[12,64,256]{2,1,0:T(8,128)} async-done(((f32[48,64,256]{2,1,0:T(8,128)}), f32[12,64,256]{2,1,0:T(8,128)}) %reduce-scatter.3.cloned.1.call-update) | async-done | bytes 786448 | tf_op jit(solution)/shard_map/reduce_scatter | solution.py:15
  57.3 2.0 %convert_element_type.7 = bf16[12,64,256]{2,1,0:T(8,128)(2,1)} convert(f32[12,64,256]{2,1,0:T(8,128)} %reduce-scatter.3.cloned.1.call-done) | non-fusion elementwise | flops 196608 | bytes 1179648 | tf_op jit(solution)/shard_map/convert_element_type | solution.py:20
  59.3 0.0 all-gather.2.cloned.1.call-update
  59.3 0.0 reduce-scatter.5.cloned.1.call-start
  59.4 63.1 %all-gather.2.cloned.1.call-done = bf16[12,2048,256]{2,1,0:T(8,128)(2,1)} async-done(((bf16[12,64,256]{2,1,0:T(8,128)(2,1)}), bf16[12,2048,256]{2,1,0:T(8,128)(2,1)}) %all-gather.2.cloned.1.call-update) | async-done | bytes 12582928 | tf_op jit(solution)/shard_map/all_gather | solution.py:24
  122.4 9.4 %convolution_bitcast_fusion = f32[64,2048]{1,0:T(8,128)} fusion(bf16[12,64,256]{2,1,0:T(8,128)(2,1)} %convert_element_type.7, bf16[12,2048,256]{2,1,0:T(8,128)(2,1)} %all-gather.2.cloned.1.call-done), kind=kOutput, calls=%fused_computation.1 | convolution fusion | flops 805306368 | bytes 13500416 | tf_op jit(solution)/shard_map/rhs,rks->hk/dot_general | solution.py:21
  131.8 0.0 reduce-scatter.5.cloned.1.call-update
  131.9 21.0 %reduce-scatter.5.cloned.1.call-done = f32[64,512]{1,0:T(8,128)} async-done(((f32[64,2048]{1,0:T(8,128)}), f32[64,512]{1,0:T(8,128)}) %reduce-scatter.5.cloned.1.call-update) | async-done | bytes 131088 | tf_op jit(solution)/shard_map/reduce_scatter | solution.py:27
  152.9 1.6 broadcast_multiply_fusion
Async XLA Ops:
  6.5 7.6 %copy-start = (bf16[256,256]{1,0:T(8,128)(2,1)S(1)}, bf16[256,256]{1,0:T(8,128)(2,1)}, u32[]{:S(2)}) copy-start(bf16[256,256]{1,0:T(8,128)(2,1)} %param.5) | copy-start | bytes 393220
  6.5 50.8 %reduce-scatter.3.cloned.1.call-start = ((), (), s32[]{:S(2)}) async-start(), calls=%async_computation.2 | async-start | bytes 3932160 | tf_op jit(solution)/shard_map/reduce_scatter | solution.py:15
  16.5 105.9 %all-gather.2.cloned.1.call-start = ((), (), s32[]{:S(2)}) async-start(), calls=%async_computation.3 | async-start | bytes 12976128 | tf_op jit(solution)/shard_map/all_gather | solution.py:24
  59.3 93.5 %reduce-scatter.5.cloned.1.call-start = ((), (), s32[]{:S(2)}) async-start(), calls=%async_computation.4 | async-start | bytes 655360 | tf_op jit(solution)/shard_map/reduce_scatter | solution.py:27
Sparse Core Ops, SparseCore 0:
  16.6 40.6 reduce-scatter.2
  59.7 62.7 all-gather.1
  132.0 20.8 reduce-scatter.4
where the time goes:
time: 161 us
  waiting for transfers between devices  125 us (78%)
  matrix products  19.3 us (12%)
  between operations  13.1 us (8%)
  other arithmetic  3.55 us (2%)
    all_gather x1, waiting for transfers between devices, local(): lax.all_gather(projected, 'rows', axis=1, tiled=True)  63.1 us
    reduce_scatter x1, waiting for transfers between devices, local(): lax.psum_scatter(jnp.einsum('rhc,cs->rhs', banded, column_basis, preferre...  40.8 us
    reduce_scatter x1, waiting for transfers between devices, local(): lax.psum_scatter(partial_rows, 'cols', scatter_dimension=1, tiled=True)  21 us
    dot_general x1, matrix products, local(): jnp.einsum('rhs,rks->hk', projected, lax.all_gather(projected, 'rows', ax...  9.42 us
    dot_general x1, matrix products, local(): jnp.einsum('hcb,br->rhc', pixels, band_basis, preferred_element_type=jnp....  7.55 us
  transfers between devices with their start and end apart: 3, of which 3 were waited for; matrix products, arithmetic and copies ran while one was open for 0% of the time, Pallas kernels for 0%

commit v1 on v0

v1 whole, which is shorter than its diff:
```python
import functools

import jax
import jax.numpy as jnp
from jax import lax
from jax.experimental import pallas as pl
from jax.experimental.pallas import tpu as pltpu
from jax.sharding import Mesh, PartitionSpec as P

R3 = 48
R2 = 256
NX = 4
RX = R3 // NX
SCALE = 1.0 / (R3 * R2)
HB = 16
BF = jnp.bfloat16
F32 = jnp.float32
VMEM_LIMIT = 48 * 1024 * 1024


def shift(v, axis, n, by):
    return lax.ppermute(v, axis, [(i, (i + by) % n) for i in range(n)])


def params():
    return pltpu.CompilerParams(vmem_limit_bytes=VMEM_LIMIT)


def band_kernel(bt_ref, pix_ref, *rest):
    outs, (basis, stage) = rest[:NX], rest[NX:]
    x = lax.axis_index("x")

    @pl.when(pl.program_id(0) == 0)
    def _():
        basis[...] = jnp.zeros_like(basis)
        for k in range(NX):

            @pl.when(x == k)
            def _():
                for j in range(NX):
                    first = RX * ((k + j) % NX)
                    basis[16 * j : 16 * j + RX, :] = bt_ref[first : first + RX, :]

    for h in range(HB):
        banded = jnp.dot(basis[...], pix_ref[h], preferred_element_type=F32)
        for t in range(2):
            stage[t, 64 * h : 64 * (h + 1), :] = banded[:, 128 * t : 128 * (t + 1)]
    for j in range(NX):
        for r in range(RX):
            for t in range(2):
                rows = stage[t, pl.ds(16 * j + r, HB, stride=64), :]
                outs[j][r, :, 128 * t : 128 * (t + 1)] = rows.astype(BF)


def band(bt, pix):
    h, bands, c = pix.shape
    return pl.pallas_call(
        band_kernel,
        grid=(h // HB,),
        in_specs=[
            pl.BlockSpec((R3, bands), lambda i: (0, 0)),
            pl.BlockSpec((HB, bands, c), lambda i: (i, 0, 0)),
        ],
        out_specs=[pl.BlockSpec((RX, HB, c), lambda i: (0, i, 0))] * NX,
        out_shape=[jax.ShapeDtypeStruct((RX, h, c), BF)] * NX,
        scratch_shapes=[pltpu.VMEM((64, bands), BF), pltpu.VMEM((2, 64 * HB, c // 2), F32)],
        compiler_params=params(),
        cost_estimate=pl.CostEstimate(
            flops=2 * h * c * bands * 64, bytes_accessed=pix.size * 2, transcendentals=0
        ),
        name="band",
    )(bt, pix)


def column_kernel(b0, b1, b2, b3, col_ref, out_ref):
    x = lax.axis_index("x")
    cols = [col_ref[lax.rem(x + NX - j, NX)] for j in range(NX)]
    rows = b0.shape[1]
    for r in range(RX):
        total = jnp.zeros((rows, R2), F32)
        for j, b in enumerate((b0, b1, b2, b3)):
            total += jnp.dot(b[r], cols[j], preferred_element_type=F32)
        out_ref[:, R2 * r : R2 * (r + 1)] = total.astype(BF)


def column(blocks, col):
    r, h, c = blocks[0].shape
    return pl.pallas_call(
        column_kernel,
        out_shape=jax.ShapeDtypeStruct((h, r * R2), BF),
        compiler_params=params(),
        cost_estimate=pl.CostEstimate(
            flops=2 * r * h * 4 * c * R2, bytes_accessed=2 * 5 * r * h * c, transcendentals=0
        ),
        name="column",
    )(*blocks, col)


def gram_kernel(*refs):
    zs, mine, theirs, outs = refs[:4], refs[4:8], refs[8:12], refs[12:16]
    lhs, rhs, sem = refs[16:]
    x, y, core = lax.axis_index("x"), lax.axis_index("y"), lax.axis_index("core")
    n = zs[0].shape[0]
    copies = []
    for d in range(4):
        copies.append(pltpu.make_async_copy(zs[d], lhs.at[pl.ds(n * d, n)], sem.at[d]))
    for e in range(4):
        owner = lax.rem(y + e + NX - x, NX)
        for half, ref in ((core, mine[e]), (1 - core, theirs[e])):
            at = pl.multiple_of((owner * 2 + half) * n, n)
            copies.append(
                pltpu.make_async_copy(ref, rhs.at[pl.ds(at, n)], sem.at[len(copies)])
            )
    for copy in copies:
        copy.start()
    for copy in copies:
        copy.wait()
    for d in range(4):
        outs[d][...] = lax.dot_general(
            lhs[...],
            rhs[2 * n * d : 2 * n * (d + 1), :],
            (((1,), (1,)), ((), ())),
            preferred_element_type=F32,
        )


def gram(zs, mine, theirs):
    n, k = zs[0].shape
    return pl.pallas_call(
        gram_kernel,
        in_specs=[pl.BlockSpec(memory_space=pl.ANY)] * 12,
        out_shape=[jax.ShapeDtypeStruct((4 * n, 2 * n), F32)] * 4,
        scratch_shapes=[
            pltpu.VMEM((4 * n, k), BF),
            pltpu.VMEM((8 * n, k), BF),
            pltpu.SemaphoreType.DMA((12,)),
        ],
        compiler_params=params(),
        cost_estimate=pl.CostEstimate(
            flops=2 * 32 * n * n * k, bytes_accessed=2 * 12 * n * k, transcendentals=0
        ),
        name="gram",
    )(*zs, *mine, *theirs)


def sum_kernel(g0, g1, g2, g3, *outs):
    n = outs[0].shape[0]
    for d in range(4):
        at = slice(n * d, n * (d + 1))
        outs[d][...] = (g0[at, :] + g1[at, :] + g2[at, :] + g3[at, :]) * SCALE


def sum_x(parts):
    n, m = parts[0].shape
    return pl.pallas_call(
        sum_kernel,
        out_shape=[jax.ShapeDtypeStruct((n // 4, m), F32)] * 4,
        name="sum_x",
    )(*parts)


def place_kernel(p0, p1, p2, p3, out_ref):
    z = lax.axis_index("z")
    m = p0.shape[1]
    for d, p in enumerate((p0, p1, p2, p3)):
        at = pl.multiple_of(lax.rem(z + 4 - d, 4) * m, m)
        out_ref[:, pl.ds(at, m)] = p[...]


def place(parts):
    n, m = parts[0].shape
    return pl.pallas_call(
        place_kernel, out_shape=jax.ShapeDtypeStruct((n, 4 * m), F32), name="place"
    )(*parts)


def local(pixels, band_basis, column_basis):
    col = lax.all_gather(column_basis, "x", axis=0, tiled=False)
    blocks = band(band_basis.T, pixels.transpose(0, 2, 1))
    blocks = [b if j == 0 else shift(b, "x", NX, j) for j, b in enumerate(blocks)]
    mine = column(blocks, col)
    ys = [mine] + [shift(mine, "y", 4, -e) for e in range(1, 4)]
    zs = [mine] + [shift(mine, "z", 4, -e) for e in range(1, 4)]
    theirs = [shift(v, "core", 2, 1) for v in ys]
    parts = gram(zs, ys, theirs)
    parts = [g if d == 0 else shift(g, "x", NX, d) for d, g in enumerate(parts)]
    parts = sum_x(parts)
    parts = [g if d == 0 else shift(g, "z", 4, d) for d, g in enumerate(parts)]
    return place(parts)


def solution(mesh):
    inner = Mesh(mesh.devices.reshape(4, 4, 2, 4), ("y", "z", "core", "x"))
    return jax.shard_map(
        local,
        mesh=inner,
        in_specs=(P(("y", "z", "core"), "x", None), P(), P("x", None)),
        out_specs=P(("y", "z", "core"), "x"),
        check_vma=False,
    )
```

time: 161 us -> 96.8 us (0.60); the launches traced: 161 us -> 95 us
  waiting for transfers between devices: 125 us -> 19.8 us
  starting transfers between devices: 0.09 us -> 31.9 us
  blocking collectives: 0 us -> 24 us
  matrix products: 19.3 us -> 0 us
  Pallas kernels: 0 us -> 16.5 us
  between operations: 13.1 us -> 0.08 us
  other arithmetic: 3.55 us -> 0 us
  local copies, waits for them, and re-layouts: 0.01 us -> 2.72 us
    all_gather x1 -> x0, waiting for transfers between devices: 63.1 us -> none  [local(): lax.all_gather(projected, 'rows', axis=1, tiled=True)]
    reduce_scatter x2 -> x0, waiting for transfers between devices: 61.8 us -> none  [the longest x1 40.8 us: local(): lax.psum_scatter(jnp.einsum('rhc,cs->rhs', banded, column_basis, preferre...]
    ppermute x0 -> x19, starting transfers between devices: none -> 31.9 us  [shift(): return lax.ppermute(v, axis, [(i, (i + by) % n) for i in range(n)])]
    all_gather x0 -> x1, blocking collectives: none -> 24 us  [local(): col = lax.all_gather(column_basis, 'x', axis=0, tiled=False)]
    ppermute x0 -> x19, waiting for transfers between devices: none -> 19.8 us  [shift(): return lax.ppermute(v, axis, [(i, (i + by) % n) for i in range(n)])]
    dot_general x3 -> x0, matrix products: 19.3 us -> none  [the longest x1 9.42 us: local(): jnp.einsum('rhs,rks->hk', projected, lax.all_gather(projected, 'rows', ax...]
    pallas_call x0 -> x5, Pallas kernels: none -> 16.5 us  [the longest x1 7.67 us: band(): pl.pallas_call(band_kernel, grid=(h // HB,), in_specs=[pl.BlockSpec((R3,...]
    unnamed x2 -> x18, local copies, waits for them, and re-layouts: 0.01 us -> 2.72 us
  transfers between devices with their start and end apart: 3 -> 19, of which waited for: 3 -> 7; matrix products, arithmetic and copies ran while one was open for 0% -> 0% of each run, Pallas kernels for 0% -> 0%
where the time goes in v1:
time: 96.8 us; the launch traced here: 95 us
  starting transfers between devices  31.9 us (33%)
  blocking collectives  24 us (25%)
  waiting for transfers between devices  19.8 us (20%)
  Pallas kernels  16.5 us (17%)
  local copies, waits for them, and re-layouts  2.72 us (3%)
    ppermute x19, starting transfers between devices, shift(): return lax.ppermute(v, axis, [(i, (i + by) % n) for i in range(n)])  31.9 us
    all_gather x1, blocking collectives, local(): col = lax.all_gather(column_basis, 'x', axis=0, tiled=False)  24 us
    ppermute x19, waiting for transfers between devices, shift(): return lax.ppermute(v, axis, [(i, (i + by) % n) for i in range(n)])  19.8 us
    pallas_call x1, Pallas kernels, band(): pl.pallas_call(band_kernel, grid=(h // HB,), in_specs=[pl.BlockSpec((R3,...  7.67 us
    pallas_call x1, Pallas kernels, gram(): pl.pallas_call(gram_kernel, in_specs=[pl.BlockSpec(memory_space=pl.ANY)]...  4.39 us
    unnamed x18, local copies, waits for them, and re-layouts  2.72 us
  transfers between devices with their start and end apart: 19, of which 7 were waited for; matrix products, arithmetic and copies ran while one was open for 0% of the time, Pallas kernels for 0%

profile of v1, /device:TPU:0, one launch (start us, length us, event | category | flops | bytes accessed | tf_op | source)
XLA Modules:
  0.0 95.0 jit_solution(17736394887834383495)
XLA Ops:
  0.0 0.8 copy-done.1
  0.8 7.7 %band.1 = (bf16[12,64,256]{2,1,0:T(8,128)(2,1)S(1)}, bf16[12,64,256]{2,1,0:T(8,128)(2,1)S(1)}, bf16[12,64,256]{2,1,0:T(8,128)(2,1)S(1)}, bf16[12,64,256]{2,1,0:T(8,128)(2,1)S(1)}) custom-call(bf16[48,424]{1,0:T(8,128)(2,1)S(1)} %bitcast.4, bf16[64,424,256]{2,1,0:T(8,128)(2,1)} %bitcast.5), custom_call_target="tpu_custom_call" | custom-call | flops 889192448 | bytes 13893632 | tf_op jit(solution)/shard_map/band/pallas_call | solution.py:57
  8.5 1.6 %collective-permute-start = (bf16[12,64,256]{2,1,0:T(8,128)(2,1)S(1)}, bf16[12,64,256]{2,1,0:T(8,128)(2,1)S(1)}, u32[]{:S(2)}, u32[]{:S(2)}) collective-permute-start(bf16[12,64,256]{2,1,0:T(8,128)(2,1)S(1)} %get-tuple-element.18), channel_id=1, source_target_pairs={{0,1},{1,2},{2,3},{3,0},{4,5},{5,6},{6,7},{7,4},{8,9},{9,10},{10,1... | collective-permute-start | bytes 1179656 | tf_op jit(solution)/shard_map/ppermute | solution.py:22
  10.1 2.7 %collective-permute-start.1 = (bf16[12,64,256]{2,1,0:T(8,128)(2,1)S(1)}, bf16[12,64,256]{2,1,0:T(8,128)(2,1)S(1)}, u32[]{:S(2)}, u32[]{:S(2)}) collective-permute-start(bf16[12,64,256]{2,1,0:T(8,128)(2,1)S(1)} %get-tuple-element.19), channel_id=1, source_target_pairs={{0,2},{1,3},{2,0},{3,1},{4,6},{5,7},{6,4},{7,5},{8,10},{9,11},{10,... | collective-permute-start | bytes 1179656 | tf_op jit(solution)/shard_map/ppermute | solution.py:22
  12.8 1.4 %collective-permute-start.2 = (bf16[12,64,256]{2,1,0:T(8,128)(2,1)S(1)}, bf16[12,64,256]{2,1,0:T(8,128)(2,1)S(1)}, u32[]{:S(2)}, u32[]{:S(2)}) collective-permute-start(bf16[12,64,256]{2,1,0:T(8,128)(2,1)S(1)} %get-tuple-element.20), channel_id=1, source_target_pairs={{0,3},{1,0},{2,1},{3,2},{4,7},{5,4},{6,5},{7,6},{8,11},{9,8},{10,9... | collective-permute-start | bytes 1179656 | tf_op jit(solution)/shard_map/ppermute | solution.py:22
  14.3 24.0 %all-gather = bf16[1024,256]{1,0:T(8,128)(2,1)S(1)} all-gather(bf16[256,256]{1,0:T(8,128)(2,1)S(1)} %copy-done.2), channel_id=2, replica_groups=mesh['y'=4,'z'=4,'core'=2,'x'=4] {'x'}, dimensions={0}, use_global_device_ids=true | all-gather | bytes 655360 | tf_op jit(solution)/shard_map/all_gather | solution.py:178
  38.3 0.0 collective-permute-done.b1
  38.3 0.0 collective-permute-done.1.b2
  38.3 0.0 collective-permute-done.2.b3
  38.3 1.2 %column.1.refs_0_.refs_4_ = bf16[64,3072]{1,0:T(8,128)(2,1)S(1)} custom-call(bf16[12,64,256]{2,1,0:T(8,128)(2,1)S(1)} %get-tuple-element.17.b0, bf16[12,64,256]{2,1,0:T(8,128)(2,1)S(1)} %collective-permute-done.b1, bf16[12,64,256]{2,1,0:T(8,128)(2,1)S(1)} %collective-permute-done.1.b2, bf16[12,64,256]{2,1,0:T(8,128)(2,1)S(1)} %collective-permute-done.2.b3, ...), custom_call_target="tpu_custom_call" | custom-call | flops 402653184 | bytes 1966080 | tf_op jit(solution)/shard_map/column/pallas_call | solution.py:88
  39.5 0.1 collective-permute-start.9
  39.6 1.5 %collective-permute-start.8 = (bf16[64,3072]{1,0:T(8,128)(2,1)S(1)}, bf16[64,3072]{1,0:T(8,128)(2,1)S(1)}, u32[]{:S(2)}, u32[]{:S(2)}) collective-permute-start(bf16[64,3072]{1,0:T(8,128)(2,1)S(1)} %column.1.refs_0_.refs_4_), channel_id=1, source_target_pairs={{0,32},{32,64},{64,96},{96,0},{1,33},{33,65},{65,97},{97,1},{2,34}... | collective-permute-start | bytes 1179656 | tf_op jit(solution)/shard_map/ppermute | solution.py:22
  41.1 2.9 %collective-permute-start.7 = (bf16[64,3072]{1,0:T(8,128)(2,1)S(1)}, bf16[64,3072]{1,0:T(8,128)(2,1)S(1)}, u32[]{:S(2)}, u32[]{:S(2)}) collective-permute-start(bf16[64,3072]{1,0:T(8,128)(2,1)S(1)} %column.1.refs_0_.refs_4_), channel_id=1, source_target_pairs={{0,64},{32,96},{64,0},{96,32},{1,65},{33,97},{65,1},{97,33},{2,66}... | collective-permute-start | bytes 1179656 | tf_op jit(solution)/shard_map/ppermute | solution.py:22
  44.0 1.3 %collective-permute-start.6 = (bf16[64,3072]{1,0:T(8,128)(2,1)S(1)}, bf16[64,3072]{1,0:T(8,128)(2,1)S(1)}, u32[]{:S(2)}, u32[]{:S(2)}) collective-permute-start(bf16[64,3072]{1,0:T(8,128)(2,1)S(1)} %column.1.refs_0_.refs_4_), channel_id=1, source_target_pairs={{0,96},{32,0},{64,32},{96,64},{1,97},{33,1},{65,33},{97,65},{2,98}... | collective-permute-start | bytes 1179656 | tf_op jit(solution)/shard_map/ppermute | solution.py:22
  45.4 1.9 %collective-permute-start.5 = (bf16[64,3072]{1,0:T(8,128)(2,1)S(1)}, bf16[64,3072]{1,0:T(8,128)(2,1)S(1)}, u32[]{:S(2)}, u32[]{:S(2)}) collective-permute-start(bf16[64,3072]{1,0:T(8,128)(2,1)S(1)} %column.1.refs_0_.refs_4_), channel_id=1, source_target_pairs={{0,8},{8,16},{16,24},{24,0},{1,9},{9,17},{17,25},{25,1},{2,10},{10... | collective-permute-start | bytes 1179656 | tf_op jit(solution)/shard_map/ppermute | solution.py:22
  47.3 0.0 collective-permute-done.9.refs_8_
  47.3 3.6 %collective-permute-start.4 = (bf16[64,3072]{1,0:T(8,128)(2,1)S(1)}, bf16[64,3072]{1,0:T(8,128)(2,1)S(1)}, u32[]{:S(2)}, u32[]{:S(2)}) collective-permute-start(bf16[64,3072]{1,0:T(8,128)(2,1)S(1)} %column.1.refs_0_.refs_4_), channel_id=1, source_target_pairs={{0,16},{8,24},{16,0},{24,8},{1,17},{9,25},{17,1},{25,9},{2,18},{10... | collective-permute-start | bytes 1179656 | tf_op jit(solution)/shard_map/ppermute | solution.py:22
  50.9 1.5 %collective-permute-done.8.refs_7_ = bf16[64,3072]{1,0:T(8,128)(2,1)S(1)} collective-permute-done((bf16[64,3072]{1,0:T(8,128)(2,1)S(1)}, bf16[64,3072]{1,0:T(8,128)(2,1)S(1)}, u32[]{:S(2)}, u32[]{:S(2)}) %collective-permute-start.8) | collective-permute-done | bytes 393248 | tf_op jit(solution)/shard_map/ppermute | solution.py:22
  52.4 3.9 %collective-permute-start.3 = (bf16[64,3072]{1,0:T(8,128)(2,1)S(1)}, bf16[64,3072]{1,0:T(8,128)(2,1)S(1)}, u32[]{:S(2)}, u32[]{:S(2)}) collective-permute-start(bf16[64,3072]{1,0:T(8,128)(2,1)S(1)} %column.1.refs_0_.refs_4_), channel_id=1, source_target_pairs={{0,24},{8,0},{16,8},{24,16},{1,25},{9,1},{17,9},{25,17},{2,26},{10... | collective-permute-start | bytes 1179656 | tf_op jit(solution)/shard_map/ppermute | solution.py:22
  56.3 5.6 %collective-permute-done.7.refs_6_ = bf16[64,3072]{1,0:T(8,128)(2,1)S(1)} collective-permute-done((bf16[64,3072]{1,0:T(8,128)(2,1)S(1)}, bf16[64,3072]{1,0:T(8,128)(2,1)S(1)}, u32[]{:S(2)}, u32[]{:S(2)}) %collective-permute-start.7) | collective-permute-done | bytes 393248 | tf_op jit(solution)/shard_map/ppermute | solution.py:22
  61.9 0.0 collective-permute-start.12
  61.9 0.0 collective-permute-done.6.refs_5_
  61.9 0.5 collective-permute-start.11
  62.4 0.0 collective-permute-done.5.refs_3_
  62.4 0.1 collective-permute-start.10
  62.5 5.4 %collective-permute-done.4.refs_2_ = bf16[64,3072]{1,0:T(8,128)(2,1)S(1)} collective-permute-done((bf16[64,3072]{1,0:T(8,128)(2,1)S(1)}, bf16[64,3072]{1,0:T(8,128)(2,1)S(1)}, u32[]{:S(2)}, u32[]{:S(2)}) %collective-permute-start.4) | collective-permute-done | bytes 393248 | tf_op jit(solution)/shard_map/ppermute | solution.py:22
  67.9 0.0 collective-permute-done.10.refs_9_
  67.9 4.4 %gram.1 = (f32[256,128]{1,0:T(8,128)S(1)}, f32[256,128]{1,0:T(8,128)S(1)}, f32[256,128]{1,0:T(8,128)S(1)}, f32[256,128]{1,0:T(8,128)S(1)}) custom-call(bf16[64,3072]{1,0:T(8,128)(2,1)S(1)} %column.1.refs_0_.refs_4_, bf16[64,3072]{1,0:T(8,128)(2,1)S(1)} %collective-permute-done.3.refs_1_, bf16[64,3072]{1,0:T(8,128)(2,1)S(1)} %collective-permute-done.4.refs_2_, ...), custom_call_target="tpu_custom_call" | custom-call | flops 805306368 | bytes 4718592 | tf_op jit(solution)/shard_map/gram/pallas_call | solution.py:129
  72.3 0.0 copy-start
  72.3 0.6 copy-done
  73.0 1.3 %collective-permute-start.13 = (f32[256,128]{1,0:T(8,128)S(1)}, f32[256,128]{1,0:T(8,128)S(1)}, u32[]{:S(2)}, u32[]{:S(2)}) collective-permute-start(f32[256,128]{1,0:T(8,128)S(1)} %get-tuple-element.22), channel_id=1, source_target_pairs={{0,1},{1,2},{2,3},{3,0},{4,5},{5,6},{6,7},{7,4},{8,9},{9,10},{10,1... | collective-permute-start | bytes 393224 | tf_op jit(solution)/shard_map/ppermute | solution.py:22
  74.3 2.7 %collective-permute-start.14 = (f32[256,128]{1,0:T(8,128)S(1)}, f32[256,128]{1,0:T(8,128)S(1)}, u32[]{:S(2)}, u32[]{:S(2)}) collective-permute-start(f32[256,128]{1,0:T(8,128)S(1)} %get-tuple-element.23), channel_id=1, source_target_pairs={{0,2},{1,3},{2,0},{3,1},{4,6},{5,7},{6,4},{7,5},{8,10},{9,11},{10,... | collective-permute-start | bytes 393224 | tf_op jit(solution)/shard_map/ppermute | solution.py:22
  76.9 0.1 collective-permute-start.15
  77.1 3.4 %collective-permute-done.13.g1 = f32[256,128]{1,0:T(8,128)S(1)} collective-permute-done((f32[256,128]{1,0:T(8,128)S(1)}, f32[256,128]{1,0:T(8,128)S(1)}, u32[]{:S(2)}, u32[]{:S(2)}) %collective-permute-start.13) | collective-permute-done | bytes 131104 | tf_op jit(solution)/shard_map/ppermute | solution.py:22
  80.4 1.4 %collective-permute-done.14.g2 = f32[256,128]{1,0:T(8,128)S(1)} collective-permute-done((f32[256,128]{1,0:T(8,128)S(1)}, f32[256,128]{1,0:T(8,128)S(1)}, u32[]{:S(2)}, u32[]{:S(2)}) %collective-permute-start.14) | collective-permute-done | bytes 131104 | tf_op jit(solution)/shard_map/ppermute | solution.py:22
  81.8 0.1 collective-permute-done.15.g3
  81.9 0.6 copy-done.4
  82.5 0.1 copy-done.5
  82.6 1.8 %sum_x.1 = (f32[64,128]{1,0:T(8,128)}, f32[64,128]{1,0:T(8,128)}, f32[64,128]{1,0:T(8,128)}, f32[64,128]{1,0:T(8,128)}) custom-call(f32[256,128]{1,0:T(8,128)} %copy-done, f32[256,128]{1,0:T(8,128)} %copy-done.3, f32[256,128]{1,0:T(8,128)} %copy-done.4, f32[256,128]{1,0:T(8,128)} %copy-done.5), custom_call_target="tpu_custom_call" | custom-call | tf_op jit(solution)/shard_map/sum_x/pallas_call | solution.py:155
  84.3 2.9 %collective-permute-start.16 = (f32[64,128]{1,0:T(8,128)}, f32[64,128]{1,0:T(8,128)S(1)}, u32[]{:S(2)}, u32[]{:S(2)}) collective-permute-start(f32[64,128]{1,0:T(8,128)} %get-tuple-element.26), channel_id=1, source_target_pairs={{0,8},{8,16},{16,24},{24,0},{1,9},{9,17},{17,25},{25,1},{2,10},{10... | collective-permute-start | bytes 98312 | tf_op jit(solution)/shard_map/ppermute | solution.py:22
  87.2 1.6 %collective-permute-start.17 = (f32[64,128]{1,0:T(8,128)}, f32[64,128]{1,0:T(8,128)S(1)}, u32[]{:S(2)}, u32[]{:S(2)}) collective-permute-start(f32[64,128]{1,0:T(8,128)} %get-tuple-element.27), channel_id=1, source_target_pairs={{0,16},{8,24},{16,0},{24,8},{1,17},{9,25},{17,1},{25,9},{2,18},{10... | collective-permute-start | bytes 98312 | tf_op jit(solution)/shard_map/ppermute | solution.py:22
  88.7 1.7 %collective-permute-start.18 = (f32[64,128]{1,0:T(8,128)}, f32[64,128]{1,0:T(8,128)S(1)}, u32[]{:S(2)}, u32[]{:S(2)}) collective-permute-start(f32[64,128]{1,0:T(8,128)} %get-tuple-element.28), channel_id=1, source_target_pairs={{0,24},{8,0},{16,8},{24,16},{1,25},{9,1},{17,9},{25,17},{2,26},{10... | collective-permute-start | bytes 98312 | tf_op jit(solution)/shard_map/ppermute | solution.py:22
  90.4 0.0 collective-permute-done.16.p1
  90.4 2.4 %collective-permute-done.17.p2 = f32[64,128]{1,0:T(8,128)S(1)} collective-permute-done((f32[64,128]{1,0:T(8,128)}, f32[64,128]{1,0:T(8,128)S(1)}, u32[]{:S(2)}, u32[]{:S(2)}) %collective-permute-start.17) | collective-permute-done | bytes 32800 | tf_op jit(solution)/shard_map/ppermute | solution.py:22
  92.8 0.0 collective-permute-done.18.p3
  92.9 0.6 copy-done.7
  93.4 0.1 copy-done.8
  93.5 1.5 %place.1 = f32[64,512]{1,0:T(8,128)} custom-call(f32[64,128]{1,0:T(8,128)} %get-tuple-element.25.p0, f32[64,128]{1,0:T(8,128)} %copy-done.6, f32[64,128]{1,0:T(8,128)} %copy-done.7, f32[64,128]{1,0:T(8,128)} %copy-done.8), custom_call_target="tpu_custom_call" | custom-call | tf_op jit(solution)/shard_map/place/pallas_call | solution.py:172
  (14 shorter events, 0.0 us)
Async XLA Ops:
  0.0 0.8 copy-start.1
  0.8 13.5 %copy-start.2 = (bf16[256,256]{1,0:T(8,128)(2,1)S(1)}, bf16[256,256]{1,0:T(8,128)(2,1)}, u32[]{:S(2)}) copy-start(bf16[256,256]{1,0:T(8,128)(2,1)} %param.5) | copy-start | bytes 393220
  8.5 29.8 %collective-permute-start = (bf16[12,64,256]{2,1,0:T(8,128)(2,1)S(1)}, bf16[12,64,256]{2,1,0:T(8,128)(2,1)S(1)}, u32[]{:S(2)}, u32[]{:S(2)}) collective-permute-start(bf16[12,64,256]{2,1,0:T(8,128)(2,1)S(1)} %get-tuple-element.18), channel_id=1, source_target_pairs={{0,1},{1,2},{2,3},{3,0},{4,5},{5,6},{6,7},{7,4},{8,9},{9,10},{10,1... | collective-permute-start | bytes 1179656 | tf_op jit(solution)/shard_map/ppermute | solution.py:22
  10.1 28.2 %collective-permute-start.1 = (bf16[12,64,256]{2,1,0:T(8,128)(2,1)S(1)}, bf16[12,64,256]{2,1,0:T(8,128)(2,1)S(1)}, u32[]{:S(2)}, u32[]{:S(2)}) collective-permute-start(bf16[12,64,256]{2,1,0:T(8,128)(2,1)S(1)} %get-tuple-element.19), channel_id=1, source_target_pairs={{0,2},{1,3},{2,0},{3,1},{4,6},{5,7},{6,4},{7,5},{8,10},{9,11},{10,... | collective-permute-start | bytes 1179656 | tf_op jit(solution)/shard_map/ppermute | solution.py:22
  12.8 25.5 %collective-permute-start.2 = (bf16[12,64,256]{2,1,0:T(8,128)(2,1)S(1)}, bf16[12,64,256]{2,1,0:T(8,128)(2,1)S(1)}, u32[]{:S(2)}, u32[]{:S(2)}) collective-permute-start(bf16[12,64,256]{2,1,0:T(8,128)(2,1)S(1)} %get-tuple-element.20), channel_id=1, source_target_pairs={{0,3},{1,0},{2,1},{3,2},{4,7},{5,4},{6,5},{7,6},{8,11},{9,8},{10,9... | collective-permute-start | bytes 1179656 | tf_op jit(solution)/shard_map/ppermute | solution.py:22
  39.5 7.8 %collective-permute-start.9 = (bf16[64,3072]{1,0:T(8,128)(2,1)S(1)}, bf16[64,3072]{1,0:T(8,128)(2,1)S(1)}, u32[]{:S(2)}, u32[]{:S(2)}) collective-permute-start(bf16[64,3072]{1,0:T(8,128)(2,1)S(1)} %column.1.refs_0_.refs_4_), channel_id=1, source_target_pairs={{0,4},{4,0},{1,5},{5,1},{2,6},{6,2},{3,7},{7,3},{8,12},{12,8},{9,1... | collective-permute-start | bytes 1179656 | tf_op jit(solution)/shard_map/ppermute | solution.py:22
  39.6 12.7 %collective-permute-start.8 = (bf16[64,3072]{1,0:T(8,128)(2,1)S(1)}, bf16[64,3072]{1,0:T(8,128)(2,1)S(1)}, u32[]{:S(2)}, u32[]{:S(2)}) collective-permute-start(bf16[64,3072]{1,0:T(8,128)(2,1)S(1)} %column.1.refs_0_.refs_4_), channel_id=1, source_target_pairs={{0,32},{32,64},{64,96},{96,0},{1,33},{33,65},{65,97},{97,1},{2,34}... | collective-permute-start | bytes 1179656 | tf_op jit(solution)/shard_map/ppermute | solution.py:22
  41.1 20.8 %collective-permute-start.7 = (bf16[64,3072]{1,0:T(8,128)(2,1)S(1)}, bf16[64,3072]{1,0:T(8,128)(2,1)S(1)}, u32[]{:S(2)}, u32[]{:S(2)}) collective-permute-start(bf16[64,3072]{1,0:T(8,128)(2,1)S(1)} %column.1.refs_0_.refs_4_), channel_id=1, source_target_pairs={{0,64},{32,96},{64,0},{96,32},{1,65},{33,97},{65,1},{97,33},{2,66}... | collective-permute-start | bytes 1179656 | tf_op jit(solution)/shard_map/ppermute | solution.py:22
  44.0 17.9 %collective-permute-start.6 = (bf16[64,3072]{1,0:T(8,128)(2,1)S(1)}, bf16[64,3072]{1,0:T(8,128)(2,1)S(1)}, u32[]{:S(2)}, u32[]{:S(2)}) collective-permute-start(bf16[64,3072]{1,0:T(8,128)(2,1)S(1)} %column.1.refs_0_.refs_4_), channel_id=1, source_target_pairs={{0,96},{32,0},{64,32},{96,64},{1,97},{33,1},{65,33},{97,65},{2,98}... | collective-permute-start | bytes 1179656 | tf_op jit(solution)/shard_map/ppermute | solution.py:22
  45.4 17.0 %collective-permute-start.5 = (bf16[64,3072]{1,0:T(8,128)(2,1)S(1)}, bf16[64,3072]{1,0:T(8,128)(2,1)S(1)}, u32[]{:S(2)}, u32[]{:S(2)}) collective-permute-start(bf16[64,3072]{1,0:T(8,128)(2,1)S(1)} %column.1.refs_0_.refs_4_), channel_id=1, source_target_pairs={{0,8},{8,16},{16,24},{24,0},{1,9},{9,17},{17,25},{25,1},{2,10},{10... | collective-permute-start | bytes 1179656 | tf_op jit(solution)/shard_map/ppermute | solution.py:22
  47.3 20.6 %collective-permute-start.4 = (bf16[64,3072]{1,0:T(8,128)(2,1)S(1)}, bf16[64,3072]{1,0:T(8,128)(2,1)S(1)}, u32[]{:S(2)}, u32[]{:S(2)}) collective-permute-start(bf16[64,3072]{1,0:T(8,128)(2,1)S(1)} %column.1.refs_0_.refs_4_), channel_id=1, source_target_pairs={{0,16},{8,24},{16,0},{24,8},{1,17},{9,25},{17,1},{25,9},{2,18},{10... | collective-permute-start | bytes 1179656 | tf_op jit(solution)/shard_map/ppermute | solution.py:22
  52.4 15.5 %collective-permute-start.3 = (bf16[64,3072]{1,0:T(8,128)(2,1)S(1)}, bf16[64,3072]{1,0:T(8,128)(2,1)S(1)}, u32[]{:S(2)}, u32[]{:S(2)}) collective-permute-start(bf16[64,3072]{1,0:T(8,128)(2,1)S(1)} %column.1.refs_0_.refs_4_), channel_id=1, source_target_pairs={{0,24},{8,0},{16,8},{24,16},{1,25},{9,1},{17,9},{25,17},{2,26},{10... | collective-permute-start | bytes 1179656 | tf_op jit(solution)/shard_map/ppermute | solution.py:22
  61.9 6.0 %collective-permute-start.12 = (bf16[64,3072]{1,0:T(8,128)(2,1)S(1)}, bf16[64,3072]{1,0:T(8,128)(2,1)S(1)}, u32[]{:S(2)}, u32[]{:S(2)}) collective-permute-start(bf16[64,3072]{1,0:T(8,128)(2,1)S(1)} %collective-permute-done.8.refs_7_), channel_id=1, source_target_pairs={{0,4},{4,0},{1,5},{5,1},{2,6},{6,2},{3,7},{7,3},{8,12},{12,8},{9,1... | collective-permute-start | bytes 1179656 | tf_op jit(solution)/shard_map/ppermute | solution.py:22
  61.9 6.0 %collective-permute-start.11 = (bf16[64,3072]{1,0:T(8,128)(2,1)S(1)}, bf16[64,3072]{1,0:T(8,128)(2,1)S(1)}, u32[]{:S(2)}, u32[]{:S(2)}) collective-permute-start(bf16[64,3072]{1,0:T(8,128)(2,1)S(1)} %collective-permute-done.7.refs_6_), channel_id=1, source_target_pairs={{0,4},{4,0},{1,5},{5,1},{2,6},{6,2},{3,7},{7,3},{8,12},{12,8},{9,1... | collective-permute-start | bytes 1179656 | tf_op jit(solution)/shard_map/ppermute | solution.py:22
  62.4 5.5 %collective-permute-start.10 = (bf16[64,3072]{1,0:T(8,128)(2,1)S(1)}, bf16[64,3072]{1,0:T(8,128)(2,1)S(1)}, u32[]{:S(2)}, u32[]{:S(2)}) collective-permute-start(bf16[64,3072]{1,0:T(8,128)(2,1)S(1)} %collective-permute-done.6.refs_5_), channel_id=1, source_target_pairs={{0,4},{4,0},{1,5},{5,1},{2,6},{6,2},{3,7},{7,3},{8,12},{12,8},{9,1... | collective-permute-start | bytes 1179656 | tf_op jit(solution)/shard_map/ppermute | solution.py:22
  72.3 0.7 copy-start
  73.0 7.5 %collective-permute-start.13 = (f32[256,128]{1,0:T(8,128)S(1)}, f32[256,128]{1,0:T(8,128)S(1)}, u32[]{:S(2)}, u32[]{:S(2)}) collective-permute-start(f32[256,128]{1,0:T(8,128)S(1)} %get-tuple-element.22), channel_id=1, source_target_pairs={{0,1},{1,2},{2,3},{3,0},{4,5},{5,6},{6,7},{7,4},{8,9},{9,10},{10,1... | collective-permute-start | bytes 393224 | tf_op jit(solution)/shard_map/ppermute | solution.py:22
  74.3 7.6 %collective-permute-start.14 = (f32[256,128]{1,0:T(8,128)S(1)}, f32[256,128]{1,0:T(8,128)S(1)}, u32[]{:S(2)}, u32[]{:S(2)}) collective-permute-start(f32[256,128]{1,0:T(8,128)S(1)} %get-tuple-element.23), channel_id=1, source_target_pairs={{0,2},{1,3},{2,0},{3,1},{4,6},{5,7},{6,4},{7,5},{8,10},{9,11},{10,... | collective-permute-start | bytes 393224 | tf_op jit(solution)/shard_map/ppermute | solution.py:22
  76.9 5.0 %collective-permute-start.15 = (f32[256,128]{1,0:T(8,128)S(1)}, f32[256,128]{1,0:T(8,128)S(1)}, u32[]{:S(2)}, u32[]{:S(2)}) collective-permute-start(f32[256,128]{1,0:T(8,128)S(1)} %get-tuple-element.24), channel_id=1, source_target_pairs={{0,3},{1,0},{2,1},{3,2},{4,7},{5,4},{6,5},{7,6},{8,11},{9,8},{10,9... | collective-permute-start | bytes 393224 | tf_op jit(solution)/shard_map/ppermute | solution.py:22
  80.4 1.5 %copy-start.3 = (f32[256,128]{1,0:T(8,128)}, f32[256,128]{1,0:T(8,128)S(1)}, u32[]{:S(2)}) copy-start(f32[256,128]{1,0:T(8,128)S(1)} %collective-permute-done.13.g1) | copy-start | bytes 393220
  81.8 0.6 copy-start.4
  81.9 0.6 copy-start.5
  84.3 6.1 %collective-permute-start.16 = (f32[64,128]{1,0:T(8,128)}, f32[64,128]{1,0:T(8,128)S(1)}, u32[]{:S(2)}, u32[]{:S(2)}) collective-permute-start(f32[64,128]{1,0:T(8,128)} %get-tuple-element.26), channel_id=1, source_target_pairs={{0,8},{8,16},{16,24},{24,0},{1,9},{9,17},{17,25},{25,1},{2,10},{10... | collective-permute-start | bytes 98312 | tf_op jit(solution)/shard_map/ppermute | solution.py:22
  87.2 5.6 %collective-permute-start.17 = (f32[64,128]{1,0:T(8,128)}, f32[64,128]{1,0:T(8,128)S(1)}, u32[]{:S(2)}, u32[]{:S(2)}) collective-permute-start(f32[64,128]{1,0:T(8,128)} %get-tuple-element.27), channel_id=1, source_target_pairs={{0,16},{8,24},{16,0},{24,8},{1,17},{9,25},{17,1},{25,9},{2,18},{10... | collective-permute-start | bytes 98312 | tf_op jit(solution)/shard_map/ppermute | solution.py:22
  88.7 4.1 %collective-permute-start.18 = (f32[64,128]{1,0:T(8,128)}, f32[64,128]{1,0:T(8,128)S(1)}, u32[]{:S(2)}, u32[]{:S(2)}) collective-permute-start(f32[64,128]{1,0:T(8,128)} %get-tuple-element.28), channel_id=1, source_target_pairs={{0,24},{8,0},{16,8},{24,16},{1,25},{9,1},{17,9},{25,17},{2,26},{10... | collective-permute-start | bytes 98312 | tf_op jit(solution)/shard_map/ppermute | solution.py:22
  90.4 2.4 %copy-start.6 = (f32[64,128]{1,0:T(8,128)}, f32[64,128]{1,0:T(8,128)S(1)}, u32[]{:S(2)}) copy-start(f32[64,128]{1,0:T(8,128)S(1)} %collective-permute-done.16.p1) | copy-start | bytes 98308
  92.8 0.6 copy-start.7
  92.9 0.6 copy-start.8

commit v2 on v0

v2 whole, which is shorter than its diff:
```python
import functools

import jax
import jax.numpy as jnp
from jax import lax
from jax.experimental import pallas as pl
from jax.experimental.pallas import tpu as pltpu
from jax.sharding import Mesh, PartitionSpec as P

R3 = 48
R2 = 256
N = 4
RX = R3 // N
SCALE = 1.0 / (R3 * R2)
IN_ROWS = 8
OUT_ROWS = 16
EARLY = 20_000_000_000
LATE = 100_000_000
BF = jnp.bfloat16
F32 = jnp.float32
VMEM = pl.BlockSpec(memory_space=pltpu.VMEM)


def shift(v, axis, by):
    names = ("core", "x") if axis == "x" else (axis, "core")
    index = (lambda i, c: N * c + i) if axis == "x" else (lambda i, c: 2 * i + c)
    pairs = [(index(i, c), index((i + by * (1 - 2 * c)) % N, c)) for i in range(N) for c in range(2)]
    return lax.ppermute(v, names, pairs)


def swap(v):
    return lax.ppermute(v, "core", [(0, 1), (1, 0)])


def params(mib):
    return pltpu.CompilerParams(vmem_limit_bytes=mib * 1024 * 1024)


def band_kernel(first, bt_hbm, pix_ref, *rest):
    outs, (bt_ref, basis, buf, stage, sem, bt_sem) = rest[:N], rest[N:]
    bt_copy = pltpu.make_async_copy(bt_hbm, bt_ref, bt_sem)
    bt_copy.start()
    h = outs[0].shape[1]
    copies = [
        pltpu.make_async_copy(
            pix_ref.at[pl.ds(first + IN_ROWS * g, IN_ROWS)], buf.at[pl.ds(IN_ROWS * g, IN_ROWS)], sem.at[g]
        )
        for g in range(h // IN_ROWS)
    ]
    for copy in copies:
        copy.start()
    x, core = lax.axis_index("x"), lax.axis_index("core")
    basis[...] = jnp.zeros_like(basis)
    bt_copy.wait()
    for k in range(N):
        for c in range(2):

            @pl.when((x == k) & (core == c))
            def _():
                for j in range(N):
                    at = RX * ((k + j * (1 - 2 * c)) % N)
                    basis[16 * j : 16 * j + RX, :] = bt_ref[at : at + RX, :]

    for q in range(h // OUT_ROWS):
        for i in range(OUT_ROWS):
            row = OUT_ROWS * q + i
            if row % IN_ROWS == 0:
                copies[row // IN_ROWS].wait()
            banded = jnp.dot(basis[...], buf[row], preferred_element_type=F32)
            for t in range(2):
                stage[t, 64 * i : 64 * (i + 1), :] = banded[:, 128 * t : 128 * (t + 1)]
        at = slice(OUT_ROWS * q, OUT_ROWS * (q + 1))
        for j in range(N):
            for r in range(RX):
                for t in range(2):
                    rows = stage[t, pl.ds(16 * j + r, OUT_ROWS, stride=64), :]
                    outs[j][r, at, 128 * t : 128 * (t + 1)] = rows.astype(BF)


def band(bt, pix, first, h):
    _, bands, c = pix.shape
    return pl.pallas_call(
        functools.partial(band_kernel, first),
        in_specs=[pl.BlockSpec(memory_space=pl.ANY)] * 2,
        out_specs=[VMEM] * N,
        out_shape=[jax.ShapeDtypeStruct((RX, h, c), BF)] * N,
        scratch_shapes=[
            pltpu.VMEM((R3, bands), BF),
            pltpu.VMEM((64, bands), BF),
            pltpu.VMEM((h, bands, c), BF),
            pltpu.VMEM((2, 64 * OUT_ROWS, c // 2), F32),
            pltpu.SemaphoreType.DMA((h // IN_ROWS,)),
            pltpu.SemaphoreType.DMA,
        ],
        compiler_params=params(48),
        cost_estimate=pl.CostEstimate(
            flops=2 * h * c * bands * 256, bytes_accessed=h * c * bands * 2, transcendentals=0
        ),
        name="band",
    )(bt, pix)


def column_kernel(*refs):
    blocks, cols, out_ref = refs[:N], refs[N : 2 * N], refs[2 * N]
    r, h, c = blocks[0].shape
    total = jnp.zeros((r * h, R2), F32)
    for b, col in zip(blocks, cols):
        total += jnp.dot(b[...].reshape(r * h, c), col[...], preferred_element_type=F32)
    for i in range(r):
        out_ref[:, R2 * i : R2 * (i + 1)] = total[h * i : h * (i + 1), :].astype(BF)


def column(blocks, cols, flops):
    r, h, c = blocks[0].shape
    return pl.pallas_call(
        column_kernel,
        in_specs=[VMEM] * (2 * N),
        out_specs=VMEM,
        out_shape=jax.ShapeDtypeStruct((h, r * R2), BF),
        compiler_params=params(8),
        cost_estimate=pl.CostEstimate(
            flops=flops, bytes_accessed=2 * 5 * r * h * c, transcendentals=0
        ),
        name="column",
    )(*blocks, *cols)


def gram_kernel(zs, ys, early, late, *refs):
    outs, rhs = refs[:N], refs[N]
    x, y, core = lax.axis_index("x"), lax.axis_index("y"), lax.axis_index("core")
    n = zs.shape[0] // N
    for d in range(N):
        owner = lax.rem((1 - 2 * core) * (y - x) + d + N, N)
        theirs = (early, 0) if d in (0, 3) else (late, 2)
        for half, (block, base), e in ((core, (ys, 0), d), (1 - core, theirs, (N - d) % N)):
            e -= base
            at = pl.multiple_of((owner * 2 + half) * n, n)
            rhs[pl.ds(at, n), :] = block[n * e : n * (e + 1), :]
    for d in range(N):
        outs[d][...] = lax.dot_general(
            zs[...],
            rhs[2 * n * d : 2 * n * (d + 1), :],
            (((1,), (1,)), ((), ())),
            preferred_element_type=F32,
        )


def gram(zs, ys, early, late):
    n, k = zs.shape
    return pl.pallas_call(
        gram_kernel,
        in_specs=[VMEM] * 4,
        out_specs=[VMEM] * N,
        out_shape=[jax.ShapeDtypeStruct((n, n // 2), F32)] * N,
        scratch_shapes=[pltpu.VMEM((2 * n, k), BF)],
        compiler_params=params(12),
        cost_estimate=pl.CostEstimate(
            flops=4 * n * n * k, bytes_accessed=2 * 3 * n * k, transcendentals=0
        ),
        name="gram",
    )(zs, ys, early, late)


def sum_kernel(g0, g1, g2, g3, *outs):
    n = outs[0].shape[0]
    for d in range(N):
        at = slice(n * d, n * (d + 1))
        outs[d][...] = (g0[at, :] + g1[at, :] + g2[at, :] + g3[at, :]) * SCALE


def sum_x(parts):
    n, m = parts[0].shape
    return pl.pallas_call(
        sum_kernel,
        in_specs=[VMEM] * N,
        out_specs=[VMEM] * N,
        out_shape=[jax.ShapeDtypeStruct((n // N, m), F32)] * N,
        compiler_params=params(2),
        name="sum_x",
    )(*parts)


def place_kernel(*refs):
    parts, out_ref = refs[:N], refs[N]
    z, core = lax.axis_index("z"), lax.axis_index("core")
    m = parts[0].shape[1]
    for d, part in enumerate(parts):
        at = pl.multiple_of(lax.rem(z - (1 - 2 * core) * d + N, N) * m, m)
        out_ref[:, pl.ds(at, m)] = part[...]


def place(parts):
    n, m = parts[0].shape
    return pl.pallas_call(
        place_kernel,
        in_specs=[VMEM] * N,
        out_shape=jax.ShapeDtypeStruct((n, N * m), F32),
        compiler_params=params(2),
        name="place",
    )(*parts)


def spread(parts, axis):
    return [parts[0]] + [shift(parts[d], axis, d) for d in range(1, N)]


def local(pixels, band_basis, column_basis):
    pix, bt = pixels.transpose(0, 2, 1), band_basis.T
    h = pix.shape[0] // 2
    near = shift(column_basis, "x", 1)
    first = band(bt, pix, 0, h)
    first, near = lax.optimization_barrier((first, near))
    cols = [column_basis, near, shift(near, "x", 1), swap(near)]
    first = spread(first, "x")
    second = list(band(bt, pix, h, h))
    first, second[0] = lax.optimization_barrier((first, second[0]))
    second = spread(second, "x")
    mine = [column(first, cols, EARLY)]
    up = [[shift(mine[0], axis, -1)] for axis in "yz"]
    second, up = lax.optimization_barrier((second, up))
    mine.append(column(second, cols, LATE))
    far = [[shift(up[i][0], axis, -1)] for i, axis in enumerate("yz")]
    whole = jnp.concatenate(mine, axis=0)
    for i, axis in enumerate("yz"):
        up[i].append(shift(mine[1], axis, -1))
    for i, axis in enumerate("yz"):
        far[i].append(shift(up[i][1], axis, -1))
    down = [shift(whole, axis, 1) for axis in "yz"]
    early = swap(jnp.concatenate(mine + up[0], axis=0))
    early, far, down = lax.optimization_barrier((early, far, down))
    late = jnp.concatenate(far[0] + [down[0]], axis=0)
    ys = jnp.concatenate(mine + up[0] + [late], axis=0)
    zs = jnp.concatenate(mine + up[1] + far[1] + [down[1]], axis=0)
    parts = sum_x(spread(gram(zs, ys, early, swap(late)), "x"))
    return place(spread(parts, "z"))


def solution(mesh):
    inner = Mesh(mesh.devices.reshape(4, 4, 2, 4), ("y", "z", "core", "x"))
    return jax.shard_map(
        local,
        mesh=inner,
        in_specs=(P(("y", "z", "core"), "x", None), P(), P("x", None)),
        out_specs=P(("y", "z", "core"), "x"),
        check_vma=False,
    )
```

time: 161 us -> 77.6 us (0.48)
  waiting for transfers between devices: 125 us -> 26.8 us
  starting transfers between devices: 0.09 us -> 37.2 us
  matrix products: 19.3 us -> 0 us
  between operations: 13.1 us -> 0.22 us
  Pallas kernels: 0 us -> 11.7 us
  other arithmetic: 3.55 us -> 0.14 us
    all_gather x1 -> x0, waiting for transfers between devices: 63.1 us -> none  [local(): lax.all_gather(projected, 'rows', axis=1, tiled=True)]
    reduce_scatter x2 -> x0, waiting for transfers between devices: 61.8 us -> none  [the longest x1 40.8 us: local(): lax.psum_scatter(jnp.einsum('rhc,cs->rhs', banded, column_basis, preferre...]
    ppermute x0 -> x27, starting transfers between devices: none -> 37.2 us  [the longest x24 37 us: shift(): return lax.ppermute(v, names, pairs)]
    ppermute x0 -> x27, waiting for transfers between devices: none -> 26.8 us  [the longest x24 24.6 us: shift(): return lax.ppermute(v, names, pairs)]
    dot_general x3 -> x0, matrix products: 19.3 us -> none  [the longest x1 9.42 us: local(): jnp.einsum('rhs,rks->hk', projected, lax.all_gather(projected, 'rows', ax...]
    pallas_call x0 -> x7, Pallas kernels: none -> 11.7 us  [the longest x2 8.27 us: band(): pl.pallas_call(functools.partial(band_kernel, first), in_specs=[pl.BlockS...]
    convert_element_type x1 -> x0, other arithmetic: 1.97 us -> none  [local(): projected = lax.psum_scatter(jnp.einsum('rhc,cs->rhs', banded, column_bas...]
  transfers between devices with their start and end apart: 3 -> 27, of which waited for: 3 -> 12; matrix products, arithmetic and copies ran while one was open for 0% -> 0% of each run, Pallas kernels for 0% -> 11%
where the time goes in v2:
time: 77.6 us; the launch traced here: 77.2 us
  starting transfers between devices  37.2 us (48%)
  waiting for transfers between devices  26.8 us (35%)
  Pallas kernels  11.7 us (15%)
  local copies, waits for them, and re-layouts  1.11 us (1%)
    ppermute x24, starting transfers between devices, shift(): return lax.ppermute(v, names, pairs)  37 us
    ppermute x24, waiting for transfers between devices, shift(): return lax.ppermute(v, names, pairs)  24.6 us
    pallas_call x2, Pallas kernels, band(): pl.pallas_call(functools.partial(band_kernel, first), in_specs=[pl.BlockS...  8.27 us
    ppermute x3, waiting for transfers between devices, swap(): return lax.ppermute(v, 'core', [(0, 1), (1, 0)])  2.17 us
    pallas_call x1, Pallas kernels, gram(): pl.pallas_call(gram_kernel, in_specs=[VMEM] * 4, out_specs=[VMEM] * N, ou...  2.01 us
  transfers between devices with their start and end apart: 27, of which 12 were waited for; matrix products, arithmetic and copies ran while one was open for 0% of the time, Pallas kernels for 11%

profile of v2, /device:TPU:0, one launch (start us, length us, event | category | flops | bytes accessed | tf_op | source)
XLA Modules:
  0.0 77.2 jit_solution(2726898291147149841)
XLA Ops:
  0.0 1.6 %collective-permute-start = (bf16[256,256]{1,0:T(8,128)(2,1)}, bf16[256,256]{1,0:T(8,128)(2,1)S(1)}, u32[]{:S(2)}, u32[]{:S(2)}) collective-permute-start(bf16[256,256]{1,0:T(8,128)(2,1)} %refs_4_.3), channel_id=1, source_target_pairs={{0,1},{4,7},{1,2},{5,4},{2,3},{6,5},{3,0},{7,6},{8,9},{12,15},{9,1... | collective-permute-start | bytes 393224 | tf_op jit(solution)/shard_map/ppermute | solution.py:28
  1.6 0.8 %copy-done = bf16[424,48]{0,1:T(8,128)(2,1)S(1)} copy-done((bf16[424,48]{0,1:T(8,128)(2,1)S(1)}, bf16[424,48]{0,1:T(8,128)(2,1)}, u32[]{:S(2)}) %copy-start) | copy-done | bytes 40728
  2.4 4.1 %band.2 = (bf16[12,32,256]{2,1,0:T(8,128)(2,1)S(1)}, bf16[12,32,256]{2,1,0:T(8,128)(2,1)S(1)}, bf16[12,32,256]{2,1,0:T(8,128)(2,1)S(1)}, bf16[12,32,256]{2,1,0:T(8,128)(2,1)S(1)}) custom-call(bf16[48,424]{1,0:T(8,128)(2,1)S(1)} %bitcast.2, bf16[64,424,256]{2,1,0:T(8,128)(2,1)} %bitcast.4), custom_call_target="tpu_custom_call" | custom-call | flops 1778384896 | bytes 6946816 | tf_op jit(solution)/shard_map/band/pallas_call | solution.py:82
  6.5 0.0 copy-start.1
  6.5 1.6 %collective-permute-start.1 = (bf16[12,32,256]{2,1,0:T(8,128)(2,1)S(1)}, bf16[12,32,256]{2,1,0:T(8,128)(2,1)S(1)}, u32[]{:S(2)}, u32[]{:S(2)}) collective-permute-start(bf16[12,32,256]{2,1,0:T(8,128)(2,1)S(1)} %get-tuple-element.49), channel_id=1, source_target_pairs={{0,1},{4,7},{1,2},{5,4},{2,3},{6,5},{3,0},{7,6},{8,9},{12,15},{9,1... | collective-permute-start | bytes 589832 | tf_op jit(solution)/shard_map/ppermute | solution.py:28
  8.1 1.6 %collective-permute-start.2 = (bf16[12,32,256]{2,1,0:T(8,128)(2,1)S(1)}, bf16[12,32,256]{2,1,0:T(8,128)(2,1)S(1)}, u32[]{:S(2)}, u32[]{:S(2)}) collective-permute-start(bf16[12,32,256]{2,1,0:T(8,128)(2,1)S(1)} %get-tuple-element.50), channel_id=1, source_target_pairs={{0,2},{4,6},{1,3},{5,7},{2,0},{6,4},{3,1},{7,5},{8,10},{12,14},{9,... | collective-permute-start | bytes 589832 | tf_op jit(solution)/shard_map/ppermute | solution.py:28
  9.7 2.2 %collective-permute-start.3 = (bf16[12,32,256]{2,1,0:T(8,128)(2,1)S(1)}, bf16[12,32,256]{2,1,0:T(8,128)(2,1)S(1)}, u32[]{:S(2)}, u32[]{:S(2)}) collective-permute-start(bf16[12,32,256]{2,1,0:T(8,128)(2,1)S(1)} %get-tuple-element.51), channel_id=1, source_target_pairs={{0,3},{4,5},{1,0},{5,6},{2,1},{6,7},{3,2},{7,4},{8,11},{12,13},{9,... | collective-permute-start | bytes 589832 | tf_op jit(solution)/shard_map/ppermute | solution.py:28
  12.0 4.1 %band.3 = (bf16[12,32,256]{2,1,0:T(8,128)(2,1)S(1)}, bf16[12,32,256]{2,1,0:T(8,128)(2,1)S(1)}, bf16[12,32,256]{2,1,0:T(8,128)(2,1)S(1)}, bf16[12,32,256]{2,1,0:T(8,128)(2,1)S(1)}) custom-call(bf16[48,424]{1,0:T(8,128)(2,1)S(1)} %bitcast.3, bf16[64,424,256]{2,1,0:T(8,128)(2,1)} %bitcast.5), custom_call_target="tpu_custom_call" | custom-call | flops 1778384896 | bytes 6946816 | tf_op jit(solution)/shard_map/band/pallas_call | solution.py:82
  16.1 2.8 %collective-permute-done.1.refs_1_ = bf16[12,32,256]{2,1,0:T(8,128)(2,1)S(1)} collective-permute-done((bf16[12,32,256]{2,1,0:T(8,128)(2,1)S(1)}, bf16[12,32,256]{2,1,0:T(8,128)(2,1)S(1)}, u32[]{:S(2)}, u32[]{:S(2)}) %collective-permute-start.1) | collective-permute-done | bytes 196640 | tf_op jit(solution)/shard_map/ppermute | solution.py:28
  18.9 2.0 %collective-permute-start.7 = (bf16[12,32,256]{2,1,0:T(8,128)(2,1)S(1)}, bf16[12,32,256]{2,1,0:T(8,128)(2,1)S(1)}, u32[]{:S(2)}, u32[]{:S(2)}) collective-permute-start(bf16[12,32,256]{2,1,0:T(8,128)(2,1)S(1)} %get-tuple-element.60), channel_id=1, source_target_pairs={{0,2},{4,6},{1,3},{5,7},{2,0},{6,4},{3,1},{7,5},{8,10},{12,14},{9,... | collective-permute-start | bytes 589832 | tf_op jit(solution)/shard_map/ppermute | solution.py:28
  20.9 1.6 %collective-permute-start.8 = (bf16[12,32,256]{2,1,0:T(8,128)(2,1)S(1)}, bf16[12,32,256]{2,1,0:T(8,128)(2,1)S(1)}, u32[]{:S(2)}, u32[]{:S(2)}) collective-permute-start(bf16[12,32,256]{2,1,0:T(8,128)(2,1)S(1)} %get-tuple-element.61), channel_id=1, source_target_pairs={{0,3},{4,5},{1,0},{5,6},{2,1},{6,7},{3,2},{7,4},{8,11},{12,13},{9,... | collective-permute-start | bytes 589832 | tf_op jit(solution)/shard_map/ppermute | solution.py:28
  22.5 0.4 column.2
  22.9 3.1 %collective-permute-start.9 = (bf16[32,3072]{1,0:T(8,128)(2,1)S(1)}, bf16[32,3072]{1,0:T(8,128)(2,1)S(1)}, u32[]{:S(2)}, u32[]{:S(2)}) collective-permute-start(bf16[32,3072]{1,0:T(8,128)(2,1)S(1)} %column.2), channel_id=1, source_target_pairs={{0,96},{4,36},{32,0},{36,68},{64,32},{68,100},{96,64},{100,4},{1,9... | collective-permute-start | bytes 589832 | tf_op jit(solution)/shard_map/ppermute | solution.py:28
  26.0 4.0 %collective-permute-start.10 = (bf16[32,3072]{1,0:T(8,128)(2,1)S(1)}, bf16[32,3072]{1,0:T(8,128)(2,1)S(1)}, u32[]{:S(2)}, u32[]{:S(2)}) collective-permute-start(bf16[32,3072]{1,0:T(8,128)(2,1)S(1)} %column.2), channel_id=1, source_target_pairs={{0,24},{4,12},{8,0},{12,20},{16,8},{20,28},{24,16},{28,4},{1,25},{... | collective-permute-start | bytes 589832 | tf_op jit(solution)/shard_map/ppermute | solution.py:28
  30.0 1.6 %collective-permute-done.6.refs_1_ = bf16[12,32,256]{2,1,0:T(8,128)(2,1)S(1)} collective-permute-done((bf16[12,32,256]{2,1,0:T(8,128)(2,1)S(1)}, bf16[12,32,256]{2,1,0:T(8,128)(2,1)S(1)}, u32[]{:S(2)}, u32[]{:S(2)}) %collective-permute-start.6) | collective-permute-done | bytes 196640 | tf_op jit(solution)/shard_map/ppermute | solution.py:28
  31.7 1.5 %collective-permute-done.10 = bf16[32,3072]{1,0:T(8,128)(2,1)S(1)} collective-permute-done((bf16[32,3072]{1,0:T(8,128)(2,1)S(1)}, bf16[32,3072]{1,0:T(8,128)(2,1)S(1)}, u32[]{:S(2)}, u32[]{:S(2)}) %collective-permute-start.10) | collective-permute-done | bytes 196640 | tf_op jit(solution)/shard_map/ppermute | solution.py:28
  33.2 0.4 column.3
  33.6 3.8 %collective-permute-start.11 = (bf16[32,3072]{1,0:T(8,128)(2,1)S(1)}, bf16[32,3072]{1,0:T(8,128)(2,1)S(1)}, u32[]{:S(2)}, u32[]{:S(2)}) collective-permute-start(bf16[32,3072]{1,0:T(8,128)(2,1)S(1)} %column.3), channel_id=1, source_target_pairs={{0,24},{4,12},{8,0},{12,20},{16,8},{20,28},{24,16},{28,4},{1,25},{... | collective-permute-start | bytes 589832 | tf_op jit(solution)/shard_map/ppermute | solution.py:28
  37.4 1.5 %collective-permute-start.12 = (bf16[32,3072]{1,0:T(8,128)(2,1)S(1)}, bf16[32,3072]{1,0:T(8,128)(2,1)S(1)}, u32[]{:S(2)}, u32[]{:S(2)}) collective-permute-start(bf16[32,3072]{1,0:T(8,128)(2,1)S(1)} %column.3), channel_id=1, source_target_pairs={{0,96},{4,36},{32,0},{36,68},{64,32},{68,100},{96,64},{100,4},{1,9... | collective-permute-start | bytes 589832 | tf_op jit(solution)/shard_map/ppermute | solution.py:28
  38.9 0.1 copy.9
  39.1 0.8 %collective-permute-start.14 = (bf16[32,3072]{1,0:T(8,128)(2,1)S(1)}, bf16[32,3072]{1,0:T(8,128)(2,1)S(1)}, u32[]{:S(2)}, u32[]{:S(2)}) collective-permute-start(bf16[32,3072]{1,0:T(8,128)(2,1)S(1)} %collective-permute-done.9), channel_id=1, source_target_pairs={{0,96},{4,36},{32,0},{36,68},{64,32},{68,100},{96,64},{100,4},{1,9... | collective-permute-start | bytes 589832 | tf_op jit(solution)/shard_map/ppermute | solution.py:28
  39.9 0.5 collective-permute-start.16
  40.4 2.7 %collective-permute-done.12 = bf16[32,3072]{1,0:T(8,128)(2,1)S(1)} collective-permute-done((bf16[32,3072]{1,0:T(8,128)(2,1)S(1)}, bf16[32,3072]{1,0:T(8,128)(2,1)S(1)}, u32[]{:S(2)}, u32[]{:S(2)}) %collective-permute-start.12) | collective-permute-done | bytes 196640 | tf_op jit(solution)/shard_map/ppermute | solution.py:28
  43.0 0.1 pad_maximum_fusion
  43.1 0.1 collective-permute-start.13
  43.2 0.2 collective-permute-start.18
  43.4 0.1 collective-permute-start.19
  43.5 1.7 %collective-permute-done.14 = bf16[32,3072]{1,0:T(8,128)(2,1)S(1)} collective-permute-done((bf16[32,3072]{1,0:T(8,128)(2,1)S(1)}, bf16[32,3072]{1,0:T(8,128)(2,1)S(1)}, u32[]{:S(2)}, u32[]{:S(2)}) %collective-permute-start.14) | collective-permute-done | bytes 196640 | tf_op jit(solution)/shard_map/ppermute | solution.py:28
  45.1 2.7 %collective-permute-start.15 = (bf16[32,3072]{1,0:T(8,128)(2,1)S(1)}, bf16[32,3072]{1,0:T(8,128)(2,1)S(1)}, u32[]{:S(2)}, u32[]{:S(2)}) collective-permute-start(bf16[32,3072]{1,0:T(8,128)(2,1)S(1)} %collective-permute-done.12), channel_id=1, source_target_pairs={{0,96},{4,36},{32,0},{36,68},{64,32},{68,100},{96,64},{100,4},{1,9... | collective-permute-start | bytes 589832 | tf_op jit(solution)/shard_map/ppermute | solution.py:28
  47.9 2.0 %collective-permute-start.17 = (bf16[32,3072]{1,0:T(8,128)(2,1)S(1)}, bf16[32,3072]{1,0:T(8,128)(2,1)S(1)}, u32[]{:S(2)}, u32[]{:S(2)}) collective-permute-start(bf16[32,3072]{1,0:T(8,128)(2,1)S(1)} %collective-permute-done.11), channel_id=1, source_target_pairs={{0,24},{4,12},{8,0},{12,20},{16,8},{20,28},{24,16},{28,4},{1,25},{... | collective-permute-start | bytes 589832 | tf_op jit(solution)/shard_map/ppermute | solution.py:28
  49.9 3.1 %collective-permute-done.15 = bf16[32,3072]{1,0:T(8,128)(2,1)S(1)} collective-permute-done((bf16[32,3072]{1,0:T(8,128)(2,1)S(1)}, bf16[32,3072]{1,0:T(8,128)(2,1)S(1)}, u32[]{:S(2)}, u32[]{:S(2)}) %collective-permute-start.15) | collective-permute-done | bytes 196640 | tf_op jit(solution)/shard_map/ppermute | solution.py:28
  52.9 2.2 %collective-permute-done.17 = bf16[32,3072]{1,0:T(8,128)(2,1)S(1)} collective-permute-done((bf16[32,3072]{1,0:T(8,128)(2,1)S(1)}, bf16[32,3072]{1,0:T(8,128)(2,1)S(1)}, u32[]{:S(2)}, u32[]{:S(2)}) %collective-permute-start.17) | collective-permute-done | bytes 196640 | tf_op jit(solution)/shard_map/ppermute | solution.py:28
  55.2 0.1 pad_maximum_fusion.1
  55.3 0.1 collective-permute-start.20
  55.4 0.1 constant_dynamic-update-slice_fusion
  55.5 2.2 %collective-permute-done.20.late = bf16[128,3072]{1,0:T(8,128)(2,1)S(1)} collective-permute-done((bf16[128,3072]{1,0:T(8,128)(2,1)S(1)}, bf16[128,3072]{1,0:T(8,128)(2,1)S(1)}, u32[]{:S(2)}, u32[]{:S(2)}) %collective-permute-start.20) | collective-permute-done | bytes 786464 | tf_op jit(solution)/shard_map/ppermute | solution.py:32
  57.6 2.0 %gram.1 = (f32[256,128]{1,0:T(8,128)S(1)}, f32[256,128]{1,0:T(8,128)S(1)}, f32[256,128]{1,0:T(8,128)S(1)}, f32[256,128]{1,0:T(8,128)S(1)}) custom-call(bf16[256,3072]{1,0:T(8,128)(2,1)S(1)} %get-tuple-element.83.zs, bf16[256,3072]{1,0:T(8,128)(2,1)S(1)} %get-tuple-element.84.ys, bf16[128,3072]{1,0:T(8,128)(2,1)S(1)} %collective-permute-done.13.early, ...), custom_call_target="tpu_custom_call" | custom-call | flops 805306368 | bytes 4718592 | tf_op jit(solution)/shard_map/gram/pallas_call | solution.py:150
  59.6 0.1 collective-permute-start.21
  59.7 2.2 %collective-permute-start.22 = (f32[256,128]{1,0:T(8,128)S(1)}, f32[256,128]{1,0:T(8,128)S(1)}, u32[]{:S(2)}, u32[]{:S(2)}) collective-permute-start(f32[256,128]{1,0:T(8,128)S(1)} %get-tuple-element.77), channel_id=1, source_target_pairs={{0,2},{4,6},{1,3},{5,7},{2,0},{6,4},{3,1},{7,5},{8,10},{12,14},{9,... | collective-permute-start | bytes 393224 | tf_op jit(solution)/shard_map/ppermute | solution.py:28
  61.9 2.1 %collective-permute-start.23 = (f32[256,128]{1,0:T(8,128)S(1)}, f32[256,128]{1,0:T(8,128)S(1)}, u32[]{:S(2)}, u32[]{:S(2)}) collective-permute-start(f32[256,128]{1,0:T(8,128)S(1)} %get-tuple-element.78), channel_id=1, source_target_pairs={{0,3},{4,5},{1,0},{5,6},{2,1},{6,7},{3,2},{7,4},{8,11},{12,13},{9,... | collective-permute-start | bytes 393224 | tf_op jit(solution)/shard_map/ppermute | solution.py:28
  64.1 5.7 %collective-permute-done.21.g1 = f32[256,128]{1,0:T(8,128)S(1)} collective-permute-done((f32[256,128]{1,0:T(8,128)S(1)}, f32[256,128]{1,0:T(8,128)S(1)}, u32[]{:S(2)}, u32[]{:S(2)}) %collective-permute-start.21) | collective-permute-done | bytes 131104 | tf_op jit(solution)/shard_map/ppermute | solution.py:28
  69.8 0.1 collective-permute-start.24
  69.9 2.7 %collective-permute-start.25 = (f32[64,128]{1,0:T(8,128)S(1)}, f32[64,128]{1,0:T(8,128)S(1)}, u32[]{:S(2)}, u32[]{:S(2)}) collective-permute-start(f32[64,128]{1,0:T(8,128)S(1)} %get-tuple-element.81), channel_id=1, source_target_pairs={{0,16},{4,20},{8,24},{12,28},{16,0},{20,4},{24,8},{28,12},{1,17},{... | collective-permute-start | bytes 98312 | tf_op jit(solution)/shard_map/ppermute | solution.py:28
  72.6 0.5 collective-permute-start.26
  73.1 1.9 %collective-permute-done.24.refs_1_ = f32[64,128]{1,0:T(8,128)S(1)} collective-permute-done((f32[64,128]{1,0:T(8,128)S(1)}, f32[64,128]{1,0:T(8,128)S(1)}, u32[]{:S(2)}, u32[]{:S(2)}) %collective-permute-start.24) | collective-permute-done | bytes 32800 | tf_op jit(solution)/shard_map/ppermute | solution.py:28
  75.0 0.4 collective-permute-done.25.refs_2_
  75.4 1.1 %collective-permute-done.26.refs_3_ = f32[64,128]{1,0:T(8,128)S(1)} collective-permute-done((f32[64,128]{1,0:T(8,128)S(1)}, f32[64,128]{1,0:T(8,128)S(1)}, u32[]{:S(2)}, u32[]{:S(2)}) %collective-permute-start.26) | collective-permute-done | bytes 32800 | tf_op jit(solution)/shard_map/ppermute | solution.py:28
  76.5 0.7 place.1
  (32 shorter events, 0.3 us)
Async XLA Ops:
  0.0 6.5 %collective-permute-start = (bf16[256,256]{1,0:T(8,128)(2,1)}, bf16[256,256]{1,0:T(8,128)(2,1)S(1)}, u32[]{:S(2)}, u32[]{:S(2)}) collective-permute-start(bf16[256,256]{1,0:T(8,128)(2,1)} %refs_4_.3), channel_id=1, source_target_pairs={{0,1},{4,7},{1,2},{5,4},{2,3},{6,5},{3,0},{7,6},{8,9},{12,15},{9,1... | collective-permute-start | bytes 393224 | tf_op jit(solution)/shard_map/ppermute | solution.py:28
  1.6 0.8 %copy-start = (bf16[424,48]{0,1:T(8,128)(2,1)S(1)}, bf16[424,48]{0,1:T(8,128)(2,1)}, u32[]{:S(2)}) copy-start(bf16[424,48]{0,1:T(8,128)(2,1)} %param.4) | copy-start | bytes 122116
  6.5 16.0 %copy-start.1 = (bf16[256,256]{1,0:T(8,128)(2,1)S(1)}, bf16[256,256]{1,0:T(8,128)(2,1)}, u32[]{:S(2)}) copy-start(bf16[256,256]{1,0:T(8,128)(2,1)} %refs_4_.3) | copy-start | bytes 393220
  6.5 12.4 %collective-permute-start.1 = (bf16[12,32,256]{2,1,0:T(8,128)(2,1)S(1)}, bf16[12,32,256]{2,1,0:T(8,128)(2,1)S(1)}, u32[]{:S(2)}, u32[]{:S(2)}) collective-permute-start(bf16[12,32,256]{2,1,0:T(8,128)(2,1)S(1)} %get-tuple-element.49), channel_id=1, source_target_pairs={{0,1},{4,7},{1,2},{5,4},{2,3},{6,5},{3,0},{7,6},{8,9},{12,15},{9,1... | collective-permute-start | bytes 589832 | tf_op jit(solution)/shard_map/ppermute | solution.py:28
  8.1 10.9 %collective-permute-start.2 = (bf16[12,32,256]{2,1,0:T(8,128)(2,1)S(1)}, bf16[12,32,256]{2,1,0:T(8,128)(2,1)S(1)}, u32[]{:S(2)}, u32[]{:S(2)}) collective-permute-start(bf16[12,32,256]{2,1,0:T(8,128)(2,1)S(1)} %get-tuple-element.50), channel_id=1, source_target_pairs={{0,2},{4,6},{1,3},{5,7},{2,0},{6,4},{3,1},{7,5},{8,10},{12,14},{9,... | collective-permute-start | bytes 589832 | tf_op jit(solution)/shard_map/ppermute | solution.py:28
  9.7 11.2 %collective-permute-start.3 = (bf16[12,32,256]{2,1,0:T(8,128)(2,1)S(1)}, bf16[12,32,256]{2,1,0:T(8,128)(2,1)S(1)}, u32[]{:S(2)}, u32[]{:S(2)}) collective-permute-start(bf16[12,32,256]{2,1,0:T(8,128)(2,1)S(1)} %get-tuple-element.51), channel_id=1, source_target_pairs={{0,3},{4,5},{1,0},{5,6},{2,1},{6,7},{3,2},{7,4},{8,11},{12,13},{9,... | collective-permute-start | bytes 589832 | tf_op jit(solution)/shard_map/ppermute | solution.py:28
  12.0 10.6 %collective-permute-start.4 = (bf16[256,256]{1,0:T(8,128)(2,1)S(1)}, bf16[256,256]{1,0:T(8,128)(2,1)S(1)}, u32[]{:S(2)}, u32[]{:S(2)}) collective-permute-start(bf16[256,256]{1,0:T(8,128)(2,1)S(1)} %collective-permute-done.refs_5_), channel_id=1, source_target_pairs={{0,1},{4,7},{1,2},{5,4},{2,3},{6,5},{3,0},{7,6},{8,9},{12,15},{9,1... | collective-permute-start | bytes 393224 | tf_op jit(solution)/shard_map/ppermute | solution.py:28
  12.0 10.6 %collective-permute-start.5 = (bf16[256,256]{1,0:T(8,128)(2,1)S(1)}, bf16[256,256]{1,0:T(8,128)(2,1)S(1)}, u32[]{:S(2)}, u32[]{:S(2)}) collective-permute-start(bf16[256,256]{1,0:T(8,128)(2,1)S(1)} %collective-permute-done.refs_5_), channel_id=1, source_target_pairs={{0,4},{4,0},{1,5},{5,1},{2,6},{6,2},{3,7},{7,3},{8,12},{12,8},{9,1... | collective-permute-start | bytes 393224 | tf_op jit(solution)/shard_map/ppermute | solution.py:32
  18.9 12.8 %collective-permute-start.6 = (bf16[12,32,256]{2,1,0:T(8,128)(2,1)S(1)}, bf16[12,32,256]{2,1,0:T(8,128)(2,1)S(1)}, u32[]{:S(2)}, u32[]{:S(2)}) collective-permute-start(bf16[12,32,256]{2,1,0:T(8,128)(2,1)S(1)} %get-tuple-element.59), channel_id=1, source_target_pairs={{0,1},{4,7},{1,2},{5,4},{2,3},{6,5},{3,0},{7,6},{8,9},{12,15},{9,1... | collective-permute-start | bytes 589832 | tf_op jit(solution)/shard_map/ppermute | solution.py:28
  18.9 12.7 %collective-permute-start.7 = (bf16[12,32,256]{2,1,0:T(8,128)(2,1)S(1)}, bf16[12,32,256]{2,1,0:T(8,128)(2,1)S(1)}, u32[]{:S(2)}, u32[]{:S(2)}) collective-permute-start(bf16[12,32,256]{2,1,0:T(8,128)(2,1)S(1)} %get-tuple-element.60), channel_id=1, source_target_pairs={{0,2},{4,6},{1,3},{5,7},{2,0},{6,4},{3,1},{7,5},{8,10},{12,14},{9,... | collective-permute-start | bytes 589832 | tf_op jit(solution)/shard_map/ppermute | solution.py:28
  20.9 10.7 %collective-permute-start.8 = (bf16[12,32,256]{2,1,0:T(8,128)(2,1)S(1)}, bf16[12,32,256]{2,1,0:T(8,128)(2,1)S(1)}, u32[]{:S(2)}, u32[]{:S(2)}) collective-permute-start(bf16[12,32,256]{2,1,0:T(8,128)(2,1)S(1)} %get-tuple-element.61), channel_id=1, source_target_pairs={{0,3},{4,5},{1,0},{5,6},{2,1},{6,7},{3,2},{7,4},{8,11},{12,13},{9,... | collective-permute-start | bytes 589832 | tf_op jit(solution)/shard_map/ppermute | solution.py:28
  22.9 8.8 %collective-permute-start.9 = (bf16[32,3072]{1,0:T(8,128)(2,1)S(1)}, bf16[32,3072]{1,0:T(8,128)(2,1)S(1)}, u32[]{:S(2)}, u32[]{:S(2)}) collective-permute-start(bf16[32,3072]{1,0:T(8,128)(2,1)S(1)} %column.2), channel_id=1, source_target_pairs={{0,96},{4,36},{32,0},{36,68},{64,32},{68,100},{96,64},{100,4},{1,9... | collective-permute-start | bytes 589832 | tf_op jit(solution)/shard_map/ppermute | solution.py:28
  26.0 7.2 %collective-permute-start.10 = (bf16[32,3072]{1,0:T(8,128)(2,1)S(1)}, bf16[32,3072]{1,0:T(8,128)(2,1)S(1)}, u32[]{:S(2)}, u32[]{:S(2)}) collective-permute-start(bf16[32,3072]{1,0:T(8,128)(2,1)S(1)} %column.2), channel_id=1, source_target_pairs={{0,24},{4,12},{8,0},{12,20},{16,8},{20,28},{24,16},{28,4},{1,25},{... | collective-permute-start | bytes 589832 | tf_op jit(solution)/shard_map/ppermute | solution.py:28
  33.6 9.8 %collective-permute-start.11 = (bf16[32,3072]{1,0:T(8,128)(2,1)S(1)}, bf16[32,3072]{1,0:T(8,128)(2,1)S(1)}, u32[]{:S(2)}, u32[]{:S(2)}) collective-permute-start(bf16[32,3072]{1,0:T(8,128)(2,1)S(1)} %column.3), channel_id=1, source_target_pairs={{0,24},{4,12},{8,0},{12,20},{16,8},{20,28},{24,16},{28,4},{1,25},{... | collective-permute-start | bytes 589832 | tf_op jit(solution)/shard_map/ppermute | solution.py:28
  37.4 5.7 %collective-permute-start.12 = (bf16[32,3072]{1,0:T(8,128)(2,1)S(1)}, bf16[32,3072]{1,0:T(8,128)(2,1)S(1)}, u32[]{:S(2)}, u32[]{:S(2)}) collective-permute-start(bf16[32,3072]{1,0:T(8,128)(2,1)S(1)} %column.3), channel_id=1, source_target_pairs={{0,96},{4,36},{32,0},{36,68},{64,32},{68,100},{96,64},{100,4},{1,9... | collective-permute-start | bytes 589832 | tf_op jit(solution)/shard_map/ppermute | solution.py:28
  39.1 6.1 %collective-permute-start.14 = (bf16[32,3072]{1,0:T(8,128)(2,1)S(1)}, bf16[32,3072]{1,0:T(8,128)(2,1)S(1)}, u32[]{:S(2)}, u32[]{:S(2)}) collective-permute-start(bf16[32,3072]{1,0:T(8,128)(2,1)S(1)} %collective-permute-done.9), channel_id=1, source_target_pairs={{0,96},{4,36},{32,0},{36,68},{64,32},{68,100},{96,64},{100,4},{1,9... | collective-permute-start | bytes 589832 | tf_op jit(solution)/shard_map/ppermute | solution.py:28
  39.9 8.0 %collective-permute-start.16 = (bf16[32,3072]{1,0:T(8,128)(2,1)S(1)}, bf16[32,3072]{1,0:T(8,128)(2,1)S(1)}, u32[]{:S(2)}, u32[]{:S(2)}) collective-permute-start(bf16[32,3072]{1,0:T(8,128)(2,1)S(1)} %collective-permute-done.10), channel_id=1, source_target_pairs={{0,24},{4,12},{8,0},{12,20},{16,8},{20,28},{24,16},{28,4},{1,25},{... | collective-permute-start | bytes 589832 | tf_op jit(solution)/shard_map/ppermute | solution.py:28
  43.1 12.1 %collective-permute-start.13 = (bf16[128,3072]{1,0:T(8,128)(2,1)S(1)}, bf16[128,3072]{1,0:T(8,128)(2,1)S(1)}, u32[]{:S(2)}, u32[]{:S(2)}) collective-permute-start(bf16[128,3072]{1,0:T(8,128)(2,1)S(1)} %pad_maximum_fusion), channel_id=1, source_target_pairs={{0,4},{4,0},{1,5},{5,1},{2,6},{6,2},{3,7},{7,3},{8,12},{12,8},{9,1... | collective-permute-start | bytes 2359304 | tf_op jit(solution)/shard_map/ppermute | solution.py:32
  43.2 11.9 %collective-permute-start.18 = (bf16[64,3072]{1,0:T(8,128)(2,1)S(1)}, bf16[64,3072]{1,0:T(8,128)(2,1)S(1)}, u32[]{:S(2)}, u32[]{:S(2)}) collective-permute-start(bf16[64,3072]{1,0:T(8,128)(2,1)S(1)} %pad_maximum_fusion.2), channel_id=1, source_target_pairs={{0,32},{4,100},{32,64},{36,4},{64,96},{68,36},{96,0},{100,68},{1,3... | collective-permute-start | bytes 1179656 | tf_op jit(solution)/shard_map/ppermute | solution.py:28
  43.4 11.8 %collective-permute-start.19 = (bf16[64,3072]{1,0:T(8,128)(2,1)S(1)}, bf16[64,3072]{1,0:T(8,128)(2,1)S(1)}, u32[]{:S(2)}, u32[]{:S(2)}) collective-permute-start(bf16[64,3072]{1,0:T(8,128)(2,1)S(1)} %pad_maximum_fusion.2), channel_id=1, source_target_pairs={{0,8},{4,28},{8,16},{12,4},{16,24},{20,12},{24,0},{28,20},{1,9},{5... | collective-permute-start | bytes 1179656 | tf_op jit(solution)/shard_map/ppermute | solution.py:28
  45.1 7.8 %collective-permute-start.15 = (bf16[32,3072]{1,0:T(8,128)(2,1)S(1)}, bf16[32,3072]{1,0:T(8,128)(2,1)S(1)}, u32[]{:S(2)}, u32[]{:S(2)}) collective-permute-start(bf16[32,3072]{1,0:T(8,128)(2,1)S(1)} %collective-permute-done.12), channel_id=1, source_target_pairs={{0,96},{4,36},{32,0},{36,68},{64,32},{68,100},{96,64},{100,4},{1,9... | collective-permute-start | bytes 589832 | tf_op jit(solution)/shard_map/ppermute | solution.py:28
  47.9 7.3 %collective-permute-start.17 = (bf16[32,3072]{1,0:T(8,128)(2,1)S(1)}, bf16[32,3072]{1,0:T(8,128)(2,1)S(1)}, u32[]{:S(2)}, u32[]{:S(2)}) collective-permute-start(bf16[32,3072]{1,0:T(8,128)(2,1)S(1)} %collective-permute-done.11), channel_id=1, source_target_pairs={{0,24},{4,12},{8,0},{12,20},{16,8},{20,28},{24,16},{28,4},{1,25},{... | collective-permute-start | bytes 589832 | tf_op jit(solution)/shard_map/ppermute | solution.py:28
  55.3 2.4 %collective-permute-start.20 = (bf16[128,3072]{1,0:T(8,128)(2,1)S(1)}, bf16[128,3072]{1,0:T(8,128)(2,1)S(1)}, u32[]{:S(2)}, u32[]{:S(2)}) collective-permute-start(bf16[128,3072]{1,0:T(8,128)(2,1)S(1)} %pad_maximum_fusion.1), channel_id=1, source_target_pairs={{0,4},{4,0},{1,5},{5,1},{2,6},{6,2},{3,7},{7,3},{8,12},{12,8},{9,1... | collective-permute-start | bytes 2359304 | tf_op jit(solution)/shard_map/ppermute | solution.py:32
  59.6 10.1 %collective-permute-start.21 = (f32[256,128]{1,0:T(8,128)S(1)}, f32[256,128]{1,0:T(8,128)S(1)}, u32[]{:S(2)}, u32[]{:S(2)}) collective-permute-start(f32[256,128]{1,0:T(8,128)S(1)} %get-tuple-element.76), channel_id=1, source_target_pairs={{0,1},{4,7},{1,2},{5,4},{2,3},{6,5},{3,0},{7,6},{8,9},{12,15},{9,1... | collective-permute-start | bytes 393224 | tf_op jit(solution)/shard_map/ppermute | solution.py:28
  59.7 10.0 %collective-permute-start.22 = (f32[256,128]{1,0:T(8,128)S(1)}, f32[256,128]{1,0:T(8,128)S(1)}, u32[]{:S(2)}, u32[]{:S(2)}) collective-permute-start(f32[256,128]{1,0:T(8,128)S(1)} %get-tuple-element.77), channel_id=1, source_target_pairs={{0,2},{4,6},{1,3},{5,7},{2,0},{6,4},{3,1},{7,5},{8,10},{12,14},{9,... | collective-permute-start | bytes 393224 | tf_op jit(solution)/shard_map/ppermute | solution.py:28
  61.9 7.8 %collective-permute-start.23 = (f32[256,128]{1,0:T(8,128)S(1)}, f32[256,128]{1,0:T(8,128)S(1)}, u32[]{:S(2)}, u32[]{:S(2)}) collective-permute-start(f32[256,128]{1,0:T(8,128)S(1)} %get-tuple-element.78), channel_id=1, source_target_pairs={{0,3},{4,5},{1,0},{5,6},{2,1},{6,7},{3,2},{7,4},{8,11},{12,13},{9,... | collective-permute-start | bytes 393224 | tf_op jit(solution)/shard_map/ppermute | solution.py:28
  69.8 5.2 %collective-permute-start.24 = (f32[64,128]{1,0:T(8,128)S(1)}, f32[64,128]{1,0:T(8,128)S(1)}, u32[]{:S(2)}, u32[]{:S(2)}) collective-permute-start(f32[64,128]{1,0:T(8,128)S(1)} %get-tuple-element.80), channel_id=1, source_target_pairs={{0,8},{4,28},{8,16},{12,4},{16,24},{20,12},{24,0},{28,20},{1,9},{5... | collective-permute-start | bytes 98312 | tf_op jit(solution)/shard_map/ppermute | solution.py:28
  69.9 5.5 %collective-permute-start.25 = (f32[64,128]{1,0:T(8,128)S(1)}, f32[64,128]{1,0:T(8,128)S(1)}, u32[]{:S(2)}, u32[]{:S(2)}) collective-permute-start(f32[64,128]{1,0:T(8,128)S(1)} %get-tuple-element.81), channel_id=1, source_target_pairs={{0,16},{4,20},{8,24},{12,28},{16,0},{20,4},{24,8},{28,12},{1,17},{... | collective-permute-start | bytes 98312 | tf_op jit(solution)/shard_map/ppermute | solution.py:28
  72.6 3.9 %collective-permute-start.26 = (f32[64,128]{1,0:T(8,128)S(1)}, f32[64,128]{1,0:T(8,128)S(1)}, u32[]{:S(2)}, u32[]{:S(2)}) collective-permute-start(f32[64,128]{1,0:T(8,128)S(1)} %get-tuple-element.82), channel_id=1, source_target_pairs={{0,24},{4,12},{8,0},{12,20},{16,8},{20,28},{24,16},{28,4},{1,25},{... | collective-permute-start | bytes 98312 | tf_op jit(solution)/shard_map/ppermute | solution.py:28

commit v3 on v2

--- a/solution.py
+++ b/solution.py
@@ -28,6 +28,10 @@
     return lax.ppermute(v, names, pairs)
 
 
+def turn(v, by):
+    return lax.ppermute(v, "x", [(i, (i + by) % N) for i in range(N)])
+
+
 def swap(v):
     return lax.ppermute(v, "core", [(0, 1), (1, 0)])
 
@@ -36,10 +40,7 @@
     return pltpu.CompilerParams(vmem_limit_bytes=mib * 1024 * 1024)
 
 
-def band_kernel(first, bt_hbm, pix_ref, *rest):
-    outs, (bt_ref, basis, buf, stage, sem, bt_sem) = rest[:N], rest[N:]
-    bt_copy = pltpu.make_async_copy(bt_hbm, bt_ref, bt_sem)
-    bt_copy.start()
+def project_rows(first, basis, col, pix_ref, outs, buf, banded, stage, sem, prepare):
     h = outs[0].shape[1]
     copies = [
         pltpu.make_async_copy(
@@ -49,26 +50,17 @@
     ]
     for copy in copies:
         copy.start()
-    x, core = lax.axis_index("x"), lax.axis_index("core")
-    basis[...] = jnp.zeros_like(basis)
-    bt_copy.wait()
-    for k in range(N):
-        for c in range(2):
-
-            @pl.when((x == k) & (core == c))
-            def _():
-                for j in range(N):
-                    at = RX * ((k + j * (1 - 2 * c)) % N)
-                    basis[16 * j : 16 * j + RX, :] = bt_ref[at : at + RX, :]
-
+    prepare()
     for q in range(h // OUT_ROWS):
         for i in range(OUT_ROWS):
             row = OUT_ROWS * q + i
             if row % IN_ROWS == 0:
                 copies[row // IN_ROWS].wait()
-            banded = jnp.dot(basis[...], buf[row], preferred_element_type=F32)
-            for t in range(2):
-                stage[t, 64 * i : 64 * (i + 1), :] = banded[:, 128 * t : 128 * (t + 1)]
+            values = jnp.dot(basis[...], buf[row], preferred_element_type=F32)
+            banded[64 * i : 64 * (i + 1), :] = values.astype(BF)
+        terms = jnp.dot(banded[...], col[...], preferred_element_type=F32)
+        for t in range(2):
+            stage[t] = terms[:, 128 * t : 128 * (t + 1)]
         at = slice(OUT_ROWS * q, OUT_ROWS * (q + 1))
         for j in range(N):
             for r in range(RX):
@@ -77,52 +69,105 @@
                     outs[j][r, at, 128 * t : 128 * (t + 1)] = rows.astype(BF)
 
 
-def band(bt, pix, first, h):
-    _, bands, c = pix.shape
-    return pl.pallas_call(
-        functools.partial(band_kernel, first),
-        in_specs=[pl.BlockSpec(memory_space=pl.ANY)] * 2,
-        out_specs=[VMEM] * N,
-        out_shape=[jax.ShapeDtypeStruct((RX, h, c), BF)] * N,
-        scratch_shapes=[
-            pltpu.VMEM((R3, bands), BF),
-            pltpu.VMEM((64, bands), BF),
-            pltpu.VMEM((h, bands, c), BF),
-            pltpu.VMEM((2, 64 * OUT_ROWS, c // 2), F32),
-            pltpu.SemaphoreType.DMA((h // IN_ROWS,)),
-            pltpu.SemaphoreType.DMA,
-        ],
+def first_kernel(bt_hbm, col_hbm, pix_ref, *rest):
+    outs, (basis, col, bt, buf, banded, stage, sem, bt_sem, col_sem) = rest[:N], rest[N:]
+    bt_copy = pltpu.make_async_copy(bt_hbm, bt, bt_sem)
+    col_copy = pltpu.make_async_copy(col_hbm, col, col_sem)
+    bt_copy.start()
+    col_copy.start()
+
+    def prepare():
+        x = lax.axis_index("x")
+        basis[...] = jnp.zeros_like(basis)
+        bt_copy.wait()
+        for k in range(N):
+
+            @pl.when(x == k)
+            def _():
+                for j in range(N):
+                    at = RX * ((k + j) % N)
+                    basis[16 * j : 16 * j + RX, :] = bt[at : at + RX, :]
+
+        col_copy.wait()
+
+    project_rows(0, basis, col, pix_ref, outs, buf, banded, stage, sem, prepare)
+
+
+def second_kernel(first, basis, col, pix_ref, *rest):
+    outs, (buf, banded, stage, sem) = rest[:N], rest[N:]
+    project_rows(first, basis, col, pix_ref, outs, buf, banded, stage, sem, lambda: None)
+
+
+ANY = pl.BlockSpec(memory_space=pl.ANY)
+
+
+def project_specs(h, bands, c):
+    terms = [jax.ShapeDtypeStruct((RX, h, R2), BF)] * N
+    scratch = [
+        pltpu.VMEM((h, bands, c), BF),
+        pltpu.VMEM((64 * OUT_ROWS, c), BF),
+        pltpu.VMEM((2, 64 * OUT_ROWS, R2 // 2), F32),
+        pltpu.SemaphoreType.DMA((h // IN_ROWS,)),
+    ]
+    common = dict(
         compiler_params=params(48),
         cost_estimate=pl.CostEstimate(
             flops=2 * h * c * bands * 256, bytes_accessed=h * c * bands * 2, transcendentals=0
         ),
-        name="band",
-    )(bt, pix)
-
-
-def column_kernel(*refs):
-    blocks, cols, out_ref = refs[:N], refs[N : 2 * N], refs[2 * N]
-    r, h, c = blocks[0].shape
-    total = jnp.zeros((r * h, R2), F32)
-    for b, col in zip(blocks, cols):
-        total += jnp.dot(b[...].reshape(r * h, c), col[...], preferred_element_type=F32)
-    for i in range(r):
-        out_ref[:, R2 * i : R2 * (i + 1)] = total[h * i : h * (i + 1), :].astype(BF)
-
-
-def column(blocks, cols, flops):
-    r, h, c = blocks[0].shape
-    return pl.pallas_call(
-        column_kernel,
-        in_specs=[VMEM] * (2 * N),
+    )
+    return terms, scratch, common
+
+
+def project_first(bt, col, pix, h):
+    _, bands, c = pix.shape
+    terms, scratch, common = project_specs(h, bands, c)
+    kept = [jax.ShapeDtypeStruct((64, bands), BF), jax.ShapeDtypeStruct(col.shape, BF)]
+    out = pl.pallas_call(
+        first_kernel,
+        in_specs=[ANY] * 3,
+        out_specs=[VMEM] * (N + 2),
+        out_shape=terms + kept,
+        scratch_shapes=[pltpu.VMEM(bt.shape, BF)] + scratch + [pltpu.SemaphoreType.DMA] * 2,
+        name="project_first",
+        **common,
+    )(bt, col, pix)
+    return list(out[:N]), out[N], out[N + 1]
+
+
+def project_second(basis, col, pix, first, h):
+    _, bands, c = pix.shape
+    terms, scratch, common = project_specs(h, bands, c)
+    return list(
+        pl.pallas_call(
+            functools.partial(second_kernel, first),
+            in_specs=[VMEM, VMEM, ANY],
+            out_specs=[VMEM] * N,
+            out_shape=terms,
+            scratch_shapes=scratch,
+            name="project_second",
+            **common,
+        )(basis, col, pix)
+    )
+
+
+def collect_kernel(*refs):
+    terms, out_ref = refs[:N], refs[N]
+    for r in range(RX):
+        total = sum(term[r].astype(F32) for term in terms)
+        out_ref[:, R2 * r : R2 * (r + 1)] = total.astype(BF)
+
+
+def collect(terms, flops):
+    r, h, s = terms[0].shape
+    return pl.pallas_call(
+        collect_kernel,
+        in_specs=[VMEM] * N,
         out_specs=VMEM,
-        out_shape=jax.ShapeDtypeStruct((h, r * R2), BF),
+        out_shape=jax.ShapeDtypeStruct((h, r * s), BF),
         compiler_params=params(8),
-        cost_estimate=pl.CostEstimate(
-            flops=flops, bytes_accessed=2 * 5 * r * h * c, transcendentals=0
-        ),
-        name="column",
-    )(*blocks, *cols)
+        cost_estimate=pl.CostEstimate(flops=flops, bytes_accessed=2 * 5 * r * h * s, transcendentals=0),
+        name="collect",
+    )(*terms)
 
 
 def gram_kernel(zs, ys, early, late, *refs):
@@ -136,13 +181,15 @@
             e -= base
             at = pl.multiple_of((owner * 2 + half) * n, n)
             rhs[pl.ds(at, n), :] = block[n * e : n * (e + 1), :]
-    for d in range(N):
-        outs[d][...] = lax.dot_general(
+    for d in range(0, N, 2):
+        pair = lax.dot_general(
             zs[...],
-            rhs[2 * n * d : 2 * n * (d + 1), :],
+            rhs[2 * n * d : 2 * n * (d + 2), :],
             (((1,), (1,)), ((), ())),
             preferred_element_type=F32,
         )
+        outs[d][...] = pair[:, : 2 * n]
+        outs[d + 1][...] = pair[:, 2 * n :]
 
 
 def gram(zs, ys, early, late):
@@ -207,18 +254,15 @@
 def local(pixels, band_basis, column_basis):
     pix, bt = pixels.transpose(0, 2, 1), band_basis.T
     h = pix.shape[0] // 2
-    near = shift(column_basis, "x", 1)
-    first = band(bt, pix, 0, h)
-    first, near = lax.optimization_barrier((first, near))
-    cols = [column_basis, near, shift(near, "x", 1), swap(near)]
-    first = spread(first, "x")
-    second = list(band(bt, pix, h, h))
+    first, basis, col = project_first(bt, column_basis, pix, h)
+    first = [first[0]] + [turn(first[j], j) for j in (1, 3, 2)]
+    second = project_second(basis, col, pix, h, h)
     first, second[0] = lax.optimization_barrier((first, second[0]))
-    second = spread(second, "x")
-    mine = [column(first, cols, EARLY)]
+    second = [second[0]] + [turn(second[j], j) for j in (1, 3, 2)]
+    mine = [collect(first, EARLY)]
     up = [[shift(mine[0], axis, -1)] for axis in "yz"]
     second, up = lax.optimization_barrier((second, up))
-    mine.append(column(second, cols, LATE))
+    mine.append(collect(second, LATE))
     far = [[shift(up[i][0], axis, -1)] for i, axis in enumerate("yz")]
     whole = jnp.concatenate(mine, axis=0)
     for i, axis in enumerate("yz"):

time: 77.6 us -> 74.4 us (0.959)
  waiting for transfers between devices: 26.8 us -> 23.6 us
  starting transfers between devices: 37.2 us -> 35.8 us
  local copies, waits for them, and re-layouts: 1.11 us -> 2.01 us
    ppermute x24 -> x16, starting transfers between devices: 37 us -> 26.7 us  [shift(): return lax.ppermute(v, names, pairs)]
    ppermute x0 -> x6, starting transfers between devices: none -> 8.93 us  [turn(): return lax.ppermute(v, 'x', [(i, (i + by) % N) for i in range(N)])]
    ppermute x24 -> x16, waiting for transfers between devices: 24.6 us -> 20.6 us  [shift(): return lax.ppermute(v, names, pairs)]
    pallas_call x4, Pallas kernels: 9.01 us -> 10.2 us  [the longest x1 5.1 us: project_first(): pl.pallas_call(first_kernel, in_specs=[ANY] * 3, out_specs=[VMEM] * (N +...]
    unnamed x15, local copies, waits for them, and re-layouts: 1.05 us -> 1.95 us
    ppermute x0 -> x6, waiting for transfers between devices: none -> 0.85 us  [turn(): return lax.ppermute(v, 'x', [(i, (i + by) % N) for i in range(N)])]
    ppermute x3 -> x2, waiting for transfers between devices: 2.17 us -> 2.17 us  [swap(): return lax.ppermute(v, 'core', [(0, 1), (1, 0)])]
  transfers between devices with their start and end apart: 27 -> 24, of which waited for: 12 -> 13; matrix products, arithmetic and copies ran while one was open for 0% -> 0% of each run, Pallas kernels for 11% -> 7%
where the time goes in v3:
time: 74.4 us; the launch traced here: 73.9 us
  starting transfers between devices  35.8 us (48%)
  waiting for transfers between devices  23.6 us (32%)
  Pallas kernels  12.1 us (16%)
  local copies, waits for them, and re-layouts  2.01 us (3%)
    ppermute x16, starting transfers between devices, shift(): return lax.ppermute(v, names, pairs)  26.7 us
    ppermute x16, waiting for transfers between devices, shift(): return lax.ppermute(v, names, pairs)  20.6 us
    ppermute x6, starting transfers between devices, turn(): return lax.ppermute(v, 'x', [(i, (i + by) % N) for i in range(N)])  8.93 us
    pallas_call x1, Pallas kernels, project_first(): pl.pallas_call(first_kernel, in_specs=[ANY] * 3, out_specs=[VMEM] * (N +...  5.1 us
    pallas_call x1, Pallas kernels, project_second(): pl.pallas_call(functools.partial(second_kernel, first), in_specs=[VMEM, V...  4.89 us
    ppermute x2, waiting for transfers between devices, swap(): return lax.ppermute(v, 'core', [(0, 1), (1, 0)])  2.17 us
    unnamed x15, local copies, waits for them, and re-layouts  1.95 us
  transfers between devices with their start and end apart: 24, of which 13 were waited for; matrix products, arithmetic and copies ran while one was open for 0% of the time, Pallas kernels for 7%

profile of v3, /device:TPU:0, one launch (start us, length us, event | category | flops | bytes accessed | tf_op | source)
XLA Modules:
  0.0 73.9 jit_solution(7057423636149219060)
XLA Ops:
  0.0 0.9 %copy-done = bf16[256,256]{1,0:T(8,128)(2,1)S(1)} copy-done((bf16[256,256]{1,0:T(8,128)(2,1)S(1)}, bf16[256,256]{1,0:T(8,128)(2,1)}, u32[]{:S(2)}) %copy-start) | copy-done | bytes 131096
  0.9 0.8 %copy-done.1 = bf16[424,48]{0,1:T(8,128)(2,1)S(1)} copy-done((bf16[424,48]{0,1:T(8,128)(2,1)S(1)}, bf16[424,48]{0,1:T(8,128)(2,1)}, u32[]{:S(2)}) %copy-start.1) | copy-done | bytes 40728
  1.7 5.1 %project_first.1 = (bf16[12,32,256]{2,1,0:T(8,128)(2,1)S(1)}, bf16[12,32,256]{2,1,0:T(8,128)(2,1)S(1)}, bf16[12,32,256]{2,1,0:T(8,128)(2,1)S(1)}, bf16[12,32,256...) custom-call(bf16[48,424]{1,0:T(8,128)(2,1)S(1)} %bitcast.2, ...), custom_call_target="tpu_custom_call" | custom-call | flops 1778384896 | bytes 6946816 | tf_op jit(solution)/shard_map/project_first/pallas_call | solution.py:125
  6.8 1.6 %collective-permute-start = (bf16[12,32,256]{2,1,0:T(8,128)(2,1)S(1)}, bf16[12,32,256]{2,1,0:T(8,128)(2,1)S(1)}, u32[]{:S(2)}, u32[]{:S(2)}) collective-permute-start(bf16[12,32,256]{2,1,0:T(8,128)(2,1)S(1)} %get-tuple-element.42), channel_id=1, source_target_pairs={{0,1},{1,2},{2,3},{3,0},{4,5},{5,6},{6,7},{7,4},{8,9},{9,10},{10,1... | collective-permute-start | bytes 589832 | tf_op jit(solution)/shard_map/ppermute | solution.py:32
  8.5 1.7 %collective-permute-start.1 = (bf16[12,32,256]{2,1,0:T(8,128)(2,1)S(1)}, bf16[12,32,256]{2,1,0:T(8,128)(2,1)S(1)}, u32[]{:S(2)}, u32[]{:S(2)}) collective-permute-start(bf16[12,32,256]{2,1,0:T(8,128)(2,1)S(1)} %get-tuple-element.43), channel_id=1, source_target_pairs={{0,3},{1,0},{2,1},{3,2},{4,7},{5,4},{6,5},{7,6},{8,11},{9,8},{10,9... | collective-permute-start | bytes 589832 | tf_op jit(solution)/shard_map/ppermute | solution.py:32
  10.1 1.9 %collective-permute-start.2 = (bf16[12,32,256]{2,1,0:T(8,128)(2,1)S(1)}, bf16[12,32,256]{2,1,0:T(8,128)(2,1)S(1)}, u32[]{:S(2)}, u32[]{:S(2)}) collective-permute-start(bf16[12,32,256]{2,1,0:T(8,128)(2,1)S(1)} %get-tuple-element.44), channel_id=1, source_target_pairs={{0,2},{1,3},{2,0},{3,1},{4,6},{5,7},{6,4},{7,5},{8,10},{9,11},{10,... | collective-permute-start | bytes 589832 | tf_op jit(solution)/shard_map/ppermute | solution.py:32
  12.0 4.9 %project_second.1 = (bf16[12,32,256]{2,1,0:T(8,128)(2,1)S(1)}, bf16[12,32,256]{2,1,0:T(8,128)(2,1)S(1)}, bf16[12,32,256]{2,1,0:T(8,128)(2,1)S(1)}, bf16[12,32,256]{2,1,0:T(8,128)(2,1)S(1)}) custom-call(bf16[64,424]{1,0:T(8,128)(2,1)S(1)} %get-tuple-element.45.basis, bf16[256,256]{1,0:T(8,128)(2,1)S(1)} %get-tuple-element.46.col, bf16[64,424,256]{2,1,0:T(8,128)(2,1)} %bitcast.4), custom_call_target="tpu_custom_call" | custom-call | flops 1778384896 | bytes 6946816 | tf_op jit(solution)/shard_map/project_second/pallas_call | solution.py:141
  16.9 0.7 collective-permute-start.3
  17.6 2.6 %collective-permute-start.4 = (bf16[12,32,256]{2,1,0:T(8,128)(2,1)S(1)}, bf16[12,32,256]{2,1,0:T(8,128)(2,1)S(1)}, u32[]{:S(2)}, u32[]{:S(2)}) collective-permute-start(bf16[12,32,256]{2,1,0:T(8,128)(2,1)S(1)} %get-tuple-element.54), channel_id=1, source_target_pairs={{0,3},{1,0},{2,1},{3,2},{4,7},{5,4},{6,5},{7,6},{8,11},{9,8},{10,9... | collective-permute-start | bytes 589832 | tf_op jit(solution)/shard_map/ppermute | solution.py:32
  20.2 0.4 collective-permute-start.5
  20.6 0.2 collective-permute-done.2.refs_3_
  20.8 0.1 collect.2
  20.9 3.1 %collective-permute-start.6 = (bf16[32,3072]{1,0:T(8,128)(2,1)S(1)}, bf16[32,3072]{1,0:T(8,128)(2,1)S(1)}, u32[]{:S(2)}, u32[]{:S(2)}) collective-permute-start(bf16[32,3072]{1,0:T(8,128)(2,1)S(1)} %collect.2), channel_id=1, source_target_pairs={{0,96},{4,36},{32,0},{36,68},{64,32},{68,100},{96,64},{100,4},{1,9... | collective-permute-start | bytes 589832 | tf_op jit(solution)/shard_map/ppermute | solution.py:28
  24.0 4.0 %collective-permute-start.7 = (bf16[32,3072]{1,0:T(8,128)(2,1)S(1)}, bf16[32,3072]{1,0:T(8,128)(2,1)S(1)}, u32[]{:S(2)}, u32[]{:S(2)}) collective-permute-start(bf16[32,3072]{1,0:T(8,128)(2,1)S(1)} %collect.2), channel_id=1, source_target_pairs={{0,24},{4,12},{8,0},{12,20},{16,8},{20,28},{24,16},{28,4},{1,25},{... | collective-permute-start | bytes 589832 | tf_op jit(solution)/shard_map/ppermute | solution.py:28
  28.1 0.7 collective-permute-done.3.refs_1_
  28.7 2.5 %collective-permute-done.7 = bf16[32,3072]{1,0:T(8,128)(2,1)S(1)} collective-permute-done((bf16[32,3072]{1,0:T(8,128)(2,1)S(1)}, bf16[32,3072]{1,0:T(8,128)(2,1)S(1)}, u32[]{:S(2)}, u32[]{:S(2)}) %collective-permute-start.7) | collective-permute-done | bytes 196640 | tf_op jit(solution)/shard_map/ppermute | solution.py:28
  31.2 0.1 collect.3
  31.3 3.8 %collective-permute-start.8 = (bf16[32,3072]{1,0:T(8,128)(2,1)S(1)}, bf16[32,3072]{1,0:T(8,128)(2,1)S(1)}, u32[]{:S(2)}, u32[]{:S(2)}) collective-permute-start(bf16[32,3072]{1,0:T(8,128)(2,1)S(1)} %collect.3), channel_id=1, source_target_pairs={{0,24},{4,12},{8,0},{12,20},{16,8},{20,28},{24,16},{28,4},{1,25},{... | collective-permute-start | bytes 589832 | tf_op jit(solution)/shard_map/ppermute | solution.py:28
  35.1 0.9 %collective-permute-start.9 = (bf16[32,3072]{1,0:T(8,128)(2,1)S(1)}, bf16[32,3072]{1,0:T(8,128)(2,1)S(1)}, u32[]{:S(2)}, u32[]{:S(2)}) collective-permute-start(bf16[32,3072]{1,0:T(8,128)(2,1)S(1)} %collect.3), channel_id=1, source_target_pairs={{0,96},{4,36},{32,0},{36,68},{64,32},{68,100},{96,64},{100,4},{1,9... | collective-permute-start | bytes 589832 | tf_op jit(solution)/shard_map/ppermute | solution.py:28
  36.0 0.1 copy.9
  36.1 0.8 %collective-permute-start.11 = (bf16[32,3072]{1,0:T(8,128)(2,1)S(1)}, bf16[32,3072]{1,0:T(8,128)(2,1)S(1)}, u32[]{:S(2)}, u32[]{:S(2)}) collective-permute-start(bf16[32,3072]{1,0:T(8,128)(2,1)S(1)} %collective-permute-done.6), channel_id=1, source_target_pairs={{0,96},{4,36},{32,0},{36,68},{64,32},{68,100},{96,64},{100,4},{1,9... | collective-permute-start | bytes 589832 | tf_op jit(solution)/shard_map/ppermute | solution.py:28
  37.0 0.4 collective-permute-start.13
  37.4 3.4 %collective-permute-done.9 = bf16[32,3072]{1,0:T(8,128)(2,1)S(1)} collective-permute-done((bf16[32,3072]{1,0:T(8,128)(2,1)S(1)}, bf16[32,3072]{1,0:T(8,128)(2,1)S(1)}, u32[]{:S(2)}, u32[]{:S(2)}) %collective-permute-start.9) | collective-permute-done | bytes 196640 | tf_op jit(solution)/shard_map/ppermute | solution.py:28
  40.8 0.1 collective-permute-start.10
  40.9 0.1 collective-permute-start.15
  41.0 0.1 collective-permute-start.16
  41.1 1.7 %collective-permute-done.11 = bf16[32,3072]{1,0:T(8,128)(2,1)S(1)} collective-permute-done((bf16[32,3072]{1,0:T(8,128)(2,1)S(1)}, bf16[32,3072]{1,0:T(8,128)(2,1)S(1)}, u32[]{:S(2)}, u32[]{:S(2)}) %collective-permute-start.11) | collective-permute-done | bytes 196640 | tf_op jit(solution)/shard_map/ppermute | solution.py:28
  42.9 2.1 %collective-permute-start.12 = (bf16[32,3072]{1,0:T(8,128)(2,1)S(1)}, bf16[32,3072]{1,0:T(8,128)(2,1)S(1)}, u32[]{:S(2)}, u32[]{:S(2)}) collective-permute-start(bf16[32,3072]{1,0:T(8,128)(2,1)S(1)} %collective-permute-done.9), channel_id=1, source_target_pairs={{0,96},{4,36},{32,0},{36,68},{64,32},{68,100},{96,64},{100,4},{1,9... | collective-permute-start | bytes 589832 | tf_op jit(solution)/shard_map/ppermute | solution.py:28
  45.0 2.6 %collective-permute-start.14 = (bf16[32,3072]{1,0:T(8,128)(2,1)S(1)}, bf16[32,3072]{1,0:T(8,128)(2,1)S(1)}, u32[]{:S(2)}, u32[]{:S(2)}) collective-permute-start(bf16[32,3072]{1,0:T(8,128)(2,1)S(1)} %collective-permute-done.8), channel_id=1, source_target_pairs={{0,24},{4,12},{8,0},{12,20},{16,8},{20,28},{24,16},{28,4},{1,25},{... | collective-permute-start | bytes 589832 | tf_op jit(solution)/shard_map/ppermute | solution.py:28
  47.6 2.8 %collective-permute-done.12 = bf16[32,3072]{1,0:T(8,128)(2,1)S(1)} collective-permute-done((bf16[32,3072]{1,0:T(8,128)(2,1)S(1)}, bf16[32,3072]{1,0:T(8,128)(2,1)S(1)}, u32[]{:S(2)}, u32[]{:S(2)}) %collective-permute-start.12) | collective-permute-done | bytes 196640 | tf_op jit(solution)/shard_map/ppermute | solution.py:28
  50.4 1.8 %collective-permute-done.14 = bf16[32,3072]{1,0:T(8,128)(2,1)S(1)} collective-permute-done((bf16[32,3072]{1,0:T(8,128)(2,1)S(1)}, bf16[32,3072]{1,0:T(8,128)(2,1)S(1)}, u32[]{:S(2)}, u32[]{:S(2)}) %collective-permute-start.14) | collective-permute-done | bytes 196640 | tf_op jit(solution)/shard_map/ppermute | solution.py:28
  52.3 0.1 pad_maximum_fusion.1
  52.4 0.1 collective-permute-start.17
  52.5 0.1 constant_dynamic-update-slice_fusion
  52.6 2.2 %collective-permute-done.17.late = bf16[128,3072]{1,0:T(8,128)(2,1)S(1)} collective-permute-done((bf16[128,3072]{1,0:T(8,128)(2,1)S(1)}, bf16[128,3072]{1,0:T(8,128)(2,1)S(1)}, u32[]{:S(2)}, u32[]{:S(2)}) %collective-permute-start.17) | collective-permute-done | bytes 786464 | tf_op jit(solution)/shard_map/ppermute | solution.py:36
  54.7 1.2 %gram.1 = (f32[256,128]{1,0:T(8,128)S(1)}, f32[256,128]{1,0:T(8,128)S(1)}, f32[256,128]{1,0:T(8,128)S(1)}, f32[256,128]{1,0:T(8,128)S(1)}) custom-call(bf16[256,3072]{1,0:T(8,128)(2,1)S(1)} %get-tuple-element.77.zs, bf16[256,3072]{1,0:T(8,128)(2,1)S(1)} %get-tuple-element.78.ys, bf16[128,3072]{1,0:T(8,128)(2,1)S(1)} %collective-permute-done.10.early, ...), custom_call_target="tpu_custom_call" | custom-call | flops 805306368 | bytes 4718592 | tf_op jit(solution)/shard_map/gram/pallas_call | solution.py:197
  56.0 0.9 %collective-permute-start.18 = (f32[256,128]{1,0:T(8,128)S(1)}, f32[256,128]{1,0:T(8,128)S(1)}, u32[]{:S(2)}, u32[]{:S(2)}) collective-permute-start(f32[256,128]{1,0:T(8,128)S(1)} %get-tuple-element.70), channel_id=1, source_target_pairs={{0,1},{4,7},{1,2},{5,4},{2,3},{6,5},{3,0},{7,6},{8,9},{12,15},{9,1... | collective-permute-start | bytes 393224 | tf_op jit(solution)/shard_map/ppermute | solution.py:28
  56.9 3.0 %collective-permute-start.19 = (f32[256,128]{1,0:T(8,128)S(1)}, f32[256,128]{1,0:T(8,128)S(1)}, u32[]{:S(2)}, u32[]{:S(2)}) collective-permute-start(f32[256,128]{1,0:T(8,128)S(1)} %get-tuple-element.71), channel_id=1, source_target_pairs={{0,2},{4,6},{1,3},{5,7},{2,0},{6,4},{3,1},{7,5},{8,10},{12,14},{9,... | collective-permute-start | bytes 393224 | tf_op jit(solution)/shard_map/ppermute | solution.py:28
  59.9 1.6 %collective-permute-start.20 = (f32[256,128]{1,0:T(8,128)S(1)}, f32[256,128]{1,0:T(8,128)S(1)}, u32[]{:S(2)}, u32[]{:S(2)}) collective-permute-start(f32[256,128]{1,0:T(8,128)S(1)} %get-tuple-element.72), channel_id=1, source_target_pairs={{0,3},{4,5},{1,0},{5,6},{2,1},{6,7},{3,2},{7,4},{8,11},{12,13},{9,... | collective-permute-start | bytes 393224 | tf_op jit(solution)/shard_map/ppermute | solution.py:28
  61.6 0.7 collective-permute-done.18.g1
  62.2 4.0 %collective-permute-done.19.g2 = f32[256,128]{1,0:T(8,128)S(1)} collective-permute-done((f32[256,128]{1,0:T(8,128)S(1)}, f32[256,128]{1,0:T(8,128)S(1)}, u32[]{:S(2)}, u32[]{:S(2)}) %collective-permute-start.19) | collective-permute-done | bytes 131104 | tf_op jit(solution)/shard_map/ppermute | solution.py:28
  66.2 0.1 collective-permute-start.21
  66.3 3.0 %collective-permute-start.22 = (f32[64,128]{1,0:T(8,128)S(1)}, f32[64,128]{1,0:T(8,128)S(1)}, u32[]{:S(2)}, u32[]{:S(2)}) collective-permute-start(f32[64,128]{1,0:T(8,128)S(1)} %get-tuple-element.75), channel_id=1, source_target_pairs={{0,16},{4,20},{8,24},{12,28},{16,0},{20,4},{24,8},{28,12},{1,17},{... | collective-permute-start | bytes 98312 | tf_op jit(solution)/shard_map/ppermute | solution.py:28
  69.3 0.2 collective-permute-start.23
  69.5 1.9 %collective-permute-done.21.refs_1_ = f32[64,128]{1,0:T(8,128)S(1)} collective-permute-done((f32[64,128]{1,0:T(8,128)S(1)}, f32[64,128]{1,0:T(8,128)S(1)}, u32[]{:S(2)}, u32[]{:S(2)}) %collective-permute-start.21) | collective-permute-done | bytes 32800 | tf_op jit(solution)/shard_map/ppermute | solution.py:28
  71.4 0.4 collective-permute-done.22.refs_2_
  71.8 1.4 %collective-permute-done.23.refs_3_ = f32[64,128]{1,0:T(8,128)S(1)} collective-permute-done((f32[64,128]{1,0:T(8,128)S(1)}, f32[64,128]{1,0:T(8,128)S(1)}, u32[]{:S(2)}, u32[]{:S(2)}) %collective-permute-start.23) | collective-permute-done | bytes 32800 | tf_op jit(solution)/shard_map/ppermute | solution.py:28
  73.2 0.7 place.1
  (26 shorter events, 0.3 us)
Async XLA Ops:
  0.0 0.9 %copy-start = (bf16[256,256]{1,0:T(8,128)(2,1)S(1)}, bf16[256,256]{1,0:T(8,128)(2,1)}, u32[]{:S(2)}) copy-start(bf16[256,256]{1,0:T(8,128)(2,1)} %col_hbm.1) | copy-start | bytes 393220
  0.9 0.8 %copy-start.1 = (bf16[424,48]{0,1:T(8,128)(2,1)S(1)}, bf16[424,48]{0,1:T(8,128)(2,1)}, u32[]{:S(2)}) copy-start(bf16[424,48]{0,1:T(8,128)(2,1)} %param.4) | copy-start | bytes 122116
  6.8 13.4 %collective-permute-start = (bf16[12,32,256]{2,1,0:T(8,128)(2,1)S(1)}, bf16[12,32,256]{2,1,0:T(8,128)(2,1)S(1)}, u32[]{:S(2)}, u32[]{:S(2)}) collective-permute-start(bf16[12,32,256]{2,1,0:T(8,128)(2,1)S(1)} %get-tuple-element.42), channel_id=1, source_target_pairs={{0,1},{1,2},{2,3},{3,0},{4,5},{5,6},{6,7},{7,4},{8,9},{9,10},{10,1... | collective-permute-start | bytes 589832 | tf_op jit(solution)/shard_map/ppermute | solution.py:32
  8.5 12.2 %collective-permute-start.1 = (bf16[12,32,256]{2,1,0:T(8,128)(2,1)S(1)}, bf16[12,32,256]{2,1,0:T(8,128)(2,1)S(1)}, u32[]{:S(2)}, u32[]{:S(2)}) collective-permute-start(bf16[12,32,256]{2,1,0:T(8,128)(2,1)S(1)} %get-tuple-element.43), channel_id=1, source_target_pairs={{0,3},{1,0},{2,1},{3,2},{4,7},{5,4},{6,5},{7,6},{8,11},{9,8},{10,9... | collective-permute-start | bytes 589832 | tf_op jit(solution)/shard_map/ppermute | solution.py:32
  10.1 10.7 %collective-permute-start.2 = (bf16[12,32,256]{2,1,0:T(8,128)(2,1)S(1)}, bf16[12,32,256]{2,1,0:T(8,128)(2,1)S(1)}, u32[]{:S(2)}, u32[]{:S(2)}) collective-permute-start(bf16[12,32,256]{2,1,0:T(8,128)(2,1)S(1)} %get-tuple-element.44), channel_id=1, source_target_pairs={{0,2},{1,3},{2,0},{3,1},{4,6},{5,7},{6,4},{7,5},{8,10},{9,11},{10,... | collective-permute-start | bytes 589832 | tf_op jit(solution)/shard_map/ppermute | solution.py:32
  16.9 11.8 %collective-permute-start.3 = (bf16[12,32,256]{2,1,0:T(8,128)(2,1)S(1)}, bf16[12,32,256]{2,1,0:T(8,128)(2,1)S(1)}, u32[]{:S(2)}, u32[]{:S(2)}) collective-permute-start(bf16[12,32,256]{2,1,0:T(8,128)(2,1)S(1)} %get-tuple-element.53), channel_id=1, source_target_pairs={{0,1},{1,2},{2,3},{3,0},{4,5},{5,6},{6,7},{7,4},{8,9},{9,10},{10,1... | collective-permute-start | bytes 589832 | tf_op jit(solution)/shard_map/ppermute | solution.py:32
  17.6 11.2 %collective-permute-start.4 = (bf16[12,32,256]{2,1,0:T(8,128)(2,1)S(1)}, bf16[12,32,256]{2,1,0:T(8,128)(2,1)S(1)}, u32[]{:S(2)}, u32[]{:S(2)}) collective-permute-start(bf16[12,32,256]{2,1,0:T(8,128)(2,1)S(1)} %get-tuple-element.54), channel_id=1, source_target_pairs={{0,3},{1,0},{2,1},{3,2},{4,7},{5,4},{6,5},{7,6},{8,11},{9,8},{10,9... | collective-permute-start | bytes 589832 | tf_op jit(solution)/shard_map/ppermute | solution.py:32
  20.2 8.5 %collective-permute-start.5 = (bf16[12,32,256]{2,1,0:T(8,128)(2,1)S(1)}, bf16[12,32,256]{2,1,0:T(8,128)(2,1)S(1)}, u32[]{:S(2)}, u32[]{:S(2)}) collective-permute-start(bf16[12,32,256]{2,1,0:T(8,128)(2,1)S(1)} %get-tuple-element.55), channel_id=1, source_target_pairs={{0,2},{1,3},{2,0},{3,1},{4,6},{5,7},{6,4},{7,5},{8,10},{9,11},{10,... | collective-permute-start | bytes 589832 | tf_op jit(solution)/shard_map/ppermute | solution.py:32
  20.9 7.8 %collective-permute-start.6 = (bf16[32,3072]{1,0:T(8,128)(2,1)S(1)}, bf16[32,3072]{1,0:T(8,128)(2,1)S(1)}, u32[]{:S(2)}, u32[]{:S(2)}) collective-permute-start(bf16[32,3072]{1,0:T(8,128)(2,1)S(1)} %collect.2), channel_id=1, source_target_pairs={{0,96},{4,36},{32,0},{36,68},{64,32},{68,100},{96,64},{100,4},{1,9... | collective-permute-start | bytes 589832 | tf_op jit(solution)/shard_map/ppermute | solution.py:28
  24.0 7.2 %collective-permute-start.7 = (bf16[32,3072]{1,0:T(8,128)(2,1)S(1)}, bf16[32,3072]{1,0:T(8,128)(2,1)S(1)}, u32[]{:S(2)}, u32[]{:S(2)}) collective-permute-start(bf16[32,3072]{1,0:T(8,128)(2,1)S(1)} %collect.2), channel_id=1, source_target_pairs={{0,24},{4,12},{8,0},{12,20},{16,8},{20,28},{24,16},{28,4},{1,25},{... | collective-permute-start | bytes 589832 | tf_op jit(solution)/shard_map/ppermute | solution.py:28
  31.3 9.7 %collective-permute-start.8 = (bf16[32,3072]{1,0:T(8,128)(2,1)S(1)}, bf16[32,3072]{1,0:T(8,128)(2,1)S(1)}, u32[]{:S(2)}, u32[]{:S(2)}) collective-permute-start(bf16[32,3072]{1,0:T(8,128)(2,1)S(1)} %collect.3), channel_id=1, source_target_pairs={{0,24},{4,12},{8,0},{12,20},{16,8},{20,28},{24,16},{28,4},{1,25},{... | collective-permute-start | bytes 589832 | tf_op jit(solution)/shard_map/ppermute | solution.py:28
  35.1 5.7 %collective-permute-start.9 = (bf16[32,3072]{1,0:T(8,128)(2,1)S(1)}, bf16[32,3072]{1,0:T(8,128)(2,1)S(1)}, u32[]{:S(2)}, u32[]{:S(2)}) collective-permute-start(bf16[32,3072]{1,0:T(8,128)(2,1)S(1)} %collect.3), channel_id=1, source_target_pairs={{0,96},{4,36},{32,0},{36,68},{64,32},{68,100},{96,64},{100,4},{1,9... | collective-permute-start | bytes 589832 | tf_op jit(solution)/shard_map/ppermute | solution.py:28
  36.1 6.7 %collective-permute-start.11 = (bf16[32,3072]{1,0:T(8,128)(2,1)S(1)}, bf16[32,3072]{1,0:T(8,128)(2,1)S(1)}, u32[]{:S(2)}, u32[]{:S(2)}) collective-permute-start(bf16[32,3072]{1,0:T(8,128)(2,1)S(1)} %collective-permute-done.6), channel_id=1, source_target_pairs={{0,96},{4,36},{32,0},{36,68},{64,32},{68,100},{96,64},{100,4},{1,9... | collective-permute-start | bytes 589832 | tf_op jit(solution)/shard_map/ppermute | solution.py:28
  37.0 8.0 %collective-permute-start.13 = (bf16[32,3072]{1,0:T(8,128)(2,1)S(1)}, bf16[32,3072]{1,0:T(8,128)(2,1)S(1)}, u32[]{:S(2)}, u32[]{:S(2)}) collective-permute-start(bf16[32,3072]{1,0:T(8,128)(2,1)S(1)} %collective-permute-done.7), channel_id=1, source_target_pairs={{0,24},{4,12},{8,0},{12,20},{16,8},{20,28},{24,16},{28,4},{1,25},{... | collective-permute-start | bytes 589832 | tf_op jit(solution)/shard_map/ppermute | solution.py:28
  40.8 11.4 %collective-permute-start.10 = (bf16[128,3072]{1,0:T(8,128)(2,1)S(1)}, bf16[128,3072]{1,0:T(8,128)(2,1)S(1)}, u32[]{:S(2)}, u32[]{:S(2)}) collective-permute-start(bf16[128,3072]{1,0:T(8,128)(2,1)S(1)} %pad_maximum_fusion), channel_id=1, source_target_pairs={{0,4},{4,0},{1,5},{5,1},{2,6},{6,2},{3,7},{7,3},{8,12},{12,8},{9,1... | collective-permute-start | bytes 2359304 | tf_op jit(solution)/shard_map/ppermute | solution.py:36
  40.9 11.3 %collective-permute-start.15 = (bf16[64,3072]{1,0:T(8,128)(2,1)S(1)}, bf16[64,3072]{1,0:T(8,128)(2,1)S(1)}, u32[]{:S(2)}, u32[]{:S(2)}) collective-permute-start(bf16[64,3072]{1,0:T(8,128)(2,1)S(1)} %pad_maximum_fusion.2), channel_id=1, source_target_pairs={{0,32},{4,100},{32,64},{36,4},{64,96},{68,36},{96,0},{100,68},{1,3... | collective-permute-start | bytes 1179656 | tf_op jit(solution)/shard_map/ppermute | solution.py:28
  41.0 11.2 %collective-permute-start.16 = (bf16[64,3072]{1,0:T(8,128)(2,1)S(1)}, bf16[64,3072]{1,0:T(8,128)(2,1)S(1)}, u32[]{:S(2)}, u32[]{:S(2)}) collective-permute-start(bf16[64,3072]{1,0:T(8,128)(2,1)S(1)} %pad_maximum_fusion.2), channel_id=1, source_target_pairs={{0,8},{4,28},{8,16},{12,4},{16,24},{20,12},{24,0},{28,20},{1,9},{5... | collective-permute-start | bytes 1179656 | tf_op jit(solution)/shard_map/ppermute | solution.py:28
  42.9 7.5 %collective-permute-start.12 = (bf16[32,3072]{1,0:T(8,128)(2,1)S(1)}, bf16[32,3072]{1,0:T(8,128)(2,1)S(1)}, u32[]{:S(2)}, u32[]{:S(2)}) collective-permute-start(bf16[32,3072]{1,0:T(8,128)(2,1)S(1)} %collective-permute-done.9), channel_id=1, source_target_pairs={{0,96},{4,36},{32,0},{36,68},{64,32},{68,100},{96,64},{100,4},{1,9... | collective-permute-start | bytes 589832 | tf_op jit(solution)/shard_map/ppermute | solution.py:28
  45.0 7.3 %collective-permute-start.14 = (bf16[32,3072]{1,0:T(8,128)(2,1)S(1)}, bf16[32,3072]{1,0:T(8,128)(2,1)S(1)}, u32[]{:S(2)}, u32[]{:S(2)}) collective-permute-start(bf16[32,3072]{1,0:T(8,128)(2,1)S(1)} %collective-permute-done.8), channel_id=1, source_target_pairs={{0,24},{4,12},{8,0},{12,20},{16,8},{20,28},{24,16},{28,4},{1,25},{... | collective-permute-start | bytes 589832 | tf_op jit(solution)/shard_map/ppermute | solution.py:28
  52.4 2.4 %collective-permute-start.17 = (bf16[128,3072]{1,0:T(8,128)(2,1)S(1)}, bf16[128,3072]{1,0:T(8,128)(2,1)S(1)}, u32[]{:S(2)}, u32[]{:S(2)}) collective-permute-start(bf16[128,3072]{1,0:T(8,128)(2,1)S(1)} %pad_maximum_fusion.1), channel_id=1, source_target_pairs={{0,4},{4,0},{1,5},{5,1},{2,6},{6,2},{3,7},{7,3},{8,12},{12,8},{9,1... | collective-permute-start | bytes 2359304 | tf_op jit(solution)/shard_map/ppermute | solution.py:36
  56.0 6.2 %collective-permute-start.18 = (f32[256,128]{1,0:T(8,128)S(1)}, f32[256,128]{1,0:T(8,128)S(1)}, u32[]{:S(2)}, u32[]{:S(2)}) collective-permute-start(f32[256,128]{1,0:T(8,128)S(1)} %get-tuple-element.70), channel_id=1, source_target_pairs={{0,1},{4,7},{1,2},{5,4},{2,3},{6,5},{3,0},{7,6},{8,9},{12,15},{9,1... | collective-permute-start | bytes 393224 | tf_op jit(solution)/shard_map/ppermute | solution.py:28
  56.9 9.3 %collective-permute-start.19 = (f32[256,128]{1,0:T(8,128)S(1)}, f32[256,128]{1,0:T(8,128)S(1)}, u32[]{:S(2)}, u32[]{:S(2)}) collective-permute-start(f32[256,128]{1,0:T(8,128)S(1)} %get-tuple-element.71), channel_id=1, source_target_pairs={{0,2},{4,6},{1,3},{5,7},{2,0},{6,4},{3,1},{7,5},{8,10},{12,14},{9,... | collective-permute-start | bytes 393224 | tf_op jit(solution)/shard_map/ppermute | solution.py:28
  59.9 6.3 %collective-permute-start.20 = (f32[256,128]{1,0:T(8,128)S(1)}, f32[256,128]{1,0:T(8,128)S(1)}, u32[]{:S(2)}, u32[]{:S(2)}) collective-permute-start(f32[256,128]{1,0:T(8,128)S(1)} %get-tuple-element.72), channel_id=1, source_target_pairs={{0,3},{4,5},{1,0},{5,6},{2,1},{6,7},{3,2},{7,4},{8,11},{12,13},{9,... | collective-permute-start | bytes 393224 | tf_op jit(solution)/shard_map/ppermute | solution.py:28
  66.2 5.2 %collective-permute-start.21 = (f32[64,128]{1,0:T(8,128)S(1)}, f32[64,128]{1,0:T(8,128)S(1)}, u32[]{:S(2)}, u32[]{:S(2)}) collective-permute-start(f32[64,128]{1,0:T(8,128)S(1)} %get-tuple-element.74), channel_id=1, source_target_pairs={{0,8},{4,28},{8,16},{12,4},{16,24},{20,12},{24,0},{28,20},{1,9},{5... | collective-permute-start | bytes 98312 | tf_op jit(solution)/shard_map/ppermute | solution.py:28
  66.3 5.5 %collective-permute-start.22 = (f32[64,128]{1,0:T(8,128)S(1)}, f32[64,128]{1,0:T(8,128)S(1)}, u32[]{:S(2)}, u32[]{:S(2)}) collective-permute-start(f32[64,128]{1,0:T(8,128)S(1)} %get-tuple-element.75), channel_id=1, source_target_pairs={{0,16},{4,20},{8,24},{12,28},{16,0},{20,4},{24,8},{28,12},{1,17},{... | collective-permute-start | bytes 98312 | tf_op jit(solution)/shard_map/ppermute | solution.py:28
  69.3 3.9 %collective-permute-start.23 = (f32[64,128]{1,0:T(8,128)S(1)}, f32[64,128]{1,0:T(8,128)S(1)}, u32[]{:S(2)}, u32[]{:S(2)}) collective-permute-start(f32[64,128]{1,0:T(8,128)S(1)} %get-tuple-element.76), channel_id=1, source_target_pairs={{0,24},{4,12},{8,0},{12,20},{16,8},{20,28},{24,16},{28,4},{1,25},{... | collective-permute-start | bytes 98312 | tf_op jit(solution)/shard_map/ppermute | solution.py:28

commit v4 on v3

--- a/solution.py
+++ b/solution.py
@@ -18,6 +18,7 @@
 LATE = 100_000_000
 BF = jnp.bfloat16
 F32 = jnp.float32
+ORDER = (0, 2, 1, 3)
 VMEM = pl.BlockSpec(memory_space=pltpu.VMEM)
 
 
@@ -66,7 +67,7 @@
             for r in range(RX):
                 for t in range(2):
                     rows = stage[t, pl.ds(16 * j + r, OUT_ROWS, stride=64), :]
-                    outs[j][r, at, 128 * t : 128 * (t + 1)] = rows.astype(BF)
+                    outs[j][r, at, 128 * t : 128 * (t + 1)] = rows.astype(outs[j].dtype)
 
 
 def first_kernel(bt_hbm, col_hbm, pix_ref, *rest):
@@ -102,7 +103,7 @@
 
 
 def project_specs(h, bands, c):
-    terms = [jax.ShapeDtypeStruct((RX, h, R2), BF)] * N
+    terms = [jax.ShapeDtypeStruct((RX, h, R2), BF if j else F32) for j in range(N)]
     scratch = [
         pltpu.VMEM((h, bands, c), BF),
         pltpu.VMEM((64 * OUT_ROWS, c), BF),
@@ -231,7 +232,7 @@
     parts, out_ref = refs[:N], refs[N]
     z, core = lax.axis_index("z"), lax.axis_index("core")
     m = parts[0].shape[1]
-    for d, part in enumerate(parts):
+    for d, part in zip(ORDER, parts):
         at = pl.multiple_of(lax.rem(z - (1 - 2 * core) * d + N, N) * m, m)
         out_ref[:, pl.ds(at, m)] = part[...]
 
@@ -263,20 +264,20 @@
     up = [[shift(mine[0], axis, -1)] for axis in "yz"]
     second, up = lax.optimization_barrier((second, up))
     mine.append(collect(second, LATE))
-    far = [[shift(up[i][0], axis, -1)] for i, axis in enumerate("yz")]
-    whole = jnp.concatenate(mine, axis=0)
     for i, axis in enumerate("yz"):
         up[i].append(shift(mine[1], axis, -1))
-    for i, axis in enumerate("yz"):
-        far[i].append(shift(up[i][1], axis, -1))
-    down = [shift(whole, axis, 1) for axis in "yz"]
+    later = mine
+    far = [shift(jnp.concatenate(up[i], axis=0), axis, -1) for i, axis in enumerate("yz")]
+    down = [shift(jnp.concatenate(later, axis=0), axis, 1) for axis in "yz"]
     early = swap(jnp.concatenate(mine + up[0], axis=0))
     early, far, down = lax.optimization_barrier((early, far, down))
-    late = jnp.concatenate(far[0] + [down[0]], axis=0)
+    late = jnp.concatenate([far[0], down[0]], axis=0)
     ys = jnp.concatenate(mine + up[0] + [late], axis=0)
-    zs = jnp.concatenate(mine + up[1] + far[1] + [down[1]], axis=0)
-    parts = sum_x(spread(gram(zs, ys, early, swap(late)), "x"))
-    return place(spread(parts, "z"))
+    zs = jnp.concatenate(mine + up[1] + [far[1], down[1]], axis=0)
+    parts = spread(gram(zs, ys, early, swap(late)), "x")
+    parts = sum_x([parts[d] for d in ORDER])
+    parts = spread(parts, "z")
+    return place([parts[d] for d in ORDER])
 
 
 def solution(mesh):

time: 74.4 us -> 74.2 us (level)
  waiting for transfers between devices: 23.6 us -> 21.1 us
  starting transfers between devices: 35.8 us -> 37.9 us
    ppermute x16 -> x14, waiting for transfers between devices: 20.6 us -> 18.1 us  [shift(): return lax.ppermute(v, names, pairs)]
    ppermute x16 -> x14, starting transfers between devices: 26.7 us -> 28.6 us  [shift(): return lax.ppermute(v, names, pairs)]
    unnamed x15 -> x13, local copies, waits for them, and re-layouts: 1.95 us -> 1.95 us
  transfers between devices with their start and end apart: 24 -> 22, of which waited for: 13 -> 13; matrix products, arithmetic and copies ran while one was open for 0% -> 1% of each run, Pallas kernels for 7% -> 7%
where the time goes in v4:
time: 74.2 us; the launch traced here: 73.5 us
  starting transfers between devices  37.9 us (51%)
  waiting for transfers between devices  21.1 us (28%)
  Pallas kernels  12.1 us (16%)
  local copies, waits for them, and re-layouts  2 us (3%)
    ppermute x14, starting transfers between devices, shift(): return lax.ppermute(v, names, pairs)  28.6 us
    ppermute x14, waiting for transfers between devices, shift(): return lax.ppermute(v, names, pairs)  18.1 us
    ppermute x6, starting transfers between devices, turn(): return lax.ppermute(v, 'x', [(i, (i + by) % N) for i in range(N)])  8.93 us
    pallas_call x1, Pallas kernels, project_first(): pl.pallas_call(first_kernel, in_specs=[ANY] * 3, out_specs=[VMEM] * (N +...  5.11 us
    pallas_call x1, Pallas kernels, project_second(): pl.pallas_call(functools.partial(second_kernel, first), in_specs=[VMEM, V...  4.9 us
    ppermute x2, waiting for transfers between devices, swap(): return lax.ppermute(v, 'core', [(0, 1), (1, 0)])  2.14 us
    unnamed x13, local copies, waits for them, and re-layouts  1.95 us
  transfers between devices with their start and end apart: 22, of which 13 were waited for; matrix products, arithmetic and copies ran while one was open for 1% of the time, Pallas kernels for 7%

profile of v4, /device:TPU:0, one launch (start us, length us, event | category | flops | bytes accessed | tf_op | source)
XLA Modules:
  0.0 73.5 jit_solution(12332276366826291169)
XLA Ops:
  0.0 0.9 %copy-done = bf16[256,256]{1,0:T(8,128)(2,1)S(1)} copy-done((bf16[256,256]{1,0:T(8,128)(2,1)S(1)}, bf16[256,256]{1,0:T(8,128)(2,1)}, u32[]{:S(2)}) %copy-start) | copy-done | bytes 131096
  0.9 0.8 %copy-done.1 = bf16[424,48]{0,1:T(8,128)(2,1)S(1)} copy-done((bf16[424,48]{0,1:T(8,128)(2,1)S(1)}, bf16[424,48]{0,1:T(8,128)(2,1)}, u32[]{:S(2)}) %copy-start.1) | copy-done | bytes 40728
  1.7 5.1 %project_first.1 = (f32[12,32,256]{2,1,0:T(8,128)S(1)}, bf16[12,32,256]{2,1,0:T(8,128)(2,1)S(1)}, bf16[12,32,256]{2,1,0:T(8,128)(2,1)S(1)}, bf16[12,32,256]{2,1,...) custom-call(bf16[48,424]{1,0:T(8,128)(2,1)S(1)} %bitcast.2, bf16[256,256]{1,0:T(8,128)(2,1)S(1)} %copy-done, ...), custom_call_target="tpu_custom_call" | custom-call | flops 1778384896 | bytes 6946816 | tf_op jit(solution)/shard_map/project_first/pallas_call | solution.py:126
  6.8 1.6 %collective-permute-start = (bf16[12,32,256]{2,1,0:T(8,128)(2,1)S(1)}, bf16[12,32,256]{2,1,0:T(8,128)(2,1)S(1)}, u32[]{:S(2)}, u32[]{:S(2)}) collective-permute-start(bf16[12,32,256]{2,1,0:T(8,128)(2,1)S(1)} %get-tuple-element.40), channel_id=1, source_target_pairs={{0,1},{1,2},{2,3},{3,0},{4,5},{5,6},{6,7},{7,4},{8,9},{9,10},{10,1... | collective-permute-start | bytes 589832 | tf_op jit(solution)/shard_map/ppermute | solution.py:33
  8.5 1.7 %collective-permute-start.1 = (bf16[12,32,256]{2,1,0:T(8,128)(2,1)S(1)}, bf16[12,32,256]{2,1,0:T(8,128)(2,1)S(1)}, u32[]{:S(2)}, u32[]{:S(2)}) collective-permute-start(bf16[12,32,256]{2,1,0:T(8,128)(2,1)S(1)} %get-tuple-element.41), channel_id=1, source_target_pairs={{0,3},{1,0},{2,1},{3,2},{4,7},{5,4},{6,5},{7,6},{8,11},{9,8},{10,9... | collective-permute-start | bytes 589832 | tf_op jit(solution)/shard_map/ppermute | solution.py:33
  10.1 1.9 %collective-permute-start.2 = (bf16[12,32,256]{2,1,0:T(8,128)(2,1)S(1)}, bf16[12,32,256]{2,1,0:T(8,128)(2,1)S(1)}, u32[]{:S(2)}, u32[]{:S(2)}) collective-permute-start(bf16[12,32,256]{2,1,0:T(8,128)(2,1)S(1)} %get-tuple-element.42), channel_id=1, source_target_pairs={{0,2},{1,3},{2,0},{3,1},{4,6},{5,7},{6,4},{7,5},{8,10},{9,11},{10,... | collective-permute-start | bytes 589832 | tf_op jit(solution)/shard_map/ppermute | solution.py:33
  12.0 4.9 %project_second.1 = (f32[12,32,256]{2,1,0:T(8,128)S(1)}, bf16[12,32,256]{2,1,0:T(8,128)(2,1)S(1)}, bf16[12,32,256]{2,1,0:T(8,128)(2,1)S(1)}, bf16[12,32,256]{2,1,0:T(8,128)(2,1)S(1)}) custom-call(bf16[64,424]{1,0:T(8,128)(2,1)S(1)} %get-tuple-element.43.basis, bf16[256,256]{1,0:T(8,128)(2,1)S(1)} %get-tuple-element.44.col, bf16[64,424,256]{2,1,0:T(8,128)(2,1)} %bitcast.4), custom_call_target="tpu_custom_call" | custom-call | flops 1778384896 | bytes 6946816 | tf_op jit(solution)/shard_map/project_second/pallas_call | solution.py:142
  16.9 0.7 collective-permute-start.3
  17.6 2.6 %collective-permute-start.4 = (bf16[12,32,256]{2,1,0:T(8,128)(2,1)S(1)}, bf16[12,32,256]{2,1,0:T(8,128)(2,1)S(1)}, u32[]{:S(2)}, u32[]{:S(2)}) collective-permute-start(bf16[12,32,256]{2,1,0:T(8,128)(2,1)S(1)} %get-tuple-element.52), channel_id=1, source_target_pairs={{0,3},{1,0},{2,1},{3,2},{4,7},{5,4},{6,5},{7,6},{8,11},{9,8},{10,9... | collective-permute-start | bytes 589832 | tf_op jit(solution)/shard_map/ppermute | solution.py:33
  20.2 0.0 collective-permute-done.refs_1_
  20.2 0.4 collective-permute-start.5
  20.7 0.0 collective-permute-done.1.refs_2_
  20.7 0.2 collective-permute-done.2.refs_3_
  20.8 0.1 collect.2
  20.9 3.1 %collective-permute-start.6 = (bf16[32,3072]{1,0:T(8,128)(2,1)S(1)}, bf16[32,3072]{1,0:T(8,128)(2,1)S(1)}, u32[]{:S(2)}, u32[]{:S(2)}) collective-permute-start(bf16[32,3072]{1,0:T(8,128)(2,1)S(1)} %collect.2), channel_id=1, source_target_pairs={{0,96},{4,36},{32,0},{36,68},{64,32},{68,100},{96,64},{100,4},{1,9... | collective-permute-start | bytes 589832 | tf_op jit(solution)/shard_map/ppermute | solution.py:29
  24.0 4.0 %collective-permute-start.7 = (bf16[32,3072]{1,0:T(8,128)(2,1)S(1)}, bf16[32,3072]{1,0:T(8,128)(2,1)S(1)}, u32[]{:S(2)}, u32[]{:S(2)}) collective-permute-start(bf16[32,3072]{1,0:T(8,128)(2,1)S(1)} %collect.2), channel_id=1, source_target_pairs={{0,24},{4,12},{8,0},{12,20},{16,8},{20,28},{24,16},{28,4},{1,25},{... | collective-permute-start | bytes 589832 | tf_op jit(solution)/shard_map/ppermute | solution.py:29
  28.1 0.7 collective-permute-done.3.refs_1_
  28.7 2.5 %collective-permute-done.7 = bf16[32,3072]{1,0:T(8,128)(2,1)S(1)} collective-permute-done((bf16[32,3072]{1,0:T(8,128)(2,1)S(1)}, bf16[32,3072]{1,0:T(8,128)(2,1)S(1)}, u32[]{:S(2)}, u32[]{:S(2)}) %collective-permute-start.7) | collective-permute-done | bytes 196640 | tf_op jit(solution)/shard_map/ppermute | solution.py:29
  31.2 0.1 collect.3
  31.3 3.8 %collective-permute-start.8 = (bf16[32,3072]{1,0:T(8,128)(2,1)S(1)}, bf16[32,3072]{1,0:T(8,128)(2,1)S(1)}, u32[]{:S(2)}, u32[]{:S(2)}) collective-permute-start(bf16[32,3072]{1,0:T(8,128)(2,1)S(1)} %collect.3), channel_id=1, source_target_pairs={{0,24},{4,12},{8,0},{12,20},{16,8},{20,28},{24,16},{28,4},{1,25},{... | collective-permute-start | bytes 589832 | tf_op jit(solution)/shard_map/ppermute | solution.py:29
  35.1 0.9 %collective-permute-start.9 = (bf16[32,3072]{1,0:T(8,128)(2,1)S(1)}, bf16[32,3072]{1,0:T(8,128)(2,1)S(1)}, u32[]{:S(2)}, u32[]{:S(2)}) collective-permute-start(bf16[32,3072]{1,0:T(8,128)(2,1)S(1)} %collect.3), channel_id=1, source_target_pairs={{0,96},{4,36},{32,0},{36,68},{64,32},{68,100},{96,64},{100,4},{1,9... | collective-permute-start | bytes 589832 | tf_op jit(solution)/shard_map/ppermute | solution.py:29
  36.0 1.2 %collective-permute-start.13 = (bf16[64,3072]{1,0:T(8,128)(2,1)S(1)}, bf16[64,3072]{1,0:T(8,128)(2,1)S(1)}, u32[]{:S(2)}, u32[]{:S(2)}) collective-permute-start(bf16[64,3072]{1,0:T(8,128)(2,1)S(1)} %pad_maximum_fusion.4), channel_id=1, source_target_pairs={{0,32},{4,100},{32,64},{36,4},{64,96},{68,36},{96,0},{100,68},{1,3... | collective-permute-start | bytes 1179656 | tf_op jit(solution)/shard_map/ppermute | solution.py:29
  37.2 0.1 copy.8
  37.4 3.4 %collective-permute-done.9 = bf16[32,3072]{1,0:T(8,128)(2,1)S(1)} collective-permute-done((bf16[32,3072]{1,0:T(8,128)(2,1)S(1)}, bf16[32,3072]{1,0:T(8,128)(2,1)S(1)}, u32[]{:S(2)}, u32[]{:S(2)}) %collective-permute-start.9) | collective-permute-done | bytes 196640 | tf_op jit(solution)/shard_map/ppermute | solution.py:29
  40.8 0.1 pad_maximum_fusion
  40.8 0.1 collective-permute-start.10
  40.9 2.2 %collective-permute-start.11 = (bf16[64,3072]{1,0:T(8,128)(2,1)S(1)}, bf16[64,3072]{1,0:T(8,128)(2,1)S(1)}, u32[]{:S(2)}, u32[]{:S(2)}) collective-permute-start(bf16[64,3072]{1,0:T(8,128)(2,1)S(1)} %pad_maximum_fusion.2), channel_id=1, source_target_pairs={{0,96},{4,36},{32,0},{36,68},{64,32},{68,100},{96,64},{100,4},{1,9... | collective-permute-start | bytes 1179656 | tf_op jit(solution)/shard_map/ppermute | solution.py:29
  43.2 2.2 %collective-permute-start.12 = (bf16[64,3072]{1,0:T(8,128)(2,1)S(1)}, bf16[64,3072]{1,0:T(8,128)(2,1)S(1)}, u32[]{:S(2)}, u32[]{:S(2)}) collective-permute-start(bf16[64,3072]{1,0:T(8,128)(2,1)S(1)} %pad_maximum_fusion.3), channel_id=1, source_target_pairs={{0,24},{4,12},{8,0},{12,20},{16,8},{20,28},{24,16},{28,4},{1,25},{... | collective-permute-start | bytes 1179656 | tf_op jit(solution)/shard_map/ppermute | solution.py:29
  45.4 1.4 %collective-permute-done.14 = bf16[64,3072]{1,0:T(8,128)(2,1)S(1)} collective-permute-done((bf16[64,3072]{1,0:T(8,128)(2,1)S(1)}, bf16[64,3072]{1,0:T(8,128)(2,1)S(1)}, u32[]{:S(2)}, u32[]{:S(2)}) %collective-permute-start.14) | collective-permute-done | bytes 393248 | tf_op jit(solution)/shard_map/ppermute | solution.py:29
  46.8 2.0 %collective-permute-done.11 = bf16[64,3072]{1,0:T(8,128)(2,1)S(1)} collective-permute-done((bf16[64,3072]{1,0:T(8,128)(2,1)S(1)}, bf16[64,3072]{1,0:T(8,128)(2,1)S(1)}, u32[]{:S(2)}, u32[]{:S(2)}) %collective-permute-start.11) | collective-permute-done | bytes 393248 | tf_op jit(solution)/shard_map/ppermute | solution.py:29
  48.8 2.2 %collective-permute-done.12 = bf16[64,3072]{1,0:T(8,128)(2,1)S(1)} collective-permute-done((bf16[64,3072]{1,0:T(8,128)(2,1)S(1)}, bf16[64,3072]{1,0:T(8,128)(2,1)S(1)}, u32[]{:S(2)}, u32[]{:S(2)}) %collective-permute-start.12) | collective-permute-done | bytes 393248 | tf_op jit(solution)/shard_map/ppermute | solution.py:29
  51.0 0.1 pad_maximum_fusion.1
  51.1 0.3 collective-permute-start.15
  51.4 0.1 constant_dynamic-update-slice_fusion
  51.5 2.1 %collective-permute-done.15.late = bf16[128,3072]{1,0:T(8,128)(2,1)S(1)} collective-permute-done((bf16[128,3072]{1,0:T(8,128)(2,1)S(1)}, bf16[128,3072]{1,0:T(8,128)(2,1)S(1)}, u32[]{:S(2)}, u32[]{:S(2)}) %collective-permute-start.15) | collective-permute-done | bytes 786464 | tf_op jit(solution)/shard_map/ppermute | solution.py:37
  53.6 1.2 %gram.1 = (f32[256,128]{1,0:T(8,128)S(1)}, f32[256,128]{1,0:T(8,128)S(1)}, f32[256,128]{1,0:T(8,128)S(1)}, f32[256,128]{1,0:T(8,128)S(1)}) custom-call(bf16[256,3072]{1,0:T(8,128)(2,1)S(1)} %get-tuple-element.73.zs, bf16[256,3072]{1,0:T(8,128)(2,1)S(1)} %get-tuple-element.74.ys, bf16[128,3072]{1,0:T(8,128)(2,1)S(1)} %collective-permute-done.10.early, ...), custom_call_target="tpu_custom_call" | custom-call | flops 805306368 | bytes 4718592 | tf_op jit(solution)/shard_map/gram/pallas_call | solution.py:198
  54.9 2.9 %collective-permute-start.16 = (f32[256,128]{1,0:T(8,128)S(1)}, f32[256,128]{1,0:T(8,128)S(1)}, u32[]{:S(2)}, u32[]{:S(2)}) collective-permute-start(f32[256,128]{1,0:T(8,128)S(1)} %get-tuple-element.66), channel_id=1, source_target_pairs={{0,2},{4,6},{1,3},{5,7},{2,0},{6,4},{3,1},{7,5},{8,10},{12,14},{9,... | collective-permute-start | bytes 393224 | tf_op jit(solution)/shard_map/ppermute | solution.py:29
  57.7 0.5 collective-permute-start.17
  58.2 2.8 %collective-permute-start.18 = (f32[256,128]{1,0:T(8,128)S(1)}, f32[256,128]{1,0:T(8,128)S(1)}, u32[]{:S(2)}, u32[]{:S(2)}) collective-permute-start(f32[256,128]{1,0:T(8,128)S(1)} %get-tuple-element.68), channel_id=1, source_target_pairs={{0,3},{4,5},{1,0},{5,6},{2,1},{6,7},{3,2},{7,4},{8,11},{12,13},{9,... | collective-permute-start | bytes 393224 | tf_op jit(solution)/shard_map/ppermute | solution.py:29
  61.0 1.8 %collective-permute-done.16.g1 = f32[256,128]{1,0:T(8,128)S(1)} collective-permute-done((f32[256,128]{1,0:T(8,128)S(1)}, f32[256,128]{1,0:T(8,128)S(1)}, u32[]{:S(2)}, u32[]{:S(2)}) %collective-permute-start.16) | collective-permute-done | bytes 131104 | tf_op jit(solution)/shard_map/ppermute | solution.py:29
  62.8 2.3 %collective-permute-done.17.g2 = f32[256,128]{1,0:T(8,128)S(1)} collective-permute-done((f32[256,128]{1,0:T(8,128)S(1)}, f32[256,128]{1,0:T(8,128)S(1)}, u32[]{:S(2)}, u32[]{:S(2)}) %collective-permute-start.17) | collective-permute-done | bytes 131104 | tf_op jit(solution)/shard_map/ppermute | solution.py:29
  65.2 1.9 %collective-permute-start.19 = (f32[64,128]{1,0:T(8,128)S(1)}, f32[64,128]{1,0:T(8,128)S(1)}, u32[]{:S(2)}, u32[]{:S(2)}) collective-permute-start(f32[64,128]{1,0:T(8,128)S(1)} %get-tuple-element.70), channel_id=1, source_target_pairs={{0,16},{4,20},{8,24},{12,28},{16,0},{20,4},{24,8},{28,12},{1,17},{... | collective-permute-start | bytes 98312 | tf_op jit(solution)/shard_map/ppermute | solution.py:29
  67.0 1.9 %collective-permute-start.20 = (f32[64,128]{1,0:T(8,128)S(1)}, f32[64,128]{1,0:T(8,128)S(1)}, u32[]{:S(2)}, u32[]{:S(2)}) collective-permute-start(f32[64,128]{1,0:T(8,128)S(1)} %get-tuple-element.71), channel_id=1, source_target_pairs={{0,8},{4,28},{8,16},{12,4},{16,24},{20,12},{24,0},{28,20},{1,9},{5... | collective-permute-start | bytes 98312 | tf_op jit(solution)/shard_map/ppermute | solution.py:29
  68.9 1.4 %collective-permute-start.21 = (f32[64,128]{1,0:T(8,128)S(1)}, f32[64,128]{1,0:T(8,128)S(1)}, u32[]{:S(2)}, u32[]{:S(2)}) collective-permute-start(f32[64,128]{1,0:T(8,128)S(1)} %get-tuple-element.72), channel_id=1, source_target_pairs={{0,24},{4,12},{8,0},{12,20},{16,8},{20,28},{24,16},{28,4},{1,25},{... | collective-permute-start | bytes 98312 | tf_op jit(solution)/shard_map/ppermute | solution.py:29
  70.3 0.4 collective-permute-done.19.refs_1_
  70.7 1.8 %collective-permute-done.20.refs_2_ = f32[64,128]{1,0:T(8,128)S(1)} collective-permute-done((f32[64,128]{1,0:T(8,128)S(1)}, f32[64,128]{1,0:T(8,128)S(1)}, u32[]{:S(2)}, u32[]{:S(2)}) %collective-permute-start.20) | collective-permute-done | bytes 32800 | tf_op jit(solution)/shard_map/ppermute | solution.py:29
  72.4 0.4 collective-permute-done.21.refs_3_
  72.8 0.7 place.1
  (22 shorter events, 0.3 us)
Async XLA Ops:
  0.0 0.9 %copy-start = (bf16[256,256]{1,0:T(8,128)(2,1)S(1)}, bf16[256,256]{1,0:T(8,128)(2,1)}, u32[]{:S(2)}) copy-start(bf16[256,256]{1,0:T(8,128)(2,1)} %col_hbm.1) | copy-start | bytes 393220
  0.9 0.8 %copy-start.1 = (bf16[424,48]{0,1:T(8,128)(2,1)S(1)}, bf16[424,48]{0,1:T(8,128)(2,1)}, u32[]{:S(2)}) copy-start(bf16[424,48]{0,1:T(8,128)(2,1)} %param.4) | copy-start | bytes 122116
  6.8 13.4 %collective-permute-start = (bf16[12,32,256]{2,1,0:T(8,128)(2,1)S(1)}, bf16[12,32,256]{2,1,0:T(8,128)(2,1)S(1)}, u32[]{:S(2)}, u32[]{:S(2)}) collective-permute-start(bf16[12,32,256]{2,1,0:T(8,128)(2,1)S(1)} %get-tuple-element.40), channel_id=1, source_target_pairs={{0,1},{1,2},{2,3},{3,0},{4,5},{5,6},{6,7},{7,4},{8,9},{9,10},{10,1... | collective-permute-start | bytes 589832 | tf_op jit(solution)/shard_map/ppermute | solution.py:33
  8.5 12.2 %collective-permute-start.1 = (bf16[12,32,256]{2,1,0:T(8,128)(2,1)S(1)}, bf16[12,32,256]{2,1,0:T(8,128)(2,1)S(1)}, u32[]{:S(2)}, u32[]{:S(2)}) collective-permute-start(bf16[12,32,256]{2,1,0:T(8,128)(2,1)S(1)} %get-tuple-element.41), channel_id=1, source_target_pairs={{0,3},{1,0},{2,1},{3,2},{4,7},{5,4},{6,5},{7,6},{8,11},{9,8},{10,9... | collective-permute-start | bytes 589832 | tf_op jit(solution)/shard_map/ppermute | solution.py:33
  10.1 10.7 %collective-permute-start.2 = (bf16[12,32,256]{2,1,0:T(8,128)(2,1)S(1)}, bf16[12,32,256]{2,1,0:T(8,128)(2,1)S(1)}, u32[]{:S(2)}, u32[]{:S(2)}) collective-permute-start(bf16[12,32,256]{2,1,0:T(8,128)(2,1)S(1)} %get-tuple-element.42), channel_id=1, source_target_pairs={{0,2},{1,3},{2,0},{3,1},{4,6},{5,7},{6,4},{7,5},{8,10},{9,11},{10,... | collective-permute-start | bytes 589832 | tf_op jit(solution)/shard_map/ppermute | solution.py:33
  16.9 11.8 %collective-permute-start.3 = (bf16[12,32,256]{2,1,0:T(8,128)(2,1)S(1)}, bf16[12,32,256]{2,1,0:T(8,128)(2,1)S(1)}, u32[]{:S(2)}, u32[]{:S(2)}) collective-permute-start(bf16[12,32,256]{2,1,0:T(8,128)(2,1)S(1)} %get-tuple-element.51), channel_id=1, source_target_pairs={{0,1},{1,2},{2,3},{3,0},{4,5},{5,6},{6,7},{7,4},{8,9},{9,10},{10,1... | collective-permute-start | bytes 589832 | tf_op jit(solution)/shard_map/ppermute | solution.py:33
  17.6 11.1 %collective-permute-start.4 = (bf16[12,32,256]{2,1,0:T(8,128)(2,1)S(1)}, bf16[12,32,256]{2,1,0:T(8,128)(2,1)S(1)}, u32[]{:S(2)}, u32[]{:S(2)}) collective-permute-start(bf16[12,32,256]{2,1,0:T(8,128)(2,1)S(1)} %get-tuple-element.52), channel_id=1, source_target_pairs={{0,3},{1,0},{2,1},{3,2},{4,7},{5,4},{6,5},{7,6},{8,11},{9,8},{10,9... | collective-permute-start | bytes 589832 | tf_op jit(solution)/shard_map/ppermute | solution.py:33
  20.2 8.5 %collective-permute-start.5 = (bf16[12,32,256]{2,1,0:T(8,128)(2,1)S(1)}, bf16[12,32,256]{2,1,0:T(8,128)(2,1)S(1)}, u32[]{:S(2)}, u32[]{:S(2)}) collective-permute-start(bf16[12,32,256]{2,1,0:T(8,128)(2,1)S(1)} %get-tuple-element.53), channel_id=1, source_target_pairs={{0,2},{1,3},{2,0},{3,1},{4,6},{5,7},{6,4},{7,5},{8,10},{9,11},{10,... | collective-permute-start | bytes 589832 | tf_op jit(solution)/shard_map/ppermute | solution.py:33
  20.9 7.8 %collective-permute-start.6 = (bf16[32,3072]{1,0:T(8,128)(2,1)S(1)}, bf16[32,3072]{1,0:T(8,128)(2,1)S(1)}, u32[]{:S(2)}, u32[]{:S(2)}) collective-permute-start(bf16[32,3072]{1,0:T(8,128)(2,1)S(1)} %collect.2), channel_id=1, source_target_pairs={{0,96},{4,36},{32,0},{36,68},{64,32},{68,100},{96,64},{100,4},{1,9... | collective-permute-start | bytes 589832 | tf_op jit(solution)/shard_map/ppermute | solution.py:29
  24.0 7.2 %collective-permute-start.7 = (bf16[32,3072]{1,0:T(8,128)(2,1)S(1)}, bf16[32,3072]{1,0:T(8,128)(2,1)S(1)}, u32[]{:S(2)}, u32[]{:S(2)}) collective-permute-start(bf16[32,3072]{1,0:T(8,128)(2,1)S(1)} %collect.2), channel_id=1, source_target_pairs={{0,24},{4,12},{8,0},{12,20},{16,8},{20,28},{24,16},{28,4},{1,25},{... | collective-permute-start | bytes 589832 | tf_op jit(solution)/shard_map/ppermute | solution.py:29
  31.3 11.8 %collective-permute-start.8 = (bf16[32,3072]{1,0:T(8,128)(2,1)S(1)}, bf16[32,3072]{1,0:T(8,128)(2,1)S(1)}, u32[]{:S(2)}, u32[]{:S(2)}) collective-permute-start(bf16[32,3072]{1,0:T(8,128)(2,1)S(1)} %collect.3), channel_id=1, source_target_pairs={{0,24},{4,12},{8,0},{12,20},{16,8},{20,28},{24,16},{28,4},{1,25},{... | collective-permute-start | bytes 589832 | tf_op jit(solution)/shard_map/ppermute | solution.py:29
  35.1 5.7 %collective-permute-start.9 = (bf16[32,3072]{1,0:T(8,128)(2,1)S(1)}, bf16[32,3072]{1,0:T(8,128)(2,1)S(1)}, u32[]{:S(2)}, u32[]{:S(2)}) collective-permute-start(bf16[32,3072]{1,0:T(8,128)(2,1)S(1)} %collect.3), channel_id=1, source_target_pairs={{0,96},{4,36},{32,0},{36,68},{64,32},{68,100},{96,64},{100,4},{1,9... | collective-permute-start | bytes 589832 | tf_op jit(solution)/shard_map/ppermute | solution.py:29
  36.0 9.4 %collective-permute-start.13 = (bf16[64,3072]{1,0:T(8,128)(2,1)S(1)}, bf16[64,3072]{1,0:T(8,128)(2,1)S(1)}, u32[]{:S(2)}, u32[]{:S(2)}) collective-permute-start(bf16[64,3072]{1,0:T(8,128)(2,1)S(1)} %pad_maximum_fusion.4), channel_id=1, source_target_pairs={{0,32},{4,100},{32,64},{36,4},{64,96},{68,36},{96,0},{100,68},{1,3... | collective-permute-start | bytes 1179656 | tf_op jit(solution)/shard_map/ppermute | solution.py:29
  37.2 9.6 %collective-permute-start.14 = (bf16[64,3072]{1,0:T(8,128)(2,1)S(1)}, bf16[64,3072]{1,0:T(8,128)(2,1)S(1)}, u32[]{:S(2)}, u32[]{:S(2)}) collective-permute-start(bf16[64,3072]{1,0:T(8,128)(2,1)S(1)} %pad_maximum_fusion.4), channel_id=1, source_target_pairs={{0,8},{4,28},{8,16},{12,4},{16,24},{20,12},{24,0},{28,20},{1,9},{5... | collective-permute-start | bytes 1179656 | tf_op jit(solution)/shard_map/ppermute | solution.py:29
  40.8 10.2 %collective-permute-start.10 = (bf16[128,3072]{1,0:T(8,128)(2,1)S(1)}, bf16[128,3072]{1,0:T(8,128)(2,1)S(1)}, u32[]{:S(2)}, u32[]{:S(2)}) collective-permute-start(bf16[128,3072]{1,0:T(8,128)(2,1)S(1)} %pad_maximum_fusion), channel_id=1, source_target_pairs={{0,4},{4,0},{1,5},{5,1},{2,6},{6,2},{3,7},{7,3},{8,12},{12,8},{9,1... | collective-permute-start | bytes 2359304 | tf_op jit(solution)/shard_map/ppermute | solution.py:37
  40.9 7.8 %collective-permute-start.11 = (bf16[64,3072]{1,0:T(8,128)(2,1)S(1)}, bf16[64,3072]{1,0:T(8,128)(2,1)S(1)}, u32[]{:S(2)}, u32[]{:S(2)}) collective-permute-start(bf16[64,3072]{1,0:T(8,128)(2,1)S(1)} %pad_maximum_fusion.2), channel_id=1, source_target_pairs={{0,96},{4,36},{32,0},{36,68},{64,32},{68,100},{96,64},{100,4},{1,9... | collective-permute-start | bytes 1179656 | tf_op jit(solution)/shard_map/ppermute | solution.py:29
  43.2 7.8 %collective-permute-start.12 = (bf16[64,3072]{1,0:T(8,128)(2,1)S(1)}, bf16[64,3072]{1,0:T(8,128)(2,1)S(1)}, u32[]{:S(2)}, u32[]{:S(2)}) collective-permute-start(bf16[64,3072]{1,0:T(8,128)(2,1)S(1)} %pad_maximum_fusion.3), channel_id=1, source_target_pairs={{0,24},{4,12},{8,0},{12,20},{16,8},{20,28},{24,16},{28,4},{1,25},{... | collective-permute-start | bytes 1179656 | tf_op jit(solution)/shard_map/ppermute | solution.py:29
  51.1 2.5 %collective-permute-start.15 = (bf16[128,3072]{1,0:T(8,128)(2,1)S(1)}, bf16[128,3072]{1,0:T(8,128)(2,1)S(1)}, u32[]{:S(2)}, u32[]{:S(2)}) collective-permute-start(bf16[128,3072]{1,0:T(8,128)(2,1)S(1)} %pad_maximum_fusion.1), channel_id=1, source_target_pairs={{0,4},{4,0},{1,5},{5,1},{2,6},{6,2},{3,7},{7,3},{8,12},{12,8},{9,1... | collective-permute-start | bytes 2359304 | tf_op jit(solution)/shard_map/ppermute | solution.py:37
  54.9 7.9 %collective-permute-start.16 = (f32[256,128]{1,0:T(8,128)S(1)}, f32[256,128]{1,0:T(8,128)S(1)}, u32[]{:S(2)}, u32[]{:S(2)}) collective-permute-start(f32[256,128]{1,0:T(8,128)S(1)} %get-tuple-element.66), channel_id=1, source_target_pairs={{0,2},{4,6},{1,3},{5,7},{2,0},{6,4},{3,1},{7,5},{8,10},{12,14},{9,... | collective-permute-start | bytes 393224 | tf_op jit(solution)/shard_map/ppermute | solution.py:29
  57.7 7.4 %collective-permute-start.17 = (f32[256,128]{1,0:T(8,128)S(1)}, f32[256,128]{1,0:T(8,128)S(1)}, u32[]{:S(2)}, u32[]{:S(2)}) collective-permute-start(f32[256,128]{1,0:T(8,128)S(1)} %get-tuple-element.67), channel_id=1, source_target_pairs={{0,1},{4,7},{1,2},{5,4},{2,3},{6,5},{3,0},{7,6},{8,9},{12,15},{9,1... | collective-permute-start | bytes 393224 | tf_op jit(solution)/shard_map/ppermute | solution.py:29
  58.2 6.9 %collective-permute-start.18 = (f32[256,128]{1,0:T(8,128)S(1)}, f32[256,128]{1,0:T(8,128)S(1)}, u32[]{:S(2)}, u32[]{:S(2)}) collective-permute-start(f32[256,128]{1,0:T(8,128)S(1)} %get-tuple-element.68), channel_id=1, source_target_pairs={{0,3},{4,5},{1,0},{5,6},{2,1},{6,7},{3,2},{7,4},{8,11},{12,13},{9,... | collective-permute-start | bytes 393224 | tf_op jit(solution)/shard_map/ppermute | solution.py:29
  65.2 5.5 %collective-permute-start.19 = (f32[64,128]{1,0:T(8,128)S(1)}, f32[64,128]{1,0:T(8,128)S(1)}, u32[]{:S(2)}, u32[]{:S(2)}) collective-permute-start(f32[64,128]{1,0:T(8,128)S(1)} %get-tuple-element.70), channel_id=1, source_target_pairs={{0,16},{4,20},{8,24},{12,28},{16,0},{20,4},{24,8},{28,12},{1,17},{... | collective-permute-start | bytes 98312 | tf_op jit(solution)/shard_map/ppermute | solution.py:29
  67.0 5.4 %collective-permute-start.20 = (f32[64,128]{1,0:T(8,128)S(1)}, f32[64,128]{1,0:T(8,128)S(1)}, u32[]{:S(2)}, u32[]{:S(2)}) collective-permute-start(f32[64,128]{1,0:T(8,128)S(1)} %get-tuple-element.71), channel_id=1, source_target_pairs={{0,8},{4,28},{8,16},{12,4},{16,24},{20,12},{24,0},{28,20},{1,9},{5... | collective-permute-start | bytes 98312 | tf_op jit(solution)/shard_map/ppermute | solution.py:29
  68.9 3.9 %collective-permute-start.21 = (f32[64,128]{1,0:T(8,128)S(1)}, f32[64,128]{1,0:T(8,128)S(1)}, u32[]{:S(2)}, u32[]{:S(2)}) collective-permute-start(f32[64,128]{1,0:T(8,128)S(1)} %get-tuple-element.72), channel_id=1, source_target_pairs={{0,24},{4,12},{8,0},{12,20},{16,8},{20,28},{24,16},{28,4},{1,25},{... | collective-permute-start | bytes 98312 | tf_op jit(solution)/shard_map/ppermute | solution.py:29

commit v5 on v4

--- a/solution.py
+++ b/solution.py
@@ -259,16 +259,15 @@
     first = [first[0]] + [turn(first[j], j) for j in (1, 3, 2)]
     second = project_second(basis, col, pix, h, h)
     first, second[0] = lax.optimization_barrier((first, second[0]))
-    second = [second[0]] + [turn(second[j], j) for j in (1, 3, 2)]
+    second = [second[0]] + [turn(second[j], j) for j in (3, 1, 2)]
     mine = [collect(first, EARLY)]
     up = [[shift(mine[0], axis, -1)] for axis in "yz"]
     second, up = lax.optimization_barrier((second, up))
     mine.append(collect(second, LATE))
     for i, axis in enumerate("yz"):
         up[i].append(shift(mine[1], axis, -1))
-    later = mine
     far = [shift(jnp.concatenate(up[i], axis=0), axis, -1) for i, axis in enumerate("yz")]
-    down = [shift(jnp.concatenate(later, axis=0), axis, 1) for axis in "yz"]
+    down = [shift(jnp.concatenate(mine, axis=0), axis, 1) for axis in "yz"]
     early = swap(jnp.concatenate(mine + up[0], axis=0))
     early, far, down = lax.optimization_barrier((early, far, down))
     late = jnp.concatenate([far[0], down[0]], axis=0)

time: 74.2 us -> 72.7 us (0.980)
  starting transfers between devices: 37.9 us -> 35.5 us
  waiting for transfers between devices: 21.1 us -> 22.4 us
    ppermute x14, starting transfers between devices: 28.6 us -> 26.2 us  [shift(): return lax.ppermute(v, names, pairs)]
    ppermute x14, waiting for transfers between devices: 18.1 us -> 19.2 us  [shift(): return lax.ppermute(v, names, pairs)]
  transfers between devices with their start and end apart: 22 -> 22, of which waited for: 13 -> 12; matrix products, arithmetic and copies ran while one was open for 1% -> 1% of each run, Pallas kernels for 7% -> 7%
where the time goes in v5:
time: 72.7 us; the launch traced here: 72.4 us
  starting transfers between devices  35.5 us (49%)
  waiting for transfers between devices  22.4 us (31%)
  Pallas kernels  12.1 us (17%)
  local copies, waits for them, and re-layouts  2 us (3%)
    ppermute x14, starting transfers between devices, shift(): return lax.ppermute(v, names, pairs)  26.2 us
    ppermute x14, waiting for transfers between devices, shift(): return lax.ppermute(v, names, pairs)  19.2 us
    ppermute x6, starting transfers between devices, turn(): return lax.ppermute(v, 'x', [(i, (i + by) % N) for i in range(N)])  8.93 us
    pallas_call x1, Pallas kernels, project_first(): pl.pallas_call(first_kernel, in_specs=[ANY] * 3, out_specs=[VMEM] * (N +...  5.11 us
    pallas_call x1, Pallas kernels, project_second(): pl.pallas_call(functools.partial(second_kernel, first), in_specs=[VMEM, V...  4.9 us
    ppermute x2, waiting for transfers between devices, swap(): return lax.ppermute(v, 'core', [(0, 1), (1, 0)])  2.14 us
    unnamed x13, local copies, waits for them, and re-layouts  1.95 us
  transfers between devices with their start and end apart: 22, of which 12 were waited for; matrix products, arithmetic and copies ran while one was open for 1% of the time, Pallas kernels for 7%

profile of v5, /device:TPU:0, one launch (start us, length us, event | category | flops | bytes accessed | tf_op | source)
XLA Modules:
  0.0 72.4 jit_solution(11340735347324481952)
XLA Ops:
  0.0 0.9 %copy-done = bf16[256,256]{1,0:T(8,128)(2,1)S(1)} copy-done((bf16[256,256]{1,0:T(8,128)(2,1)S(1)}, bf16[256,256]{1,0:T(8,128)(2,1)}, u32[]{:S(2)}) %copy-start) | copy-done | bytes 131096
  0.9 0.8 %copy-done.1 = bf16[424,48]{0,1:T(8,128)(2,1)S(1)} copy-done((bf16[424,48]{0,1:T(8,128)(2,1)S(1)}, bf16[424,48]{0,1:T(8,128)(2,1)}, u32[]{:S(2)}) %copy-start.1) | copy-done | bytes 40728
  1.7 5.1 %project_first.1 = (f32[12,32,256]{2,1,0:T(8,128)S(1)}, bf16[12,32,256]{2,1,0:T(8,128)(2,1)S(1)}, bf16[12,32,256]{2,1,0:T(8,128)(2,1)S(1)}, bf16[12,32,256]{2,1,...) custom-call(bf16[48,424]{1,0:T(8,128)(2,1)S(1)} %bitcast.2, bf16[256,256]{1,0:T(8,128)(2,1)S(1)} %copy-done, ...), custom_call_target="tpu_custom_call" | custom-call | flops 1778384896 | bytes 6946816 | tf_op jit(solution)/shard_map/project_first/pallas_call | solution.py:126
  6.8 1.6 %collective-permute-start = (bf16[12,32,256]{2,1,0:T(8,128)(2,1)S(1)}, bf16[12,32,256]{2,1,0:T(8,128)(2,1)S(1)}, u32[]{:S(2)}, u32[]{:S(2)}) collective-permute-start(bf16[12,32,256]{2,1,0:T(8,128)(2,1)S(1)} %get-tuple-element.40), channel_id=1, source_target_pairs={{0,1},{1,2},{2,3},{3,0},{4,5},{5,6},{6,7},{7,4},{8,9},{9,10},{10,1... | collective-permute-start | bytes 589832 | tf_op jit(solution)/shard_map/ppermute | solution.py:33
  8.5 1.7 %collective-permute-start.1 = (bf16[12,32,256]{2,1,0:T(8,128)(2,1)S(1)}, bf16[12,32,256]{2,1,0:T(8,128)(2,1)S(1)}, u32[]{:S(2)}, u32[]{:S(2)}) collective-permute-start(bf16[12,32,256]{2,1,0:T(8,128)(2,1)S(1)} %get-tuple-element.41), channel_id=1, source_target_pairs={{0,3},{1,0},{2,1},{3,2},{4,7},{5,4},{6,5},{7,6},{8,11},{9,8},{10,9... | collective-permute-start | bytes 589832 | tf_op jit(solution)/shard_map/ppermute | solution.py:33
  10.1 1.9 %collective-permute-start.2 = (bf16[12,32,256]{2,1,0:T(8,128)(2,1)S(1)}, bf16[12,32,256]{2,1,0:T(8,128)(2,1)S(1)}, u32[]{:S(2)}, u32[]{:S(2)}) collective-permute-start(bf16[12,32,256]{2,1,0:T(8,128)(2,1)S(1)} %get-tuple-element.42), channel_id=1, source_target_pairs={{0,2},{1,3},{2,0},{3,1},{4,6},{5,7},{6,4},{7,5},{8,10},{9,11},{10,... | collective-permute-start | bytes 589832 | tf_op jit(solution)/shard_map/ppermute | solution.py:33
  12.0 4.9 %project_second.1 = (f32[12,32,256]{2,1,0:T(8,128)S(1)}, bf16[12,32,256]{2,1,0:T(8,128)(2,1)S(1)}, bf16[12,32,256]{2,1,0:T(8,128)(2,1)S(1)}, bf16[12,32,256]{2,1,0:T(8,128)(2,1)S(1)}) custom-call(bf16[64,424]{1,0:T(8,128)(2,1)S(1)} %get-tuple-element.43.basis, bf16[256,256]{1,0:T(8,128)(2,1)S(1)} %get-tuple-element.44.col, bf16[64,424,256]{2,1,0:T(8,128)(2,1)} %bitcast.4), custom_call_target="tpu_custom_call" | custom-call | flops 1778384896 | bytes 6946816 | tf_op jit(solution)/shard_map/project_second/pallas_call | solution.py:142
  16.9 1.2 %collective-permute-start.3 = (bf16[12,32,256]{2,1,0:T(8,128)(2,1)S(1)}, bf16[12,32,256]{2,1,0:T(8,128)(2,1)S(1)}, u32[]{:S(2)}, u32[]{:S(2)}) collective-permute-start(bf16[12,32,256]{2,1,0:T(8,128)(2,1)S(1)} %get-tuple-element.51), channel_id=1, source_target_pairs={{0,3},{1,0},{2,1},{3,2},{4,7},{5,4},{6,5},{7,6},{8,11},{9,8},{10,9... | collective-permute-start | bytes 589832 | tf_op jit(solution)/shard_map/ppermute | solution.py:33
  18.1 0.9 %collective-permute-start.4 = (bf16[12,32,256]{2,1,0:T(8,128)(2,1)S(1)}, bf16[12,32,256]{2,1,0:T(8,128)(2,1)S(1)}, u32[]{:S(2)}, u32[]{:S(2)}) collective-permute-start(bf16[12,32,256]{2,1,0:T(8,128)(2,1)S(1)} %get-tuple-element.52), channel_id=1, source_target_pairs={{0,1},{1,2},{2,3},{3,0},{4,5},{5,6},{6,7},{7,4},{8,9},{9,10},{10,1... | collective-permute-start | bytes 589832 | tf_op jit(solution)/shard_map/ppermute | solution.py:33
  19.0 0.0 collective-permute-done.refs_1_
  19.0 1.6 %collective-permute-start.5 = (bf16[12,32,256]{2,1,0:T(8,128)(2,1)S(1)}, bf16[12,32,256]{2,1,0:T(8,128)(2,1)S(1)}, u32[]{:S(2)}, u32[]{:S(2)}) collective-permute-start(bf16[12,32,256]{2,1,0:T(8,128)(2,1)S(1)} %get-tuple-element.53), channel_id=1, source_target_pairs={{0,2},{1,3},{2,0},{3,1},{4,6},{5,7},{6,4},{7,5},{8,10},{9,11},{10,... | collective-permute-start | bytes 589832 | tf_op jit(solution)/shard_map/ppermute | solution.py:33
  20.7 0.0 collective-permute-done.1.refs_2_
  20.7 0.0 collective-permute-done.2.refs_3_
  20.7 0.1 collect.2
  20.8 3.2 %collective-permute-start.6 = (bf16[32,3072]{1,0:T(8,128)(2,1)S(1)}, bf16[32,3072]{1,0:T(8,128)(2,1)S(1)}, u32[]{:S(2)}, u32[]{:S(2)}) collective-permute-start(bf16[32,3072]{1,0:T(8,128)(2,1)S(1)} %collect.2), channel_id=1, source_target_pairs={{0,96},{4,36},{32,0},{36,68},{64,32},{68,100},{96,64},{100,4},{1,9... | collective-permute-start | bytes 589832 | tf_op jit(solution)/shard_map/ppermute | solution.py:29
  23.9 4.0 %collective-permute-start.7 = (bf16[32,3072]{1,0:T(8,128)(2,1)S(1)}, bf16[32,3072]{1,0:T(8,128)(2,1)S(1)}, u32[]{:S(2)}, u32[]{:S(2)}) collective-permute-start(bf16[32,3072]{1,0:T(8,128)(2,1)S(1)} %collect.2), channel_id=1, source_target_pairs={{0,24},{4,12},{8,0},{12,20},{16,8},{20,28},{24,16},{28,4},{1,25},{... | collective-permute-start | bytes 589832 | tf_op jit(solution)/shard_map/ppermute | solution.py:29
  28.0 1.1 %collective-permute-done.4.refs_2_ = bf16[12,32,256]{2,1,0:T(8,128)(2,1)S(1)} collective-permute-done((bf16[12,32,256]{2,1,0:T(8,128)(2,1)S(1)}, bf16[12,32,256]{2,1,0:T(8,128)(2,1)S(1)}, u32[]{:S(2)}, u32[]{:S(2)}) %collective-permute-start.4) | collective-permute-done | bytes 196640 | tf_op jit(solution)/shard_map/ppermute | solution.py:33
  29.1 2.1 %collective-permute-done.7 = bf16[32,3072]{1,0:T(8,128)(2,1)S(1)} collective-permute-done((bf16[32,3072]{1,0:T(8,128)(2,1)S(1)}, bf16[32,3072]{1,0:T(8,128)(2,1)S(1)}, u32[]{:S(2)}, u32[]{:S(2)}) %collective-permute-start.7) | collective-permute-done | bytes 196640 | tf_op jit(solution)/shard_map/ppermute | solution.py:29
  31.1 0.1 collect.3
  31.3 3.8 %collective-permute-start.8 = (bf16[32,3072]{1,0:T(8,128)(2,1)S(1)}, bf16[32,3072]{1,0:T(8,128)(2,1)S(1)}, u32[]{:S(2)}, u32[]{:S(2)}) collective-permute-start(bf16[32,3072]{1,0:T(8,128)(2,1)S(1)} %collect.3), channel_id=1, source_target_pairs={{0,24},{4,12},{8,0},{12,20},{16,8},{20,28},{24,16},{28,4},{1,25},{... | collective-permute-start | bytes 589832 | tf_op jit(solution)/shard_map/ppermute | solution.py:29
  35.0 1.3 %collective-permute-start.9 = (bf16[32,3072]{1,0:T(8,128)(2,1)S(1)}, bf16[32,3072]{1,0:T(8,128)(2,1)S(1)}, u32[]{:S(2)}, u32[]{:S(2)}) collective-permute-start(bf16[32,3072]{1,0:T(8,128)(2,1)S(1)} %collect.3), channel_id=1, source_target_pairs={{0,96},{4,36},{32,0},{36,68},{64,32},{68,100},{96,64},{100,4},{1,9... | collective-permute-start | bytes 589832 | tf_op jit(solution)/shard_map/ppermute | solution.py:29
  36.4 0.8 %collective-permute-start.13 = (bf16[64,3072]{1,0:T(8,128)(2,1)S(1)}, bf16[64,3072]{1,0:T(8,128)(2,1)S(1)}, u32[]{:S(2)}, u32[]{:S(2)}) collective-permute-start(bf16[64,3072]{1,0:T(8,128)(2,1)S(1)} %pad_maximum_fusion.4), channel_id=1, source_target_pairs={{0,32},{4,100},{32,64},{36,4},{64,96},{68,36},{96,0},{100,68},{1,3... | collective-permute-start | bytes 1179656 | tf_op jit(solution)/shard_map/ppermute | solution.py:29
  37.2 0.1 copy.8
  37.3 3.4 %collective-permute-done.9 = bf16[32,3072]{1,0:T(8,128)(2,1)S(1)} collective-permute-done((bf16[32,3072]{1,0:T(8,128)(2,1)S(1)}, bf16[32,3072]{1,0:T(8,128)(2,1)S(1)}, u32[]{:S(2)}, u32[]{:S(2)}) %collective-permute-start.9) | collective-permute-done | bytes 196640 | tf_op jit(solution)/shard_map/ppermute | solution.py:29
  40.7 0.1 pad_maximum_fusion
  40.7 0.1 collective-permute-start.10
  40.9 2.6 %collective-permute-start.11 = (bf16[64,3072]{1,0:T(8,128)(2,1)S(1)}, bf16[64,3072]{1,0:T(8,128)(2,1)S(1)}, u32[]{:S(2)}, u32[]{:S(2)}) collective-permute-start(bf16[64,3072]{1,0:T(8,128)(2,1)S(1)} %pad_maximum_fusion.2), channel_id=1, source_target_pairs={{0,96},{4,36},{32,0},{36,68},{64,32},{68,100},{96,64},{100,4},{1,9... | collective-permute-start | bytes 1179656 | tf_op jit(solution)/shard_map/ppermute | solution.py:29
  43.5 0.7 %collective-permute-start.12 = (bf16[64,3072]{1,0:T(8,128)(2,1)S(1)}, bf16[64,3072]{1,0:T(8,128)(2,1)S(1)}, u32[]{:S(2)}, u32[]{:S(2)}) collective-permute-start(bf16[64,3072]{1,0:T(8,128)(2,1)S(1)} %pad_maximum_fusion.3), channel_id=1, source_target_pairs={{0,24},{4,12},{8,0},{12,20},{16,8},{20,28},{24,16},{28,4},{1,25},{... | collective-permute-start | bytes 1179656 | tf_op jit(solution)/shard_map/ppermute | solution.py:29
  44.3 1.3 %collective-permute-done.13 = bf16[64,3072]{1,0:T(8,128)(2,1)S(1)} collective-permute-done((bf16[64,3072]{1,0:T(8,128)(2,1)S(1)}, bf16[64,3072]{1,0:T(8,128)(2,1)S(1)}, u32[]{:S(2)}, u32[]{:S(2)}) %collective-permute-start.13) | collective-permute-done | bytes 393248 | tf_op jit(solution)/shard_map/ppermute | solution.py:29
  45.5 1.3 %collective-permute-done.14 = bf16[64,3072]{1,0:T(8,128)(2,1)S(1)} collective-permute-done((bf16[64,3072]{1,0:T(8,128)(2,1)S(1)}, bf16[64,3072]{1,0:T(8,128)(2,1)S(1)}, u32[]{:S(2)}, u32[]{:S(2)}) %collective-permute-start.14) | collective-permute-done | bytes 393248 | tf_op jit(solution)/shard_map/ppermute | solution.py:29
  46.8 1.9 %collective-permute-done.11 = bf16[64,3072]{1,0:T(8,128)(2,1)S(1)} collective-permute-done((bf16[64,3072]{1,0:T(8,128)(2,1)S(1)}, bf16[64,3072]{1,0:T(8,128)(2,1)S(1)}, u32[]{:S(2)}, u32[]{:S(2)}) %collective-permute-start.11) | collective-permute-done | bytes 393248 | tf_op jit(solution)/shard_map/ppermute | solution.py:29
  48.8 2.6 %collective-permute-done.12 = bf16[64,3072]{1,0:T(8,128)(2,1)S(1)} collective-permute-done((bf16[64,3072]{1,0:T(8,128)(2,1)S(1)}, bf16[64,3072]{1,0:T(8,128)(2,1)S(1)}, u32[]{:S(2)}, u32[]{:S(2)}) %collective-permute-start.12) | collective-permute-done | bytes 393248 | tf_op jit(solution)/shard_map/ppermute | solution.py:29
  51.3 0.1 pad_maximum_fusion.1
  51.4 0.3 collective-permute-start.15
  51.7 0.1 constant_dynamic-update-slice_fusion
  51.8 2.1 %collective-permute-done.15.late = bf16[128,3072]{1,0:T(8,128)(2,1)S(1)} collective-permute-done((bf16[128,3072]{1,0:T(8,128)(2,1)S(1)}, bf16[128,3072]{1,0:T(8,128)(2,1)S(1)}, u32[]{:S(2)}, u32[]{:S(2)}) %collective-permute-start.15) | collective-permute-done | bytes 786464 | tf_op jit(solution)/shard_map/ppermute | solution.py:37
  53.9 1.2 %gram.1 = (f32[256,128]{1,0:T(8,128)S(1)}, f32[256,128]{1,0:T(8,128)S(1)}, f32[256,128]{1,0:T(8,128)S(1)}, f32[256,128]{1,0:T(8,128)S(1)}) custom-call(bf16[256,3072]{1,0:T(8,128)(2,1)S(1)} %get-tuple-element.73.zs, bf16[256,3072]{1,0:T(8,128)(2,1)S(1)} %get-tuple-element.74.ys, bf16[128,3072]{1,0:T(8,128)(2,1)S(1)} %collective-permute-done.10.early, ...), custom_call_target="tpu_custom_call" | custom-call | flops 805306368 | bytes 4718592 | tf_op jit(solution)/shard_map/gram/pallas_call | solution.py:198
  55.2 1.3 %collective-permute-start.16 = (f32[256,128]{1,0:T(8,128)S(1)}, f32[256,128]{1,0:T(8,128)S(1)}, u32[]{:S(2)}, u32[]{:S(2)}) collective-permute-start(f32[256,128]{1,0:T(8,128)S(1)} %get-tuple-element.66), channel_id=1, source_target_pairs={{0,2},{4,6},{1,3},{5,7},{2,0},{6,4},{3,1},{7,5},{8,10},{12,14},{9,... | collective-permute-start | bytes 393224 | tf_op jit(solution)/shard_map/ppermute | solution.py:29
  56.5 1.0 %collective-permute-start.17 = (f32[256,128]{1,0:T(8,128)S(1)}, f32[256,128]{1,0:T(8,128)S(1)}, u32[]{:S(2)}, u32[]{:S(2)}) collective-permute-start(f32[256,128]{1,0:T(8,128)S(1)} %get-tuple-element.67), channel_id=1, source_target_pairs={{0,1},{4,7},{1,2},{5,4},{2,3},{6,5},{3,0},{7,6},{8,9},{12,15},{9,1... | collective-permute-start | bytes 393224 | tf_op jit(solution)/shard_map/ppermute | solution.py:29
  57.5 2.3 %collective-permute-start.18 = (f32[256,128]{1,0:T(8,128)S(1)}, f32[256,128]{1,0:T(8,128)S(1)}, u32[]{:S(2)}, u32[]{:S(2)}) collective-permute-start(f32[256,128]{1,0:T(8,128)S(1)} %get-tuple-element.68), channel_id=1, source_target_pairs={{0,3},{4,5},{1,0},{5,6},{2,1},{6,7},{3,2},{7,4},{8,11},{12,13},{9,... | collective-permute-start | bytes 393224 | tf_op jit(solution)/shard_map/ppermute | solution.py:29
  59.8 3.3 %collective-permute-done.16.g1 = f32[256,128]{1,0:T(8,128)S(1)} collective-permute-done((f32[256,128]{1,0:T(8,128)S(1)}, f32[256,128]{1,0:T(8,128)S(1)}, u32[]{:S(2)}, u32[]{:S(2)}) %collective-permute-start.16) | collective-permute-done | bytes 131104 | tf_op jit(solution)/shard_map/ppermute | solution.py:29
  63.1 1.4 %collective-permute-done.17.g2 = f32[256,128]{1,0:T(8,128)S(1)} collective-permute-done((f32[256,128]{1,0:T(8,128)S(1)}, f32[256,128]{1,0:T(8,128)S(1)}, u32[]{:S(2)}, u32[]{:S(2)}) %collective-permute-start.17) | collective-permute-done | bytes 131104 | tf_op jit(solution)/shard_map/ppermute | solution.py:29
  64.6 2.0 %collective-permute-start.19 = (f32[64,128]{1,0:T(8,128)S(1)}, f32[64,128]{1,0:T(8,128)S(1)}, u32[]{:S(2)}, u32[]{:S(2)}) collective-permute-start(f32[64,128]{1,0:T(8,128)S(1)} %get-tuple-element.70), channel_id=1, source_target_pairs={{0,16},{4,20},{8,24},{12,28},{16,0},{20,4},{24,8},{28,12},{1,17},{... | collective-permute-start | bytes 98312 | tf_op jit(solution)/shard_map/ppermute | solution.py:29
  66.6 1.2 %collective-permute-start.20 = (f32[64,128]{1,0:T(8,128)S(1)}, f32[64,128]{1,0:T(8,128)S(1)}, u32[]{:S(2)}, u32[]{:S(2)}) collective-permute-start(f32[64,128]{1,0:T(8,128)S(1)} %get-tuple-element.71), channel_id=1, source_target_pairs={{0,8},{4,28},{8,16},{12,4},{16,24},{20,12},{24,0},{28,20},{1,9},{5... | collective-permute-start | bytes 98312 | tf_op jit(solution)/shard_map/ppermute | solution.py:29
  67.8 2.0 %collective-permute-start.21 = (f32[64,128]{1,0:T(8,128)S(1)}, f32[64,128]{1,0:T(8,128)S(1)}, u32[]{:S(2)}, u32[]{:S(2)}) collective-permute-start(f32[64,128]{1,0:T(8,128)S(1)} %get-tuple-element.72), channel_id=1, source_target_pairs={{0,24},{4,12},{8,0},{12,20},{16,8},{20,28},{24,16},{28,4},{1,25},{... | collective-permute-start | bytes 98312 | tf_op jit(solution)/shard_map/ppermute | solution.py:29
  69.8 0.3 collective-permute-done.19.refs_1_
  70.1 1.6 %collective-permute-done.20.refs_2_ = f32[64,128]{1,0:T(8,128)S(1)} collective-permute-done((f32[64,128]{1,0:T(8,128)S(1)}, f32[64,128]{1,0:T(8,128)S(1)}, u32[]{:S(2)}, u32[]{:S(2)}) %collective-permute-start.20) | collective-permute-done | bytes 32800 | tf_op jit(solution)/shard_map/ppermute | solution.py:29
  71.7 0.7 place.1
  (22 shorter events, 0.3 us)
Async XLA Ops:
  0.0 0.9 %copy-start = (bf16[256,256]{1,0:T(8,128)(2,1)S(1)}, bf16[256,256]{1,0:T(8,128)(2,1)}, u32[]{:S(2)}) copy-start(bf16[256,256]{1,0:T(8,128)(2,1)} %col_hbm.1) | copy-start | bytes 393220
  0.9 0.8 %copy-start.1 = (bf16[424,48]{0,1:T(8,128)(2,1)S(1)}, bf16[424,48]{0,1:T(8,128)(2,1)}, u32[]{:S(2)}) copy-start(bf16[424,48]{0,1:T(8,128)(2,1)} %param.4) | copy-start | bytes 122116
  6.8 12.2 %collective-permute-start = (bf16[12,32,256]{2,1,0:T(8,128)(2,1)S(1)}, bf16[12,32,256]{2,1,0:T(8,128)(2,1)S(1)}, u32[]{:S(2)}, u32[]{:S(2)}) collective-permute-start(bf16[12,32,256]{2,1,0:T(8,128)(2,1)S(1)} %get-tuple-element.40), channel_id=1, source_target_pairs={{0,1},{1,2},{2,3},{3,0},{4,5},{5,6},{6,7},{7,4},{8,9},{9,10},{10,1... | collective-permute-start | bytes 589832 | tf_op jit(solution)/shard_map/ppermute | solution.py:33
  8.5 12.2 %collective-permute-start.1 = (bf16[12,32,256]{2,1,0:T(8,128)(2,1)S(1)}, bf16[12,32,256]{2,1,0:T(8,128)(2,1)S(1)}, u32[]{:S(2)}, u32[]{:S(2)}) collective-permute-start(bf16[12,32,256]{2,1,0:T(8,128)(2,1)S(1)} %get-tuple-element.41), channel_id=1, source_target_pairs={{0,3},{1,0},{2,1},{3,2},{4,7},{5,4},{6,5},{7,6},{8,11},{9,8},{10,9... | collective-permute-start | bytes 589832 | tf_op jit(solution)/shard_map/ppermute | solution.py:33
  10.1 10.5 %collective-permute-start.2 = (bf16[12,32,256]{2,1,0:T(8,128)(2,1)S(1)}, bf16[12,32,256]{2,1,0:T(8,128)(2,1)S(1)}, u32[]{:S(2)}, u32[]{:S(2)}) collective-permute-start(bf16[12,32,256]{2,1,0:T(8,128)(2,1)S(1)} %get-tuple-element.42), channel_id=1, source_target_pairs={{0,2},{1,3},{2,0},{3,1},{4,6},{5,7},{6,4},{7,5},{8,10},{9,11},{10,... | collective-permute-start | bytes 589832 | tf_op jit(solution)/shard_map/ppermute | solution.py:33
  16.9 11.0 %collective-permute-start.3 = (bf16[12,32,256]{2,1,0:T(8,128)(2,1)S(1)}, bf16[12,32,256]{2,1,0:T(8,128)(2,1)S(1)}, u32[]{:S(2)}, u32[]{:S(2)}) collective-permute-start(bf16[12,32,256]{2,1,0:T(8,128)(2,1)S(1)} %get-tuple-element.51), channel_id=1, source_target_pairs={{0,3},{1,0},{2,1},{3,2},{4,7},{5,4},{6,5},{7,6},{8,11},{9,8},{10,9... | collective-permute-start | bytes 589832 | tf_op jit(solution)/shard_map/ppermute | solution.py:33
  18.1 10.9 %collective-permute-start.4 = (bf16[12,32,256]{2,1,0:T(8,128)(2,1)S(1)}, bf16[12,32,256]{2,1,0:T(8,128)(2,1)S(1)}, u32[]{:S(2)}, u32[]{:S(2)}) collective-permute-start(bf16[12,32,256]{2,1,0:T(8,128)(2,1)S(1)} %get-tuple-element.52), channel_id=1, source_target_pairs={{0,1},{1,2},{2,3},{3,0},{4,5},{5,6},{6,7},{7,4},{8,9},{9,10},{10,1... | collective-permute-start | bytes 589832 | tf_op jit(solution)/shard_map/ppermute | solution.py:33
  19.0 10.1 %collective-permute-start.5 = (bf16[12,32,256]{2,1,0:T(8,128)(2,1)S(1)}, bf16[12,32,256]{2,1,0:T(8,128)(2,1)S(1)}, u32[]{:S(2)}, u32[]{:S(2)}) collective-permute-start(bf16[12,32,256]{2,1,0:T(8,128)(2,1)S(1)} %get-tuple-element.53), channel_id=1, source_target_pairs={{0,2},{1,3},{2,0},{3,1},{4,6},{5,7},{6,4},{7,5},{8,10},{9,11},{10,... | collective-permute-start | bytes 589832 | tf_op jit(solution)/shard_map/ppermute | solution.py:33
  20.8 8.3 %collective-permute-start.6 = (bf16[32,3072]{1,0:T(8,128)(2,1)S(1)}, bf16[32,3072]{1,0:T(8,128)(2,1)S(1)}, u32[]{:S(2)}, u32[]{:S(2)}) collective-permute-start(bf16[32,3072]{1,0:T(8,128)(2,1)S(1)} %collect.2), channel_id=1, source_target_pairs={{0,96},{4,36},{32,0},{36,68},{64,32},{68,100},{96,64},{100,4},{1,9... | collective-permute-start | bytes 589832 | tf_op jit(solution)/shard_map/ppermute | solution.py:29
  23.9 7.2 %collective-permute-start.7 = (bf16[32,3072]{1,0:T(8,128)(2,1)S(1)}, bf16[32,3072]{1,0:T(8,128)(2,1)S(1)}, u32[]{:S(2)}, u32[]{:S(2)}) collective-permute-start(bf16[32,3072]{1,0:T(8,128)(2,1)S(1)} %collect.2), channel_id=1, source_target_pairs={{0,24},{4,12},{8,0},{12,20},{16,8},{20,28},{24,16},{28,4},{1,25},{... | collective-permute-start | bytes 589832 | tf_op jit(solution)/shard_map/ppermute | solution.py:29
  31.3 12.2 %collective-permute-start.8 = (bf16[32,3072]{1,0:T(8,128)(2,1)S(1)}, bf16[32,3072]{1,0:T(8,128)(2,1)S(1)}, u32[]{:S(2)}, u32[]{:S(2)}) collective-permute-start(bf16[32,3072]{1,0:T(8,128)(2,1)S(1)} %collect.3), channel_id=1, source_target_pairs={{0,24},{4,12},{8,0},{12,20},{16,8},{20,28},{24,16},{28,4},{1,25},{... | collective-permute-start | bytes 589832 | tf_op jit(solution)/shard_map/ppermute | solution.py:29
  35.0 5.7 %collective-permute-start.9 = (bf16[32,3072]{1,0:T(8,128)(2,1)S(1)}, bf16[32,3072]{1,0:T(8,128)(2,1)S(1)}, u32[]{:S(2)}, u32[]{:S(2)}) collective-permute-start(bf16[32,3072]{1,0:T(8,128)(2,1)S(1)} %collect.3), channel_id=1, source_target_pairs={{0,96},{4,36},{32,0},{36,68},{64,32},{68,100},{96,64},{100,4},{1,9... | collective-permute-start | bytes 589832 | tf_op jit(solution)/shard_map/ppermute | solution.py:29
  36.4 9.2 %collective-permute-start.13 = (bf16[64,3072]{1,0:T(8,128)(2,1)S(1)}, bf16[64,3072]{1,0:T(8,128)(2,1)S(1)}, u32[]{:S(2)}, u32[]{:S(2)}) collective-permute-start(bf16[64,3072]{1,0:T(8,128)(2,1)S(1)} %pad_maximum_fusion.4), channel_id=1, source_target_pairs={{0,32},{4,100},{32,64},{36,4},{64,96},{68,36},{96,0},{100,68},{1,3... | collective-permute-start | bytes 1179656 | tf_op jit(solution)/shard_map/ppermute | solution.py:29
  37.1 9.7 %collective-permute-start.14 = (bf16[64,3072]{1,0:T(8,128)(2,1)S(1)}, bf16[64,3072]{1,0:T(8,128)(2,1)S(1)}, u32[]{:S(2)}, u32[]{:S(2)}) collective-permute-start(bf16[64,3072]{1,0:T(8,128)(2,1)S(1)} %pad_maximum_fusion.4), channel_id=1, source_target_pairs={{0,8},{4,28},{8,16},{12,4},{16,24},{20,12},{24,0},{28,20},{1,9},{5... | collective-permute-start | bytes 1179656 | tf_op jit(solution)/shard_map/ppermute | solution.py:29
  40.7 10.6 %collective-permute-start.10 = (bf16[128,3072]{1,0:T(8,128)(2,1)S(1)}, bf16[128,3072]{1,0:T(8,128)(2,1)S(1)}, u32[]{:S(2)}, u32[]{:S(2)}) collective-permute-start(bf16[128,3072]{1,0:T(8,128)(2,1)S(1)} %pad_maximum_fusion), channel_id=1, source_target_pairs={{0,4},{4,0},{1,5},{5,1},{2,6},{6,2},{3,7},{7,3},{8,12},{12,8},{9,1... | collective-permute-start | bytes 2359304 | tf_op jit(solution)/shard_map/ppermute | solution.py:37
  40.9 7.9 %collective-permute-start.11 = (bf16[64,3072]{1,0:T(8,128)(2,1)S(1)}, bf16[64,3072]{1,0:T(8,128)(2,1)S(1)}, u32[]{:S(2)}, u32[]{:S(2)}) collective-permute-start(bf16[64,3072]{1,0:T(8,128)(2,1)S(1)} %pad_maximum_fusion.2), channel_id=1, source_target_pairs={{0,96},{4,36},{32,0},{36,68},{64,32},{68,100},{96,64},{100,4},{1,9... | collective-permute-start | bytes 1179656 | tf_op jit(solution)/shard_map/ppermute | solution.py:29
  43.5 7.8 %collective-permute-start.12 = (bf16[64,3072]{1,0:T(8,128)(2,1)S(1)}, bf16[64,3072]{1,0:T(8,128)(2,1)S(1)}, u32[]{:S(2)}, u32[]{:S(2)}) collective-permute-start(bf16[64,3072]{1,0:T(8,128)(2,1)S(1)} %pad_maximum_fusion.3), channel_id=1, source_target_pairs={{0,24},{4,12},{8,0},{12,20},{16,8},{20,28},{24,16},{28,4},{1,25},{... | collective-permute-start | bytes 1179656 | tf_op jit(solution)/shard_map/ppermute | solution.py:29
  51.4 2.5 %collective-permute-start.15 = (bf16[128,3072]{1,0:T(8,128)(2,1)S(1)}, bf16[128,3072]{1,0:T(8,128)(2,1)S(1)}, u32[]{:S(2)}, u32[]{:S(2)}) collective-permute-start(bf16[128,3072]{1,0:T(8,128)(2,1)S(1)} %pad_maximum_fusion.1), channel_id=1, source_target_pairs={{0,4},{4,0},{1,5},{5,1},{2,6},{6,2},{3,7},{7,3},{8,12},{12,8},{9,1... | collective-permute-start | bytes 2359304 | tf_op jit(solution)/shard_map/ppermute | solution.py:37
  55.2 7.9 %collective-permute-start.16 = (f32[256,128]{1,0:T(8,128)S(1)}, f32[256,128]{1,0:T(8,128)S(1)}, u32[]{:S(2)}, u32[]{:S(2)}) collective-permute-start(f32[256,128]{1,0:T(8,128)S(1)} %get-tuple-element.66), channel_id=1, source_target_pairs={{0,2},{4,6},{1,3},{5,7},{2,0},{6,4},{3,1},{7,5},{8,10},{12,14},{9,... | collective-permute-start | bytes 393224 | tf_op jit(solution)/shard_map/ppermute | solution.py:29
  56.5 8.0 %collective-permute-start.17 = (f32[256,128]{1,0:T(8,128)S(1)}, f32[256,128]{1,0:T(8,128)S(1)}, u32[]{:S(2)}, u32[]{:S(2)}) collective-permute-start(f32[256,128]{1,0:T(8,128)S(1)} %get-tuple-element.67), channel_id=1, source_target_pairs={{0,1},{4,7},{1,2},{5,4},{2,3},{6,5},{3,0},{7,6},{8,9},{12,15},{9,1... | collective-permute-start | bytes 393224 | tf_op jit(solution)/shard_map/ppermute | solution.py:29
  57.5 7.1 %collective-permute-start.18 = (f32[256,128]{1,0:T(8,128)S(1)}, f32[256,128]{1,0:T(8,128)S(1)}, u32[]{:S(2)}, u32[]{:S(2)}) collective-permute-start(f32[256,128]{1,0:T(8,128)S(1)} %get-tuple-element.68), channel_id=1, source_target_pairs={{0,3},{4,5},{1,0},{5,6},{2,1},{6,7},{3,2},{7,4},{8,11},{12,13},{9,... | collective-permute-start | bytes 393224 | tf_op jit(solution)/shard_map/ppermute | solution.py:29
  64.6 5.5 %collective-permute-start.19 = (f32[64,128]{1,0:T(8,128)S(1)}, f32[64,128]{1,0:T(8,128)S(1)}, u32[]{:S(2)}, u32[]{:S(2)}) collective-permute-start(f32[64,128]{1,0:T(8,128)S(1)} %get-tuple-element.70), channel_id=1, source_target_pairs={{0,16},{4,20},{8,24},{12,28},{16,0},{20,4},{24,8},{28,12},{1,17},{... | collective-permute-start | bytes 98312 | tf_op jit(solution)/shard_map/ppermute | solution.py:29
  66.6 5.1 %collective-permute-start.20 = (f32[64,128]{1,0:T(8,128)S(1)}, f32[64,128]{1,0:T(8,128)S(1)}, u32[]{:S(2)}, u32[]{:S(2)}) collective-permute-start(f32[64,128]{1,0:T(8,128)S(1)} %get-tuple-element.71), channel_id=1, source_target_pairs={{0,8},{4,28},{8,16},{12,4},{16,24},{20,12},{24,0},{28,20},{1,9},{5... | collective-permute-start | bytes 98312 | tf_op jit(solution)/shard_map/ppermute | solution.py:29
  67.8 3.9 %collective-permute-start.21 = (f32[64,128]{1,0:T(8,128)S(1)}, f32[64,128]{1,0:T(8,128)S(1)}, u32[]{:S(2)}, u32[]{:S(2)}) collective-permute-start(f32[64,128]{1,0:T(8,128)S(1)} %get-tuple-element.72), channel_id=1, source_target_pairs={{0,24},{4,12},{8,0},{12,20},{16,8},{20,28},{24,16},{28,4},{1,25},{... | collective-permute-start | bytes 98312 | tf_op jit(solution)/shard_map/ppermute | solution.py:29

commit v6 on v5

--- a/solution.py
+++ b/solution.py
@@ -58,7 +58,7 @@
             if row % IN_ROWS == 0:
                 copies[row // IN_ROWS].wait()
             values = jnp.dot(basis[...], buf[row], preferred_element_type=F32)
-            banded[64 * i : 64 * (i + 1), :] = values.astype(BF)
+            banded[R3 * i : R3 * (i + 1), :] = values.astype(BF)
         terms = jnp.dot(banded[...], col[...], preferred_element_type=F32)
         for t in range(2):
             stage[t] = terms[:, 128 * t : 128 * (t + 1)]
@@ -66,7 +66,7 @@
         for j in range(N):
             for r in range(RX):
                 for t in range(2):
-                    rows = stage[t, pl.ds(16 * j + r, OUT_ROWS, stride=64), :]
+                    rows = stage[t, pl.ds(RX * j + r, OUT_ROWS, stride=R3), :]
                     outs[j][r, at, 128 * t : 128 * (t + 1)] = rows.astype(outs[j].dtype)
 
 
@@ -79,15 +79,14 @@
 
     def prepare():
         x = lax.axis_index("x")
-        basis[...] = jnp.zeros_like(basis)
         bt_copy.wait()
         for k in range(N):
 
             @pl.when(x == k)
             def _():
-                for j in range(N):
-                    at = RX * ((k + j) % N)
-                    basis[16 * j : 16 * j + RX, :] = bt[at : at + RX, :]
+                rows = bt[...].astype(F32)
+                turned = jnp.concatenate([rows[RX * k :], rows[: RX * k]], axis=0) if k else rows
+                basis[...] = turned.astype(BF)
 
         col_copy.wait()
 
@@ -106,8 +105,8 @@
     terms = [jax.ShapeDtypeStruct((RX, h, R2), BF if j else F32) for j in range(N)]
     scratch = [
         pltpu.VMEM((h, bands, c), BF),
-        pltpu.VMEM((64 * OUT_ROWS, c), BF),
-        pltpu.VMEM((2, 64 * OUT_ROWS, R2 // 2), F32),
+        pltpu.VMEM((R3 * OUT_ROWS, c), BF),
+        pltpu.VMEM((2, R3 * OUT_ROWS, R2 // 2), F32),
         pltpu.SemaphoreType.DMA((h // IN_ROWS,)),
     ]
     common = dict(
@@ -122,7 +121,7 @@
 def project_first(bt, col, pix, h):
     _, bands, c = pix.shape
     terms, scratch, common = project_specs(h, bands, c)
-    kept = [jax.ShapeDtypeStruct((64, bands), BF), jax.ShapeDtypeStruct(col.shape, BF)]
+    kept = [jax.ShapeDtypeStruct((R3, bands), BF), jax.ShapeDtypeStruct(col.shape, BF)]
     out = pl.pallas_call(
         first_kernel,
         in_specs=[ANY] * 3,

time: 72.7 us -> 72.6 us (level)
  Pallas kernels: 12.1 us -> 10.8 us
  starting transfers between devices: 35.5 us -> 36.3 us
    ppermute x14, starting transfers between devices: 26.2 us -> 27.2 us  [shift(): return lax.ppermute(v, names, pairs)]
  transfers between devices with their start and end apart: 22 -> 22, of which waited for: 12 -> 13; matrix products, arithmetic and copies ran while one was open for 1% -> 1% of each run, Pallas kernels for 7% -> 6%
where the time goes in v6:
time: 72.6 us; the launch traced here: 71.9 us
  starting transfers between devices  36.3 us (50%)
  waiting for transfers between devices  22.5 us (31%)
  Pallas kernels  10.8 us (15%)
  local copies, waits for them, and re-layouts  2 us (3%)
    ppermute x14, starting transfers between devices, shift(): return lax.ppermute(v, names, pairs)  27.2 us
    ppermute x14, waiting for transfers between devices, shift(): return lax.ppermute(v, names, pairs)  18.7 us
    ppermute x6, starting transfers between devices, turn(): return lax.ppermute(v, 'x', [(i, (i + by) % N) for i in range(N)])  8.93 us
    pallas_call x1, Pallas kernels, project_first(): pl.pallas_call(first_kernel, in_specs=[ANY] * 3, out_specs=[VMEM] * (N +...  4.42 us
    pallas_call x1, Pallas kernels, project_second(): pl.pallas_call(functools.partial(second_kernel, first), in_specs=[VMEM, V...  4.21 us
    ppermute x2, waiting for transfers between devices, swap(): return lax.ppermute(v, 'core', [(0, 1), (1, 0)])  2.14 us
    unnamed x13, local copies, waits for them, and re-layouts  1.95 us
    ppermute x6, waiting for transfers between devices, turn(): return lax.ppermute(v, 'x', [(i, (i + by) % N) for i in range(N)])  1.69 us
  transfers between devices with their start and end apart: 22, of which 13 were waited for; matrix products, arithmetic and copies ran while one was open for 1% of the time, Pallas kernels for 6%

profile of v6, /device:TPU:0, one launch (start us, length us, event | category | flops | bytes accessed | tf_op | source)
XLA Modules:
  0.0 71.9 jit_solution(8206468867008964093)
XLA Ops:
  0.0 0.9 %copy-done = bf16[256,256]{1,0:T(8,128)(2,1)S(1)} copy-done((bf16[256,256]{1,0:T(8,128)(2,1)S(1)}, bf16[256,256]{1,0:T(8,128)(2,1)}, u32[]{:S(2)}) %copy-start) | copy-done | bytes 131096
  0.9 0.8 %copy-done.1 = bf16[424,48]{0,1:T(8,128)(2,1)S(1)} copy-done((bf16[424,48]{0,1:T(8,128)(2,1)S(1)}, bf16[424,48]{0,1:T(8,128)(2,1)}, u32[]{:S(2)}) %copy-start.1) | copy-done | bytes 40728
  1.7 4.4 %project_first.1 = (f32[12,32,256]{2,1,0:T(8,128)S(1)}, bf16[12,32,256]{2,1,0:T(8,128)(2,1)S(1)}, bf16[12,32,256]{2,1,0:T(8,128)(2,1)S(1)}, bf16[12,32,256]{2,1,...) custom-call(bf16[48,424]{1,0:T(8,128)(2,1)S(1)} %bitcast.2, bf16[256,256]{1,0:T(8,128)(2,1)S(1)} %copy-done, ...), custom_call_target="tpu_custom_call" | custom-call | flops 1778384896 | bytes 6946816 | tf_op jit(solution)/shard_map/project_first/pallas_call | solution.py:125
  6.1 1.6 %collective-permute-start = (bf16[12,32,256]{2,1,0:T(8,128)(2,1)S(1)}, bf16[12,32,256]{2,1,0:T(8,128)(2,1)S(1)}, u32[]{:S(2)}, u32[]{:S(2)}) collective-permute-start(bf16[12,32,256]{2,1,0:T(8,128)(2,1)S(1)} %get-tuple-element.40), channel_id=1, source_target_pairs={{0,1},{1,2},{2,3},{3,0},{4,5},{5,6},{6,7},{7,4},{8,9},{9,10},{10,1... | collective-permute-start | bytes 589832 | tf_op jit(solution)/shard_map/ppermute | solution.py:33
  7.8 1.7 %collective-permute-start.1 = (bf16[12,32,256]{2,1,0:T(8,128)(2,1)S(1)}, bf16[12,32,256]{2,1,0:T(8,128)(2,1)S(1)}, u32[]{:S(2)}, u32[]{:S(2)}) collective-permute-start(bf16[12,32,256]{2,1,0:T(8,128)(2,1)S(1)} %get-tuple-element.41), channel_id=1, source_target_pairs={{0,3},{1,0},{2,1},{3,2},{4,7},{5,4},{6,5},{7,6},{8,11},{9,8},{10,9... | collective-permute-start | bytes 589832 | tf_op jit(solution)/shard_map/ppermute | solution.py:33
  9.4 1.9 %collective-permute-start.2 = (bf16[12,32,256]{2,1,0:T(8,128)(2,1)S(1)}, bf16[12,32,256]{2,1,0:T(8,128)(2,1)S(1)}, u32[]{:S(2)}, u32[]{:S(2)}) collective-permute-start(bf16[12,32,256]{2,1,0:T(8,128)(2,1)S(1)} %get-tuple-element.42), channel_id=1, source_target_pairs={{0,2},{1,3},{2,0},{3,1},{4,6},{5,7},{6,4},{7,5},{8,10},{9,11},{10,... | collective-permute-start | bytes 589832 | tf_op jit(solution)/shard_map/ppermute | solution.py:33
  11.3 4.2 %project_second.1 = (f32[12,32,256]{2,1,0:T(8,128)S(1)}, bf16[12,32,256]{2,1,0:T(8,128)(2,1)S(1)}, bf16[12,32,256]{2,1,0:T(8,128)(2,1)S(1)}, bf16[12,32,256]{2,1,0:T(8,128)(2,1)S(1)}) custom-call(bf16[48,424]{1,0:T(8,128)(2,1)S(1)} %get-tuple-element.43.basis, bf16[256,256]{1,0:T(8,128)(2,1)S(1)} %get-tuple-element.44.col, bf16[64,424,256]{2,1,0:T(8,128)(2,1)} %bitcast.4), custom_call_target="tpu_custom_call" | custom-call | flops 1778384896 | bytes 6946816 | tf_op jit(solution)/shard_map/project_second/pallas_call | solution.py:141
  15.6 1.2 %collective-permute-start.3 = (bf16[12,32,256]{2,1,0:T(8,128)(2,1)S(1)}, bf16[12,32,256]{2,1,0:T(8,128)(2,1)S(1)}, u32[]{:S(2)}, u32[]{:S(2)}) collective-permute-start(bf16[12,32,256]{2,1,0:T(8,128)(2,1)S(1)} %get-tuple-element.51), channel_id=1, source_target_pairs={{0,3},{1,0},{2,1},{3,2},{4,7},{5,4},{6,5},{7,6},{8,11},{9,8},{10,9... | collective-permute-start | bytes 589832 | tf_op jit(solution)/shard_map/ppermute | solution.py:33
  16.8 0.9 %collective-permute-start.4 = (bf16[12,32,256]{2,1,0:T(8,128)(2,1)S(1)}, bf16[12,32,256]{2,1,0:T(8,128)(2,1)S(1)}, u32[]{:S(2)}, u32[]{:S(2)}) collective-permute-start(bf16[12,32,256]{2,1,0:T(8,128)(2,1)S(1)} %get-tuple-element.52), channel_id=1, source_target_pairs={{0,1},{1,2},{2,3},{3,0},{4,5},{5,6},{6,7},{7,4},{8,9},{9,10},{10,1... | collective-permute-start | bytes 589832 | tf_op jit(solution)/shard_map/ppermute | solution.py:33
  17.6 0.0 collective-permute-done.refs_1_
  17.6 1.6 %collective-permute-start.5 = (bf16[12,32,256]{2,1,0:T(8,128)(2,1)S(1)}, bf16[12,32,256]{2,1,0:T(8,128)(2,1)S(1)}, u32[]{:S(2)}, u32[]{:S(2)}) collective-permute-start(bf16[12,32,256]{2,1,0:T(8,128)(2,1)S(1)} %get-tuple-element.53), channel_id=1, source_target_pairs={{0,2},{1,3},{2,0},{3,1},{4,6},{5,7},{6,4},{7,5},{8,10},{9,11},{10,... | collective-permute-start | bytes 589832 | tf_op jit(solution)/shard_map/ppermute | solution.py:33
  19.3 0.8 %collective-permute-done.2.refs_3_ = bf16[12,32,256]{2,1,0:T(8,128)(2,1)S(1)} collective-permute-done((bf16[12,32,256]{2,1,0:T(8,128)(2,1)S(1)}, bf16[12,32,256]{2,1,0:T(8,128)(2,1)S(1)}, u32[]{:S(2)}, u32[]{:S(2)}) %collective-permute-start.2) | collective-permute-done | bytes 196640 | tf_op jit(solution)/shard_map/ppermute | solution.py:33
  20.1 0.1 collect.2
  20.2 3.0 %collective-permute-start.6 = (bf16[32,3072]{1,0:T(8,128)(2,1)S(1)}, bf16[32,3072]{1,0:T(8,128)(2,1)S(1)}, u32[]{:S(2)}, u32[]{:S(2)}) collective-permute-start(bf16[32,3072]{1,0:T(8,128)(2,1)S(1)} %collect.2), channel_id=1, source_target_pairs={{0,96},{4,36},{32,0},{36,68},{64,32},{68,100},{96,64},{100,4},{1,9... | collective-permute-start | bytes 589832 | tf_op jit(solution)/shard_map/ppermute | solution.py:29
  23.1 4.0 %collective-permute-start.7 = (bf16[32,3072]{1,0:T(8,128)(2,1)S(1)}, bf16[32,3072]{1,0:T(8,128)(2,1)S(1)}, u32[]{:S(2)}, u32[]{:S(2)}) collective-permute-start(bf16[32,3072]{1,0:T(8,128)(2,1)S(1)} %collect.2), channel_id=1, source_target_pairs={{0,24},{4,12},{8,0},{12,20},{16,8},{20,28},{24,16},{28,4},{1,25},{... | collective-permute-start | bytes 589832 | tf_op jit(solution)/shard_map/ppermute | solution.py:29
  27.2 0.9 %collective-permute-done.4.refs_2_ = bf16[12,32,256]{2,1,0:T(8,128)(2,1)S(1)} collective-permute-done((bf16[12,32,256]{2,1,0:T(8,128)(2,1)S(1)}, bf16[12,32,256]{2,1,0:T(8,128)(2,1)S(1)}, u32[]{:S(2)}, u32[]{:S(2)}) %collective-permute-start.4) | collective-permute-done | bytes 196640 | tf_op jit(solution)/shard_map/ppermute | solution.py:33
  28.1 2.3 %collective-permute-done.7 = bf16[32,3072]{1,0:T(8,128)(2,1)S(1)} collective-permute-done((bf16[32,3072]{1,0:T(8,128)(2,1)S(1)}, bf16[32,3072]{1,0:T(8,128)(2,1)S(1)}, u32[]{:S(2)}, u32[]{:S(2)}) %collective-permute-start.7) | collective-permute-done | bytes 196640 | tf_op jit(solution)/shard_map/ppermute | solution.py:29
  30.4 0.1 collect.3
  30.5 3.8 %collective-permute-start.8 = (bf16[32,3072]{1,0:T(8,128)(2,1)S(1)}, bf16[32,3072]{1,0:T(8,128)(2,1)S(1)}, u32[]{:S(2)}, u32[]{:S(2)}) collective-permute-start(bf16[32,3072]{1,0:T(8,128)(2,1)S(1)} %collect.3), channel_id=1, source_target_pairs={{0,24},{4,12},{8,0},{12,20},{16,8},{20,28},{24,16},{28,4},{1,25},{... | collective-permute-start | bytes 589832 | tf_op jit(solution)/shard_map/ppermute | solution.py:29
  34.2 1.1 %collective-permute-start.9 = (bf16[32,3072]{1,0:T(8,128)(2,1)S(1)}, bf16[32,3072]{1,0:T(8,128)(2,1)S(1)}, u32[]{:S(2)}, u32[]{:S(2)}) collective-permute-start(bf16[32,3072]{1,0:T(8,128)(2,1)S(1)} %collect.3), channel_id=1, source_target_pairs={{0,96},{4,36},{32,0},{36,68},{64,32},{68,100},{96,64},{100,4},{1,9... | collective-permute-start | bytes 589832 | tf_op jit(solution)/shard_map/ppermute | solution.py:29
  35.3 1.0 %collective-permute-start.13 = (bf16[64,3072]{1,0:T(8,128)(2,1)S(1)}, bf16[64,3072]{1,0:T(8,128)(2,1)S(1)}, u32[]{:S(2)}, u32[]{:S(2)}) collective-permute-start(bf16[64,3072]{1,0:T(8,128)(2,1)S(1)} %pad_maximum_fusion.4), channel_id=1, source_target_pairs={{0,32},{4,100},{32,64},{36,4},{64,96},{68,36},{96,0},{100,68},{1,3... | collective-permute-start | bytes 1179656 | tf_op jit(solution)/shard_map/ppermute | solution.py:29
  36.4 0.1 copy.8
  36.5 3.4 %collective-permute-done.9 = bf16[32,3072]{1,0:T(8,128)(2,1)S(1)} collective-permute-done((bf16[32,3072]{1,0:T(8,128)(2,1)S(1)}, bf16[32,3072]{1,0:T(8,128)(2,1)S(1)}, u32[]{:S(2)}, u32[]{:S(2)}) %collective-permute-start.9) | collective-permute-done | bytes 196640 | tf_op jit(solution)/shard_map/ppermute | solution.py:29
  39.9 0.1 pad_maximum_fusion
  40.0 0.1 collective-permute-start.10
  40.1 2.3 %collective-permute-start.11 = (bf16[64,3072]{1,0:T(8,128)(2,1)S(1)}, bf16[64,3072]{1,0:T(8,128)(2,1)S(1)}, u32[]{:S(2)}, u32[]{:S(2)}) collective-permute-start(bf16[64,3072]{1,0:T(8,128)(2,1)S(1)} %pad_maximum_fusion.2), channel_id=1, source_target_pairs={{0,96},{4,36},{32,0},{36,68},{64,32},{68,100},{96,64},{100,4},{1,9... | collective-permute-start | bytes 1179656 | tf_op jit(solution)/shard_map/ppermute | solution.py:29
  42.5 1.7 %collective-permute-start.12 = (bf16[64,3072]{1,0:T(8,128)(2,1)S(1)}, bf16[64,3072]{1,0:T(8,128)(2,1)S(1)}, u32[]{:S(2)}, u32[]{:S(2)}) collective-permute-start(bf16[64,3072]{1,0:T(8,128)(2,1)S(1)} %pad_maximum_fusion.3), channel_id=1, source_target_pairs={{0,24},{4,12},{8,0},{12,20},{16,8},{20,28},{24,16},{28,4},{1,25},{... | collective-permute-start | bytes 1179656 | tf_op jit(solution)/shard_map/ppermute | solution.py:29
  44.2 0.2 collective-permute-done.13
  44.4 1.7 %collective-permute-done.14 = bf16[64,3072]{1,0:T(8,128)(2,1)S(1)} collective-permute-done((bf16[64,3072]{1,0:T(8,128)(2,1)S(1)}, bf16[64,3072]{1,0:T(8,128)(2,1)S(1)}, u32[]{:S(2)}, u32[]{:S(2)}) %collective-permute-start.14) | collective-permute-done | bytes 393248 | tf_op jit(solution)/shard_map/ppermute | solution.py:29
  46.0 1.9 %collective-permute-done.11 = bf16[64,3072]{1,0:T(8,128)(2,1)S(1)} collective-permute-done((bf16[64,3072]{1,0:T(8,128)(2,1)S(1)}, bf16[64,3072]{1,0:T(8,128)(2,1)S(1)}, u32[]{:S(2)}, u32[]{:S(2)}) %collective-permute-start.11) | collective-permute-done | bytes 393248 | tf_op jit(solution)/shard_map/ppermute | solution.py:29
  47.9 2.4 %collective-permute-done.12 = bf16[64,3072]{1,0:T(8,128)(2,1)S(1)} collective-permute-done((bf16[64,3072]{1,0:T(8,128)(2,1)S(1)}, bf16[64,3072]{1,0:T(8,128)(2,1)S(1)}, u32[]{:S(2)}, u32[]{:S(2)}) %collective-permute-start.12) | collective-permute-done | bytes 393248 | tf_op jit(solution)/shard_map/ppermute | solution.py:29
  50.3 0.1 pad_maximum_fusion.1
  50.4 0.1 collective-permute-start.15
  50.5 0.1 constant_dynamic-update-slice_fusion
  50.6 2.1 %collective-permute-done.15.late = bf16[128,3072]{1,0:T(8,128)(2,1)S(1)} collective-permute-done((bf16[128,3072]{1,0:T(8,128)(2,1)S(1)}, bf16[128,3072]{1,0:T(8,128)(2,1)S(1)}, u32[]{:S(2)}, u32[]{:S(2)}) %collective-permute-start.15) | collective-permute-done | bytes 786464 | tf_op jit(solution)/shard_map/ppermute | solution.py:37
  52.7 1.2 %gram.1 = (f32[256,128]{1,0:T(8,128)S(1)}, f32[256,128]{1,0:T(8,128)S(1)}, f32[256,128]{1,0:T(8,128)S(1)}, f32[256,128]{1,0:T(8,128)S(1)}) custom-call(bf16[256,3072]{1,0:T(8,128)(2,1)S(1)} %get-tuple-element.73.zs, bf16[256,3072]{1,0:T(8,128)(2,1)S(1)} %get-tuple-element.74.ys, bf16[128,3072]{1,0:T(8,128)(2,1)S(1)} %collective-permute-done.10.early, ...), custom_call_target="tpu_custom_call" | custom-call | flops 805306368 | bytes 4718592 | tf_op jit(solution)/shard_map/gram/pallas_call | solution.py:197
  54.0 1.0 %collective-permute-start.16 = (f32[256,128]{1,0:T(8,128)S(1)}, f32[256,128]{1,0:T(8,128)S(1)}, u32[]{:S(2)}, u32[]{:S(2)}) collective-permute-start(f32[256,128]{1,0:T(8,128)S(1)} %get-tuple-element.66), channel_id=1, source_target_pairs={{0,2},{4,6},{1,3},{5,7},{2,0},{6,4},{3,1},{7,5},{8,10},{12,14},{9,... | collective-permute-start | bytes 393224 | tf_op jit(solution)/shard_map/ppermute | solution.py:29
  55.0 1.9 %collective-permute-start.17 = (f32[256,128]{1,0:T(8,128)S(1)}, f32[256,128]{1,0:T(8,128)S(1)}, u32[]{:S(2)}, u32[]{:S(2)}) collective-permute-start(f32[256,128]{1,0:T(8,128)S(1)} %get-tuple-element.67), channel_id=1, source_target_pairs={{0,1},{4,7},{1,2},{5,4},{2,3},{6,5},{3,0},{7,6},{8,9},{12,15},{9,1... | collective-permute-start | bytes 393224 | tf_op jit(solution)/shard_map/ppermute | solution.py:29
  56.8 1.6 %collective-permute-start.18 = (f32[256,128]{1,0:T(8,128)S(1)}, f32[256,128]{1,0:T(8,128)S(1)}, u32[]{:S(2)}, u32[]{:S(2)}) collective-permute-start(f32[256,128]{1,0:T(8,128)S(1)} %get-tuple-element.68), channel_id=1, source_target_pairs={{0,3},{4,5},{1,0},{5,6},{2,1},{6,7},{3,2},{7,4},{8,11},{12,13},{9,... | collective-permute-start | bytes 393224 | tf_op jit(solution)/shard_map/ppermute | solution.py:29
  58.4 3.5 %collective-permute-done.16.g1 = f32[256,128]{1,0:T(8,128)S(1)} collective-permute-done((f32[256,128]{1,0:T(8,128)S(1)}, f32[256,128]{1,0:T(8,128)S(1)}, u32[]{:S(2)}, u32[]{:S(2)}) %collective-permute-start.16) | collective-permute-done | bytes 131104 | tf_op jit(solution)/shard_map/ppermute | solution.py:29
  61.9 1.2 %collective-permute-done.17.g2 = f32[256,128]{1,0:T(8,128)S(1)} collective-permute-done((f32[256,128]{1,0:T(8,128)S(1)}, f32[256,128]{1,0:T(8,128)S(1)}, u32[]{:S(2)}, u32[]{:S(2)}) %collective-permute-start.17) | collective-permute-done | bytes 131104 | tf_op jit(solution)/shard_map/ppermute | solution.py:29
  63.1 0.0 collective-permute-done.18.g3
  63.2 2.6 %collective-permute-start.19 = (f32[64,128]{1,0:T(8,128)S(1)}, f32[64,128]{1,0:T(8,128)S(1)}, u32[]{:S(2)}, u32[]{:S(2)}) collective-permute-start(f32[64,128]{1,0:T(8,128)S(1)} %get-tuple-element.70), channel_id=1, source_target_pairs={{0,16},{4,20},{8,24},{12,28},{16,0},{20,4},{24,8},{28,12},{1,17},{... | collective-permute-start | bytes 98312 | tf_op jit(solution)/shard_map/ppermute | solution.py:29
  65.8 1.5 %collective-permute-start.20 = (f32[64,128]{1,0:T(8,128)S(1)}, f32[64,128]{1,0:T(8,128)S(1)}, u32[]{:S(2)}, u32[]{:S(2)}) collective-permute-start(f32[64,128]{1,0:T(8,128)S(1)} %get-tuple-element.71), channel_id=1, source_target_pairs={{0,8},{4,28},{8,16},{12,4},{16,24},{20,12},{24,0},{28,20},{1,9},{5... | collective-permute-start | bytes 98312 | tf_op jit(solution)/shard_map/ppermute | solution.py:29
  67.3 1.7 %collective-permute-start.21 = (f32[64,128]{1,0:T(8,128)S(1)}, f32[64,128]{1,0:T(8,128)S(1)}, u32[]{:S(2)}, u32[]{:S(2)}) collective-permute-start(f32[64,128]{1,0:T(8,128)S(1)} %get-tuple-element.72), channel_id=1, source_target_pairs={{0,24},{4,12},{8,0},{12,20},{16,8},{20,28},{24,16},{28,4},{1,25},{... | collective-permute-start | bytes 98312 | tf_op jit(solution)/shard_map/ppermute | solution.py:29
  69.0 2.0 %collective-permute-done.20.refs_2_ = f32[64,128]{1,0:T(8,128)S(1)} collective-permute-done((f32[64,128]{1,0:T(8,128)S(1)}, f32[64,128]{1,0:T(8,128)S(1)}, u32[]{:S(2)}, u32[]{:S(2)}) %collective-permute-start.20) | collective-permute-done | bytes 32800 | tf_op jit(solution)/shard_map/ppermute | solution.py:29
  71.0 0.3 collective-permute-done.21.refs_3_
  71.2 0.7 place.1
  (22 shorter events, 0.3 us)
Async XLA Ops:
  0.0 0.9 %copy-start = (bf16[256,256]{1,0:T(8,128)(2,1)S(1)}, bf16[256,256]{1,0:T(8,128)(2,1)}, u32[]{:S(2)}) copy-start(bf16[256,256]{1,0:T(8,128)(2,1)} %col_hbm.1) | copy-start | bytes 393220
  0.9 0.8 %copy-start.1 = (bf16[424,48]{0,1:T(8,128)(2,1)S(1)}, bf16[424,48]{0,1:T(8,128)(2,1)}, u32[]{:S(2)}) copy-start(bf16[424,48]{0,1:T(8,128)(2,1)} %param.4) | copy-start | bytes 122116
  6.1 11.5 %collective-permute-start = (bf16[12,32,256]{2,1,0:T(8,128)(2,1)S(1)}, bf16[12,32,256]{2,1,0:T(8,128)(2,1)S(1)}, u32[]{:S(2)}, u32[]{:S(2)}) collective-permute-start(bf16[12,32,256]{2,1,0:T(8,128)(2,1)S(1)} %get-tuple-element.40), channel_id=1, source_target_pairs={{0,1},{1,2},{2,3},{3,0},{4,5},{5,6},{6,7},{7,4},{8,9},{9,10},{10,1... | collective-permute-start | bytes 589832 | tf_op jit(solution)/shard_map/ppermute | solution.py:33
  7.8 11.5 %collective-permute-start.1 = (bf16[12,32,256]{2,1,0:T(8,128)(2,1)S(1)}, bf16[12,32,256]{2,1,0:T(8,128)(2,1)S(1)}, u32[]{:S(2)}, u32[]{:S(2)}) collective-permute-start(bf16[12,32,256]{2,1,0:T(8,128)(2,1)S(1)} %get-tuple-element.41), channel_id=1, source_target_pairs={{0,3},{1,0},{2,1},{3,2},{4,7},{5,4},{6,5},{7,6},{8,11},{9,8},{10,9... | collective-permute-start | bytes 589832 | tf_op jit(solution)/shard_map/ppermute | solution.py:33
  9.4 10.6 %collective-permute-start.2 = (bf16[12,32,256]{2,1,0:T(8,128)(2,1)S(1)}, bf16[12,32,256]{2,1,0:T(8,128)(2,1)S(1)}, u32[]{:S(2)}, u32[]{:S(2)}) collective-permute-start(bf16[12,32,256]{2,1,0:T(8,128)(2,1)S(1)} %get-tuple-element.42), channel_id=1, source_target_pairs={{0,2},{1,3},{2,0},{3,1},{4,6},{5,7},{6,4},{7,5},{8,10},{9,11},{10,... | collective-permute-start | bytes 589832 | tf_op jit(solution)/shard_map/ppermute | solution.py:33
  15.6 11.6 %collective-permute-start.3 = (bf16[12,32,256]{2,1,0:T(8,128)(2,1)S(1)}, bf16[12,32,256]{2,1,0:T(8,128)(2,1)S(1)}, u32[]{:S(2)}, u32[]{:S(2)}) collective-permute-start(bf16[12,32,256]{2,1,0:T(8,128)(2,1)S(1)} %get-tuple-element.51), channel_id=1, source_target_pairs={{0,3},{1,0},{2,1},{3,2},{4,7},{5,4},{6,5},{7,6},{8,11},{9,8},{10,9... | collective-permute-start | bytes 589832 | tf_op jit(solution)/shard_map/ppermute | solution.py:33
  16.8 11.3 %collective-permute-start.4 = (bf16[12,32,256]{2,1,0:T(8,128)(2,1)S(1)}, bf16[12,32,256]{2,1,0:T(8,128)(2,1)S(1)}, u32[]{:S(2)}, u32[]{:S(2)}) collective-permute-start(bf16[12,32,256]{2,1,0:T(8,128)(2,1)S(1)} %get-tuple-element.52), channel_id=1, source_target_pairs={{0,1},{1,2},{2,3},{3,0},{4,5},{5,6},{6,7},{7,4},{8,9},{9,10},{10,1... | collective-permute-start | bytes 589832 | tf_op jit(solution)/shard_map/ppermute | solution.py:33
  17.6 10.5 %collective-permute-start.5 = (bf16[12,32,256]{2,1,0:T(8,128)(2,1)S(1)}, bf16[12,32,256]{2,1,0:T(8,128)(2,1)S(1)}, u32[]{:S(2)}, u32[]{:S(2)}) collective-permute-start(bf16[12,32,256]{2,1,0:T(8,128)(2,1)S(1)} %get-tuple-element.53), channel_id=1, source_target_pairs={{0,2},{1,3},{2,0},{3,1},{4,6},{5,7},{6,4},{7,5},{8,10},{9,11},{10,... | collective-permute-start | bytes 589832 | tf_op jit(solution)/shard_map/ppermute | solution.py:33
  20.2 7.9 %collective-permute-start.6 = (bf16[32,3072]{1,0:T(8,128)(2,1)S(1)}, bf16[32,3072]{1,0:T(8,128)(2,1)S(1)}, u32[]{:S(2)}, u32[]{:S(2)}) collective-permute-start(bf16[32,3072]{1,0:T(8,128)(2,1)S(1)} %collect.2), channel_id=1, source_target_pairs={{0,96},{4,36},{32,0},{36,68},{64,32},{68,100},{96,64},{100,4},{1,9... | collective-permute-start | bytes 589832 | tf_op jit(solution)/shard_map/ppermute | solution.py:29
  23.1 7.2 %collective-permute-start.7 = (bf16[32,3072]{1,0:T(8,128)(2,1)S(1)}, bf16[32,3072]{1,0:T(8,128)(2,1)S(1)}, u32[]{:S(2)}, u32[]{:S(2)}) collective-permute-start(bf16[32,3072]{1,0:T(8,128)(2,1)S(1)} %collect.2), channel_id=1, source_target_pairs={{0,24},{4,12},{8,0},{12,20},{16,8},{20,28},{24,16},{28,4},{1,25},{... | collective-permute-start | bytes 589832 | tf_op jit(solution)/shard_map/ppermute | solution.py:29
  30.5 12.0 %collective-permute-start.8 = (bf16[32,3072]{1,0:T(8,128)(2,1)S(1)}, bf16[32,3072]{1,0:T(8,128)(2,1)S(1)}, u32[]{:S(2)}, u32[]{:S(2)}) collective-permute-start(bf16[32,3072]{1,0:T(8,128)(2,1)S(1)} %collect.3), channel_id=1, source_target_pairs={{0,24},{4,12},{8,0},{12,20},{16,8},{20,28},{24,16},{28,4},{1,25},{... | collective-permute-start | bytes 589832 | tf_op jit(solution)/shard_map/ppermute | solution.py:29
  34.2 5.7 %collective-permute-start.9 = (bf16[32,3072]{1,0:T(8,128)(2,1)S(1)}, bf16[32,3072]{1,0:T(8,128)(2,1)S(1)}, u32[]{:S(2)}, u32[]{:S(2)}) collective-permute-start(bf16[32,3072]{1,0:T(8,128)(2,1)S(1)} %collect.3), channel_id=1, source_target_pairs={{0,96},{4,36},{32,0},{36,68},{64,32},{68,100},{96,64},{100,4},{1,9... | collective-permute-start | bytes 589832 | tf_op jit(solution)/shard_map/ppermute | solution.py:29
  35.3 9.1 %collective-permute-start.13 = (bf16[64,3072]{1,0:T(8,128)(2,1)S(1)}, bf16[64,3072]{1,0:T(8,128)(2,1)S(1)}, u32[]{:S(2)}, u32[]{:S(2)}) collective-permute-start(bf16[64,3072]{1,0:T(8,128)(2,1)S(1)} %pad_maximum_fusion.4), channel_id=1, source_target_pairs={{0,32},{4,100},{32,64},{36,4},{64,96},{68,36},{96,0},{100,68},{1,3... | collective-permute-start | bytes 1179656 | tf_op jit(solution)/shard_map/ppermute | solution.py:29
  36.4 9.7 %collective-permute-start.14 = (bf16[64,3072]{1,0:T(8,128)(2,1)S(1)}, bf16[64,3072]{1,0:T(8,128)(2,1)S(1)}, u32[]{:S(2)}, u32[]{:S(2)}) collective-permute-start(bf16[64,3072]{1,0:T(8,128)(2,1)S(1)} %pad_maximum_fusion.4), channel_id=1, source_target_pairs={{0,8},{4,28},{8,16},{12,4},{16,24},{20,12},{24,0},{28,20},{1,9},{5... | collective-permute-start | bytes 1179656 | tf_op jit(solution)/shard_map/ppermute | solution.py:29
  40.0 10.3 %collective-permute-start.10 = (bf16[128,3072]{1,0:T(8,128)(2,1)S(1)}, bf16[128,3072]{1,0:T(8,128)(2,1)S(1)}, u32[]{:S(2)}, u32[]{:S(2)}) collective-permute-start(bf16[128,3072]{1,0:T(8,128)(2,1)S(1)} %pad_maximum_fusion), channel_id=1, source_target_pairs={{0,4},{4,0},{1,5},{5,1},{2,6},{6,2},{3,7},{7,3},{8,12},{12,8},{9,1... | collective-permute-start | bytes 2359304 | tf_op jit(solution)/shard_map/ppermute | solution.py:37
  40.1 7.8 %collective-permute-start.11 = (bf16[64,3072]{1,0:T(8,128)(2,1)S(1)}, bf16[64,3072]{1,0:T(8,128)(2,1)S(1)}, u32[]{:S(2)}, u32[]{:S(2)}) collective-permute-start(bf16[64,3072]{1,0:T(8,128)(2,1)S(1)} %pad_maximum_fusion.2), channel_id=1, source_target_pairs={{0,96},{4,36},{32,0},{36,68},{64,32},{68,100},{96,64},{100,4},{1,9... | collective-permute-start | bytes 1179656 | tf_op jit(solution)/shard_map/ppermute | solution.py:29
  42.5 7.8 %collective-permute-start.12 = (bf16[64,3072]{1,0:T(8,128)(2,1)S(1)}, bf16[64,3072]{1,0:T(8,128)(2,1)S(1)}, u32[]{:S(2)}, u32[]{:S(2)}) collective-permute-start(bf16[64,3072]{1,0:T(8,128)(2,1)S(1)} %pad_maximum_fusion.3), channel_id=1, source_target_pairs={{0,24},{4,12},{8,0},{12,20},{16,8},{20,28},{24,16},{28,4},{1,25},{... | collective-permute-start | bytes 1179656 | tf_op jit(solution)/shard_map/ppermute | solution.py:29
  50.4 2.4 %collective-permute-start.15 = (bf16[128,3072]{1,0:T(8,128)(2,1)S(1)}, bf16[128,3072]{1,0:T(8,128)(2,1)S(1)}, u32[]{:S(2)}, u32[]{:S(2)}) collective-permute-start(bf16[128,3072]{1,0:T(8,128)(2,1)S(1)} %pad_maximum_fusion.1), channel_id=1, source_target_pairs={{0,4},{4,0},{1,5},{5,1},{2,6},{6,2},{3,7},{7,3},{8,12},{12,8},{9,1... | collective-permute-start | bytes 2359304 | tf_op jit(solution)/shard_map/ppermute | solution.py:37
  54.0 7.9 %collective-permute-start.16 = (f32[256,128]{1,0:T(8,128)S(1)}, f32[256,128]{1,0:T(8,128)S(1)}, u32[]{:S(2)}, u32[]{:S(2)}) collective-permute-start(f32[256,128]{1,0:T(8,128)S(1)} %get-tuple-element.66), channel_id=1, source_target_pairs={{0,2},{4,6},{1,3},{5,7},{2,0},{6,4},{3,1},{7,5},{8,10},{12,14},{9,... | collective-permute-start | bytes 393224 | tf_op jit(solution)/shard_map/ppermute | solution.py:29
  55.0 8.1 %collective-permute-start.17 = (f32[256,128]{1,0:T(8,128)S(1)}, f32[256,128]{1,0:T(8,128)S(1)}, u32[]{:S(2)}, u32[]{:S(2)}) collective-permute-start(f32[256,128]{1,0:T(8,128)S(1)} %get-tuple-element.67), channel_id=1, source_target_pairs={{0,1},{4,7},{1,2},{5,4},{2,3},{6,5},{3,0},{7,6},{8,9},{12,15},{9,1... | collective-permute-start | bytes 393224 | tf_op jit(solution)/shard_map/ppermute | solution.py:29
  56.8 6.3 %collective-permute-start.18 = (f32[256,128]{1,0:T(8,128)S(1)}, f32[256,128]{1,0:T(8,128)S(1)}, u32[]{:S(2)}, u32[]{:S(2)}) collective-permute-start(f32[256,128]{1,0:T(8,128)S(1)} %get-tuple-element.68), channel_id=1, source_target_pairs={{0,3},{4,5},{1,0},{5,6},{2,1},{6,7},{3,2},{7,4},{8,11},{12,13},{9,... | collective-permute-start | bytes 393224 | tf_op jit(solution)/shard_map/ppermute | solution.py:29
  63.2 5.9 %collective-permute-start.19 = (f32[64,128]{1,0:T(8,128)S(1)}, f32[64,128]{1,0:T(8,128)S(1)}, u32[]{:S(2)}, u32[]{:S(2)}) collective-permute-start(f32[64,128]{1,0:T(8,128)S(1)} %get-tuple-element.70), channel_id=1, source_target_pairs={{0,16},{4,20},{8,24},{12,28},{16,0},{20,4},{24,8},{28,12},{1,17},{... | collective-permute-start | bytes 98312 | tf_op jit(solution)/shard_map/ppermute | solution.py:29
  65.8 5.2 %collective-permute-start.20 = (f32[64,128]{1,0:T(8,128)S(1)}, f32[64,128]{1,0:T(8,128)S(1)}, u32[]{:S(2)}, u32[]{:S(2)}) collective-permute-start(f32[64,128]{1,0:T(8,128)S(1)} %get-tuple-element.71), channel_id=1, source_target_pairs={{0,8},{4,28},{8,16},{12,4},{16,24},{20,12},{24,0},{28,20},{1,9},{5... | collective-permute-start | bytes 98312 | tf_op jit(solution)/shard_map/ppermute | solution.py:29
  67.3 3.9 %collective-permute-start.21 = (f32[64,128]{1,0:T(8,128)S(1)}, f32[64,128]{1,0:T(8,128)S(1)}, u32[]{:S(2)}, u32[]{:S(2)}) collective-permute-start(f32[64,128]{1,0:T(8,128)S(1)} %get-tuple-element.72), channel_id=1, source_target_pairs={{0,24},{4,12},{8,0},{12,20},{16,8},{20,28},{24,16},{28,4},{1,25},{... | collective-permute-start | bytes 98312 | tf_op jit(solution)/shard_map/ppermute | solution.py:29
